TPU v7x, 32 devices: a whole 2x2x4 slice. The times are simulated.
32 devices in a mesh: groups: 2 (over x), gx: 16 (over z, y, core).
Axes of the slice: x: 2, y: 2, z: 4, core: 2. Of those that a mesh axis runs over, the one named last changes fastest.
Arguments:
- u_prev: float32 [256, 256, 256], P(('groups', 'gx')), parts along dimension 0, may hold values from -7 to 7
- u_cur: float32 [256, 256, 256], P(('groups', 'gx')), parts along dimension 0, may hold values from -7 to 7
- courant_sq: float32 [256, 256, 256], P(('groups', 'gx')), parts along dimension 0, may hold values from 0.1 to 0.33
- patch_map: int32 [256, 4, 256], P(('groups', 'gx')), parts along dimension 0, may hold values from 0 to 159
- absorb: float32 [320], P('groups'), parts along dimension 0, may hold values from 0.05 to 1
- checkpoint: int32 [2], P('groups'), parts along dimension 0, may hold values from 0 to 60
- target_curve: float32 [128], P('groups'), parts along dimension 0, may hold values from 0 to 2.5
- tail_energy: float32 [2], P('groups'), parts along dimension 0, may hold values from 0.5 to 4
Outputs:
- grad_prev: float32 [256, 256, 256], P(('groups', 'gx')), parts along dimension 0
- grad_cur: float32 [256, 256, 256], P(('groups', 'gx')), parts along dimension 0
- grad_absorb: float32 [320], P(('groups', 'gx')), parts along dimension 0
There are 2 independent parts, one for each index of `groups`. A program takes and returns all parts, laid end to end along the dimension named above; each array names one. Nothing has to cross between parts.
All inputs are finite; a program needn't handle non-finite values.
Results may differ from a plain program's by a relative error of at most 0.00002.
Values sent between devices are 32-bit elements; how exact they have to be, the bound alone decides.
No kernel may reach another device: no remote copies, remote signals or barrier semaphores. Data moves between devices by JAX's collectives and lax.ppermute only.
A program may use at most 128 MiB of HBM per device.

v0:
```python
import jax
import jax.numpy as jnp
from jax import lax
from jax.sharding import PartitionSpec as P

STEPS = 4
PATCH_CELLS = 819


def extended(cells, sides, width):
    for axis, dim in sides:
        count = lax.axis_size(axis)
        ends = count - 1
        head = lax.slice_in_dim(cells, 0, width, axis=dim)
        tail = lax.slice_in_dim(cells, cells.shape[dim] - width, cells.shape[dim], axis=dim)
        cells = jnp.concatenate(
            [
                lax.ppermute(tail, axis, [(i, (i + 1) % count) for i in range(ends)]),
                cells,
                lax.ppermute(head, axis, [((i + 1) % count, i) for i in range(ends)]),
            ],
            axis=dim,
        )
    return cells


def neighbours(padded):
    full = jnp.pad(padded, ((0, 0), (1, 1), (1, 1)))
    total = full[2:, 1:-1, 1:-1] + full[:-2, 1:-1, 1:-1]
    total = total + full[1:-1, 2:, 1:-1] + full[1:-1, :-2, 1:-1]
    return total + full[1:-1, 1:-1, 2:] + full[1:-1, 1:-1, :-2]


def advance(prior, now, beside_all, courant, damping):
    return (
        2.0 * now - (1.0 - damping) * prior + courant * (neighbours(beside_all) - 6.0 * now)
    ) / (1.0 + damping)


def spread_faces(faces, side_cells):
    damping = jnp.zeros((faces.shape[0], side_cells, side_cells), jnp.float32)
    damping = damping.at[:, 0, :].add(faces[:, 0])
    damping = damping.at[:, -1, :].add(faces[:, 1])
    damping = damping.at[:, :, 0].add(faces[:, 2])
    return damping.at[:, :, -1].add(faces[:, 3])


def collect_faces(field):
    return jnp.stack([field[:, 0, :], field[:, -1, :], field[:, :, 0], field[:, :, -1]], axis=1)


def face_layers(field):
    return extended(field, (("gx", 0),), 1)


def adjoint_layers(field):
    return extended(field, (("gx", 0),), 1)


def on_device(u_prev, u_cur, courant_sq, patch_map, absorb, checkpoint, target_curve, tail_energy):
    depth_cells = u_cur.shape[0]
    side_cells = u_cur.shape[1]
    all_cells = float(depth_cells * lax.axis_size("gx") * side_cells * side_cells)
    face_absorb = absorb[patch_map]
    damping_wide = spread_faces(face_absorb, side_cells)
    states = [u_prev, u_cur]
    for turn_index in range(STEPS):
        beside_all = face_layers(states[-1])
        states.append(advance(states[-2], states[-1], beside_all, courant_sq, damping_wide))
    local_energy = jnp.stack([jnp.sum(field * field) for field in states[2:]])
    energy = lax.psum(local_energy, "gx") / all_cells
    targets = lax.dynamic_slice_in_dim(target_curve, checkpoint[0], STEPS)
    schroeder = tail_energy[0] + jnp.cumsum(energy[::-1])[::-1]
    slopes = 2.0 * (jnp.log(schroeder) - targets) / schroeder
    weights = jnp.cumsum(slopes)
    inverse_gain = 1.0 / (1.0 + damping_wide)
    retain = 1.0 - damping_wide
    adjoint = 2.0 * weights[STEPS - 1] * states[STEPS + 1]
    w_later = jnp.zeros_like(adjoint)
    grad_damp = jnp.zeros_like(u_cur)
    for back_index in range(STEPS, 0, -1):
        weighted = inverse_gain * adjoint
        grad_damp = grad_damp + weighted * (states[back_index - 1] - states[back_index + 1])
        product = courant_sq * weighted
        beside_all = adjoint_layers(product)
        fresh = 2.0 * weighted + neighbours(beside_all) - 6.0 * product - retain * w_later
        if back_index > 1:
            fresh = fresh + 2.0 * weights[back_index - 2] * states[back_index]
        w_later = weighted
        adjoint = fresh
    grad_prev = -retain * w_later
    faces_grad = collect_faces(grad_damp)
    partial_value = jax.ops.segment_sum(
        faces_grad.reshape(-1), patch_map.reshape(-1), absorb.shape[0]
    )
    owned_sum = lax.psum_scatter(partial_value, "gx", scatter_dimension=0, tiled=True)
    return (grad_prev, adjoint, owned_sum / float(PATCH_CELLS))


def solution(mesh):
    return jax.shard_map(
        on_device,
        mesh=mesh,
        in_specs=(
            P(("groups", "gx"), None, None),
            P(("groups", "gx"), None, None),
            P(("groups", "gx"), None, None),
            P(("groups", "gx"), None, None),
            P("groups"),
            P("groups"),
            P("groups"),
            P("groups"),
        ),
        out_specs=(
            P(("groups", "gx"), None, None),
            P(("groups", "gx"), None, None),
            P(("groups", "gx")),
        ),
        check_vma=False,
    )
```

profile of v0, /device:TPU:0, one launch (start us, length us, event | category | flops | bytes accessed | tf_op | source)
XLA Modules:
  0.0 343.8 jit_solution(4479685540915618978)
XLA Ops:
  0.7 2.9 copy.48
  6.7 3.7 %collective-permute-start.1 = (f32[1,256,256]{1,2,0:T(8,128)}, f32[1,256,256]{1,2,0:T(8,128)}, u32[]{:S(2)}, u32[]{:S(2)}) collective-permute-start(f32[1,256,256]{1,2,0:T(8,128)} %get-tuple-element.91), channel_id=1, source_target_pairs={{0,1},{1,2},{2,3},{3,4},{4,5},{5,6},{6,7},{7,8},{8,9},{9,10},{10,1... | collective-permute-start | bytes 786440 | tf_op jit(solution)/shard_map/ppermute | solution.py:18
  10.5 51.0 %gather_fusion = f32[8192]{0:T(1024)S(1)} fusion(f32[160]{0:T(256)S(1)} %copy-done, s32[8192]{0:T(1024)S(1)} %broadcast_clamp_fusion), kind=kCustom, calls=%fused_computation | custom fusion | bytes 98304 | tf_op jit(solution)/shard_map/gather | solution.py:64
  63.5 4.3 %scatter-add.21 = f32[8,256,256]{1,2,0:T(8,128)S(1)} dynamic-update-slice(f32[8,256,256]{1,2,0:T(8,128)S(1)} %scatter-add.20, f32[8,1,256]{1,2,0:T(8,128)} %copy.73, s32[]{:T(128)} %constant.129.clone.1, s32[]{:T(128)} %constant.132.clone.1, s32[]{:T(128)} %constant.129.clone.1) | dynamic-update-slice | bytes 16388 | tf_op jit(solution)/shard_map/scatter-add | solution.py:43
  67.9 2.9 copy.56
  70.8 2.9 copy.49
  73.7 3.5 %select_maximum_fusion.14 = f32[10,258,258]{1,2,0:T(8,128)S(1)} fusion(f32[1,256,256]{1,2,0:T(8,128)S(1)} %collective-permute-done, f32[8,256,256]{1,2,0:T(8,128)} %copy.48, f32[1,256,256]{1,2,0:T(8,128)} %collective-permute-done.1), kind=kLoop, calls=%fused_computation.20 | loop fusion | flops 9984600 | bytes 5284000 | tf_op jit(solution)/shard_map/concatenate | solution.py:16
  77.3 3.9 %multiply_reduce_fusion.3 = (f32[]{:T(128)}, f32[8,256,256]{1,2,0:T(8,128)S(1)}) fusion(f32[8,256,256]{1,2,0:T(8,128)S(1)} %scatter-add.30, f32[8,256,256]{1,2,0:T(8,128)S(1)} %copy-done.2, f32[8,256,256]{1,2,0:T(8,128)S(1)} %copy-done.14, f32[10,258,258]{1,2,0:T(8,128)S(1)} %select_maximum_fusion.14, f32[1,256,256]{1,2,0:T(8,128)} %collective-permute-done.1, ...), kind=kLoop, calls=%fused_computation.120 | loop fusion | flops 9961471 | bytes 19398660 | tf_op jit(solution)/shard_map/reduce_sum | solution.py:70
  82.6 4.4 %collective-permute-start.3 = (f32[1,256,256]{1,2,0:T(8,128)S(1)}, f32[1,256,256]{1,2,0:T(8,128)S(1)}, u32[]{:S(2)}, u32[]{:S(2)}) collective-permute-start(f32[1,256,256]{1,2,0:T(8,128)S(1)} %get-tuple-element.89), channel_id=1, source_target_pairs={{0,1},{1,2},{2,3},{3,4},{4,5},{5,6},{6,7},{7,8},{8,9},{9,10},{10,1... | collective-permute-start | bytes 786440 | tf_op jit(solution)/shard_map/ppermute | solution.py:18
  91.0 3.1 multiply_reduce_fusion.2
  95.4 9.1 %collective-permute-start.5 = (f32[1,256,256]{1,2,0:T(8,128)S(1)}, f32[1,256,256]{1,2,0:T(8,128)S(1)}, u32[]{:S(2)}, u32[]{:S(2)}) collective-permute-start(f32[1,256,256]{1,2,0:T(8,128)S(1)} %get-tuple-element.87), channel_id=1, source_target_pairs={{0,1},{1,2},{2,3},{3,4},{4,5},{5,6},{6,7},{7,8},{8,9},{9,10},{10,1... | collective-permute-start | bytes 786440 | tf_op jit(solution)/shard_map/ppermute | solution.py:18
  108.6 3.1 multiply_reduce_fusion.1
  114.4 8.3 %collective-permute-start.7 = (f32[1,256,256]{1,2,0:T(8,128)S(1)}, f32[1,256,256]{1,2,0:T(8,128)S(1)}, u32[]{:S(2)}, u32[]{:S(2)}) collective-permute-start(f32[1,256,256]{1,2,0:T(8,128)S(1)} %get-tuple-element.85), channel_id=1, source_target_pairs={{0,1},{1,2},{2,3},{3,4},{4,5},{5,6},{6,7},{7,8},{8,9},{9,10},{10,1... | collective-permute-start | bytes 786440 | tf_op jit(solution)/shard_map/ppermute | solution.py:18
  124.0 3.4 select_maximum_fusion.8
  127.5 4.1 %multiply_reduce_fusion = (f32[]{:T(128)}, f32[8,256,256]{1,2,0:T(8,128)}) fusion(f32[8,256,256]{1,2,0:T(8,128)S(1)} %scatter-add.30, f32[8,256,256]{1,2,0:T(8,128)S(1)} %copy-done.3, f32[8,256,256]{1,2,0:T(8,128)S(1)} %copy-done.11, f32[10,258,258]{1,2,0:T(8,128)S(1)} %select_maximum_fusion.8, f32[1,256,256]{1,2,0:T(8,128)S(1)} %collective-permute-done.7, ...), kind=kLoop, calls=%fused_computation.117 | loop fusion | flops 9961471 | bytes 19398660 | tf_op jit(solution)/shard_map/reduce_sum | solution.py:70
  134.1 34.5 %psum.7 = f32[4]{0:T(128)S(1)} all-reduce(f32[4]{0:T(128)S(1)} %reverse.3), channel_id=1, replica_groups=mesh['groups'=2,'gx'=16] {'gx'}, use_global_device_ids=true, to_apply=%region_4.5 | all-reduce | flops 4 | bytes 32 | tf_op jit(solution)/shard_map/psum | solution.py:71
  174.4 3.0 collective-permute-start.9
  178.6 2.8 select_maximum_fusion.6
  185.6 4.7 %collective-permute-start.11 = (f32[1,256,256]{1,2,0:T(8,128)S(1)}, f32[1,256,256]{1,2,0:T(8,128)S(1)}, u32[]{:S(2)}, u32[]{:S(2)}) collective-permute-start(f32[1,256,256]{1,2,0:T(8,128)S(1)} %get-tuple-element.81), channel_id=1, source_target_pairs={{0,1},{1,2},{2,3},{3,4},{4,5},{5,6},{6,7},{7,8},{8,9},{9,10},{10,1... | collective-permute-start | bytes 786440 | tf_op jit(solution)/shard_map/ppermute | solution.py:18
  191.4 2.9 select_maximum_fusion.4
  194.3 4.0 %fusion.53 = (f32[8,256,256]{1,2,0:T(8,128)S(1)}, f32[8,256,256]{1,2,0:T(8,128)}) fusion(f32[8,256,256]{1,2,0:T(8,128)S(1)} %copy-done.4, f32[8,256,256]{1,2,0:T(8,128)S(1)} %copy-done.8, f32[]{:T(128)} %bitcast.13, f32[8,256,256]{1,2,0:T(8,128)S(1)} %copy-done.17, f32[]{:T(128)} %bitcast.11, f32[8,256,256]{1,2,0:T(8,128)S(1)} %scatter-add.30, ...), kind=kLoop, calls=%fused_computation.141 | loop fusion | flops 11534336 | bytes 25690120 | tf_op jit(solution)/shard_map/mul | solution.py:84
  200.9 7.4 %collective-permute-start.13 = (f32[1,256,256]{1,2,0:T(8,128)S(1)}, f32[1,256,256]{1,2,0:T(8,128)S(1)}, u32[]{:S(2)}, u32[]{:S(2)}) collective-permute-start(f32[1,256,256]{1,2,0:T(8,128)S(1)} %get-tuple-element.79), channel_id=1, source_target_pairs={{0,1},{1,2},{2,3},{3,4},{4,5},{5,6},{6,7},{7,8},{8,9},{9,10},{10,1... | collective-permute-start | bytes 786440 | tf_op jit(solution)/shard_map/ppermute | solution.py:18
  210.3 3.5 %select_maximum_fusion.2 = f32[10,258,258]{1,2,0:T(8,128)S(1)} fusion(f32[1,256,256]{1,2,0:T(8,128)S(1)} %collective-permute-done.12, f32[8,256,256]{1,2,0:T(8,128)} %copy-done.18, f32[1,256,256]{1,2,0:T(8,128)S(1)} %collective-permute-done.13), kind=kLoop, calls=%fused_computation.8 | loop fusion | flops 9984600 | bytes 5284000 | tf_op jit(solution)/shard_map/concatenate | solution.py:16
  213.9 8.9 %multiply_add_fusion = (f32[8,256,256]{1,2,0:T(8,128)}, f32[8,256,256]{1,2,0:T(8,128)S(1)}) fusion(f32[8,256,256]{1,2,0:T(8,128)} %copy.49, f32[8,256,256]{1,2,0:T(8,128)} %copy-done.16, f32[8,256,256]{1,2,0:T(8,128)} %get-tuple-element.60, f32[8,256,256]{1,2,0:T(8,128)S(1)} %copy-done.15, f32[8,256,256]{1,2,0:T(8,128)S(1)} %copy-done.9, ...), kind=kLoop, calls=%fused_computation.115 | loop fusion | flops 16777216 | bytes 34078728 | tf_op jit(solution)/shard_map/add | solution.py:83
  222.8 4.0 %fusion.61 = (f32[8,1,256]{1,2,0:T(8,128)}, f32[8,1,256]{1,2,0:T(8,128)}) fusion(f32[8,256,256]{1,2,0:T(8,128)} %get-tuple-element.57), kind=kLoop, calls=%fused_computation.143 | loop fusion | bytes 32768 | tf_op jit(solution)/shard_map/slice | solution.py:49
  230.6 7.4 %collective-permute-start.15 = (f32[1,256,256]{1,2,0:T(8,128)}, f32[1,256,256]{1,2,0:T(8,128)}, u32[]{:S(2)}, u32[]{:S(2)}) collective-permute-start(f32[1,256,256]{1,2,0:T(8,128)} %get-tuple-element.77), channel_id=1, source_target_pairs={{0,1},{1,2},{2,3},{3,4},{4,5},{5,6},{6,7},{7,8},{8,9},{9,10},{10,1... | collective-permute-start | bytes 786440 | tf_op jit(solution)/shard_map/ppermute | solution.py:18
  240.9 57.0 %scatter_custom_fusion = f32[160]{0:T(256)S(1)} fusion(s32[8192]{0:T(1024)S(1)} %bitcast.42, f32[8192]{0:T(1024)S(1)} %bitcast.43, f32[]{:T(128)} %constant.131.clone.1), kind=kCustom, calls=%fused_computation.136 | custom fusion | flops 8192 | bytes 644 | tf_op jit(solution)/shard_map/scatter-add | solution.py:93
  297.9 31.2 %all-reduce.9 = f32[160]{0:T(256)S(1)} all-reduce(f32[160]{0:T(256)S(1)} %scatter_custom_fusion), channel_id=2, replica_groups=mesh['groups'=2,'gx'=16] {'gx'}, use_global_device_ids=true, to_apply=%region_8.9.clone | all-reduce | flops 160 | bytes 1280
  329.7 3.5 %select_maximum_fusion = f32[10,258,258]{1,2,0:T(8,128)S(1)} fusion(f32[1,256,256]{1,2,0:T(8,128)S(1)} %collective-permute-done.14, f32[8,256,256]{1,2,0:T(8,128)} %copy-done.19, f32[1,256,256]{1,2,0:T(8,128)} %collective-permute-done.15), kind=kLoop, calls=%fused_computation.6 | loop fusion | flops 9984600 | bytes 5284000 | tf_op jit(solution)/shard_map/concatenate | solution.py:16
  333.3 4.7 %fusion.5 = (f32[8,256,256]{1,2,0:T(8,128)}, f32[8,256,256]{1,2,0:T(8,128)}) fusion(f32[10,258,258]{1,2,0:T(8,128)S(1)} %select_maximum_fusion, f32[8,256,256]{1,2,0:T(8,128)S(1)} %copy-done.20, f32[1,256,256]{1,2,0:T(8,128)} %collective-permute-done.15, f32[1,256,256]{1,2,0:T(8,128)S(1)} %collective-permute-done.14, f32[8,256,256]{1,2,0:T(8,128)S(1)} %copy-done.22, ...), kind=kLoop, calls=%fused_computation.28 | loop fusion | flops 8388608 | bytes 21495808 | tf_op jit(solution)/shard_map/sub | solution.py:86
  338.0 2.9 copy.70
  340.9 2.9 copy.71
  (129 shorter events, 42.1 us)
Async XLA Ops:
  0.6 9.9 %copy-start = (f32[160]{0:T(256)S(1)}, f32[160]{0:T(256)}, u32[]{:S(2)}) copy-start(f32[160]{0:T(256)} %param.20) | copy-start | bytes 1924
  0.6 9.8 %copy-start.29 = (s32[8,4,256]{2,1,0:T(4,128)S(1)}, s32[8,4,256]{2,1,0:T(4,128)}, u32[]{:S(2)}) copy-start(s32[8,4,256]{2,1,0:T(4,128)} %param.19) | copy-start | bytes 98308
  5.4 68.2 %collective-permute-start = (f32[1,256,256]{1,2,0:T(8,128)}, f32[1,256,256]{1,2,0:T(8,128)S(1)}, u32[]{:S(2)}, u32[]{:S(2)}) collective-permute-start(f32[1,256,256]{1,2,0:T(8,128)} %get-tuple-element.92), channel_id=1, source_target_pairs={{1,0},{2,1},{3,2},{4,3},{5,4},{6,5},{7,6},{8,7},{9,8},{10,9},{11,1... | collective-permute-start | bytes 786440 | tf_op jit(solution)/shard_map/ppermute | solution.py:20
  6.7 67.0 %collective-permute-start.1 = (f32[1,256,256]{1,2,0:T(8,128)}, f32[1,256,256]{1,2,0:T(8,128)}, u32[]{:S(2)}, u32[]{:S(2)}) collective-permute-start(f32[1,256,256]{1,2,0:T(8,128)} %get-tuple-element.91), channel_id=1, source_target_pairs={{0,1},{1,2},{2,3},{3,4},{4,5},{5,6},{6,7},{7,8},{8,9},{9,10},{10,1... | collective-permute-start | bytes 786440 | tf_op jit(solution)/shard_map/ppermute | solution.py:18
  73.7 3.6 %copy-start.25 = (f32[8,256,256]{1,2,0:T(8,128)S(1)}, f32[8,256,256]{1,2,0:T(8,128)}, u32[]{:S(2)}) copy-start(f32[8,256,256]{1,2,0:T(8,128)} %copy.49) | copy-start | bytes 6291460
  81.2 27.3 %copy-start.16 = (f32[8,256,256]{1,2,0:T(8,128)}, f32[8,256,256]{1,2,0:T(8,128)S(1)}, u32[]{:S(2)}) copy-start(f32[8,256,256]{1,2,0:T(8,128)S(1)} %get-tuple-element.64) | copy-start | bytes 6291460
  81.3 5.8 %collective-permute-start.2 = (f32[1,256,256]{1,2,0:T(8,128)S(1)}, f32[1,256,256]{1,2,0:T(8,128)S(1)}, u32[]{:S(2)}, u32[]{:S(2)}) collective-permute-start(f32[1,256,256]{1,2,0:T(8,128)S(1)} %get-tuple-element.90), channel_id=1, source_target_pairs={{1,0},{2,1},{3,2},{4,3},{5,4},{6,5},{7,6},{8,7},{9,8},{10,9},{11,1... | collective-permute-start | bytes 786440 | tf_op jit(solution)/shard_map/ppermute | solution.py:20
  82.6 5.6 %collective-permute-start.3 = (f32[1,256,256]{1,2,0:T(8,128)S(1)}, f32[1,256,256]{1,2,0:T(8,128)S(1)}, u32[]{:S(2)}, u32[]{:S(2)}) collective-permute-start(f32[1,256,256]{1,2,0:T(8,128)S(1)} %get-tuple-element.89), channel_id=1, source_target_pairs={{0,1},{1,2},{2,3},{3,4},{4,5},{5,6},{6,7},{7,8},{8,9},{9,10},{10,1... | collective-permute-start | bytes 786440 | tf_op jit(solution)/shard_map/ppermute | solution.py:18
  94.1 14.5 %copy-start.6 = (f32[8,256,256]{1,2,0:T(8,128)}, f32[8,256,256]{1,2,0:T(8,128)S(1)}, u32[]{:S(2)}) copy-start(f32[8,256,256]{1,2,0:T(8,128)S(1)} %get-tuple-element.66) | copy-start | bytes 6291460
  94.1 10.4 %collective-permute-start.4 = (f32[1,256,256]{1,2,0:T(8,128)S(1)}, f32[1,256,256]{1,2,0:T(8,128)S(1)}, u32[]{:S(2)}, u32[]{:S(2)}) collective-permute-start(f32[1,256,256]{1,2,0:T(8,128)S(1)} %get-tuple-element.88), channel_id=1, source_target_pairs={{1,0},{2,1},{3,2},{4,3},{5,4},{6,5},{7,6},{8,7},{9,8},{10,9},{11,1... | collective-permute-start | bytes 786440 | tf_op jit(solution)/shard_map/ppermute | solution.py:20
  95.4 10.3 %collective-permute-start.5 = (f32[1,256,256]{1,2,0:T(8,128)S(1)}, f32[1,256,256]{1,2,0:T(8,128)S(1)}, u32[]{:S(2)}, u32[]{:S(2)}) collective-permute-start(f32[1,256,256]{1,2,0:T(8,128)S(1)} %get-tuple-element.87), channel_id=1, source_target_pairs={{0,1},{1,2},{2,3},{3,4},{4,5},{5,6},{6,7},{7,8},{8,9},{9,10},{10,1... | collective-permute-start | bytes 786440 | tf_op jit(solution)/shard_map/ppermute | solution.py:18
  113.1 10.9 %collective-permute-start.6 = (f32[1,256,256]{1,2,0:T(8,128)S(1)}, f32[1,256,256]{1,2,0:T(8,128)S(1)}, u32[]{:S(2)}, u32[]{:S(2)}) collective-permute-start(f32[1,256,256]{1,2,0:T(8,128)S(1)} %get-tuple-element.86), channel_id=1, source_target_pairs={{1,0},{2,1},{3,2},{4,3},{5,4},{6,5},{7,6},{8,7},{9,8},{10,9},{11,1... | collective-permute-start | bytes 786440 | tf_op jit(solution)/shard_map/ppermute | solution.py:20
  114.4 9.6 %collective-permute-start.7 = (f32[1,256,256]{1,2,0:T(8,128)S(1)}, f32[1,256,256]{1,2,0:T(8,128)S(1)}, u32[]{:S(2)}, u32[]{:S(2)}) collective-permute-start(f32[1,256,256]{1,2,0:T(8,128)S(1)} %get-tuple-element.85), channel_id=1, source_target_pairs={{0,1},{1,2},{2,3},{3,4},{4,5},{5,6},{6,7},{7,8},{8,9},{9,10},{10,1... | collective-permute-start | bytes 786440 | tf_op jit(solution)/shard_map/ppermute | solution.py:18
  127.5 41.5 %copy-start.30 = (f32[64]{0:T(128)S(1)}, f32[64]{0:T(128)}, u32[]{:S(2)}) copy-start(f32[64]{0:T(128)} %param.22) | copy-start | bytes 772
  173.1 5.0 %collective-permute-start.8 = (f32[1,256,256]{1,2,0:T(8,128)S(1)}, f32[1,256,256]{1,2,0:T(8,128)S(1)}, u32[]{:S(2)}, u32[]{:S(2)}) collective-permute-start(f32[1,256,256]{1,2,0:T(8,128)S(1)} %get-tuple-element.84), channel_id=1, source_target_pairs={{1,0},{2,1},{3,2},{4,3},{5,4},{6,5},{7,6},{8,7},{9,8},{10,9},{11,1... | collective-permute-start | bytes 786440 | tf_op jit(solution)/shard_map/ppermute | solution.py:20
  174.4 4.2 %collective-permute-start.9 = (f32[1,256,256]{1,2,0:T(8,128)S(1)}, f32[1,256,256]{1,2,0:T(8,128)S(1)}, u32[]{:S(2)}, u32[]{:S(2)}) collective-permute-start(f32[1,256,256]{1,2,0:T(8,128)S(1)} %get-tuple-element.83), channel_id=1, source_target_pairs={{0,1},{1,2},{2,3},{3,4},{4,5},{5,6},{6,7},{7,8},{8,9},{9,10},{10,1... | collective-permute-start | bytes 786440 | tf_op jit(solution)/shard_map/ppermute | solution.py:18
  184.2 10.1 %copy-start.21 = (f32[8,256,256]{1,2,0:T(8,128)}, f32[8,256,256]{1,2,0:T(8,128)S(1)}, u32[]{:S(2)}) copy-start(f32[8,256,256]{1,2,0:T(8,128)S(1)} %get-tuple-element.62) | copy-start | bytes 6291460
  184.3 6.6 %collective-permute-start.10 = (f32[1,256,256]{1,2,0:T(8,128)S(1)}, f32[1,256,256]{1,2,0:T(8,128)S(1)}, u32[]{:S(2)}, u32[]{:S(2)}) collective-permute-start(f32[1,256,256]{1,2,0:T(8,128)S(1)} %get-tuple-element.82), channel_id=1, source_target_pairs={{1,0},{2,1},{3,2},{4,3},{5,4},{6,5},{7,6},{8,7},{9,8},{10,9},{11,1... | collective-permute-start | bytes 786440 | tf_op jit(solution)/shard_map/ppermute | solution.py:20
  185.6 5.9 %collective-permute-start.11 = (f32[1,256,256]{1,2,0:T(8,128)S(1)}, f32[1,256,256]{1,2,0:T(8,128)S(1)}, u32[]{:S(2)}, u32[]{:S(2)}) collective-permute-start(f32[1,256,256]{1,2,0:T(8,128)S(1)} %get-tuple-element.81), channel_id=1, source_target_pairs={{0,1},{1,2},{2,3},{3,4},{4,5},{5,6},{6,7},{7,8},{8,9},{9,10},{10,1... | collective-permute-start | bytes 786440 | tf_op jit(solution)/shard_map/ppermute | solution.py:18
  194.3 14.1 %copy-start.31 = (u32[32]{0:T(128)S(1)}, u32[32]{0:T(128)}, u32[]{:S(2)}) copy-start(u32[32]{0:T(128)} %constant.165) | copy-start | bytes 388
  199.6 10.6 %collective-permute-start.12 = (f32[1,256,256]{1,2,0:T(8,128)S(1)}, f32[1,256,256]{1,2,0:T(8,128)S(1)}, u32[]{:S(2)}, u32[]{:S(2)}) collective-permute-start(f32[1,256,256]{1,2,0:T(8,128)S(1)} %get-tuple-element.80), channel_id=1, source_target_pairs={{1,0},{2,1},{3,2},{4,3},{5,4},{6,5},{7,6},{8,7},{9,8},{10,9},{11,1... | collective-permute-start | bytes 786440 | tf_op jit(solution)/shard_map/ppermute | solution.py:20
  200.9 9.3 %collective-permute-start.13 = (f32[1,256,256]{1,2,0:T(8,128)S(1)}, f32[1,256,256]{1,2,0:T(8,128)S(1)}, u32[]{:S(2)}, u32[]{:S(2)}) collective-permute-start(f32[1,256,256]{1,2,0:T(8,128)S(1)} %get-tuple-element.79), channel_id=1, source_target_pairs={{0,1},{1,2},{2,3},{3,4},{4,5},{5,6},{6,7},{7,8},{8,9},{9,10},{10,1... | collective-permute-start | bytes 786440 | tf_op jit(solution)/shard_map/ppermute | solution.py:18
  210.2 3.6 %copy-start.9 = (f32[8,256,256]{1,2,0:T(8,128)S(1)}, f32[8,256,256]{1,2,0:T(8,128)}, u32[]{:S(2)}) copy-start(f32[8,256,256]{1,2,0:T(8,128)} %copy-done.6) | copy-start | bytes 6291460
  210.2 3.6 %copy-start.13 = (f32[8,256,256]{1,2,0:T(8,128)S(1)}, f32[8,256,256]{1,2,0:T(8,128)}, u32[]{:S(2)}) copy-start(f32[8,256,256]{1,2,0:T(8,128)} %copy-done.10) | copy-start | bytes 6291460
  210.2 3.7 %copy-start.15 = (f32[8,256,256]{1,2,0:T(8,128)S(1)}, f32[8,256,256]{1,2,0:T(8,128)}, u32[]{:S(2)}) copy-start(f32[8,256,256]{1,2,0:T(8,128)} %copy.48) | copy-start | bytes 6291460
  210.3 3.6 %copy-start.27 = (f32[1,256,256]{1,2,0:T(8,128)}, f32[1,256,256]{1,2,0:T(8,128)S(1)}, u32[]{:S(2)}) copy-start(f32[1,256,256]{1,2,0:T(8,128)S(1)} %collective-permute-done.12) | copy-start | bytes 786436
  222.8 4.0 %copy-start.23 = (f32[8,256,256]{1,2,0:T(8,128)}, f32[8,256,256]{1,2,0:T(8,128)S(1)}, u32[]{:S(2)}) copy-start(f32[8,256,256]{1,2,0:T(8,128)S(1)} %get-tuple-element.58) | copy-start | bytes 6291460
  222.8 4.0 %copy-start.5 = (f32[8,256,256]{1,2,0:T(8,128)S(1)}, f32[8,256,256]{1,2,0:T(8,128)}, u32[]{:S(2)}) copy-start(f32[8,256,256]{1,2,0:T(8,128)} %copy.56) | copy-start | bytes 6291460
  228.5 12.0 %copy-start.26 = (f32[8,1,256]{1,2,0:T(8,128)S(1)}, f32[8,1,256]{1,2,0:T(8,128)}, u32[]{:S(2)}) copy-start(f32[8,1,256]{1,2,0:T(8,128)} %get-tuple-element.74) | copy-start | bytes 24580
  229.3 100.4 %collective-permute-start.14 = (f32[1,256,256]{1,2,0:T(8,128)}, f32[1,256,256]{1,2,0:T(8,128)S(1)}, u32[]{:S(2)}, u32[]{:S(2)}) collective-permute-start(f32[1,256,256]{1,2,0:T(8,128)} %get-tuple-element.78), channel_id=1, source_target_pairs={{1,0},{2,1},{3,2},{4,3},{5,4},{6,5},{7,6},{8,7},{9,8},{10,9},{11,1... | collective-permute-start | bytes 786440 | tf_op jit(solution)/shard_map/ppermute | solution.py:20
  230.6 99.1 %collective-permute-start.15 = (f32[1,256,256]{1,2,0:T(8,128)}, f32[1,256,256]{1,2,0:T(8,128)}, u32[]{:S(2)}, u32[]{:S(2)}) collective-permute-start(f32[1,256,256]{1,2,0:T(8,128)} %get-tuple-element.77), channel_id=1, source_target_pairs={{0,1},{1,2},{2,3},{3,4},{4,5},{5,6},{6,7},{7,8},{8,9},{9,10},{10,1... | collective-permute-start | bytes 786440 | tf_op jit(solution)/shard_map/ppermute | solution.py:18
  329.7 3.6 %copy-start.24 = (f32[8,256,256]{1,2,0:T(8,128)S(1)}, f32[8,256,256]{1,2,0:T(8,128)}, u32[]{:S(2)}) copy-start(f32[8,256,256]{1,2,0:T(8,128)} %copy-done.23) | copy-start | bytes 6291460
  (16 other events, 48.5 us)
where the time goes:
time: 345 us; the launch traced here: 344 us
  other arithmetic  123 us (36%)
  local copies, waits for them, and re-layouts  87.3 us (25%)
  blocking collectives  65.8 us (19%)
  starting transfers between devices  58.5 us (17%)
  between operations  5.71 us (2%)
    scatter-add x1, other arithmetic, on_device(): jax.ops.segment_sum(faces_grad.reshape(-1), patch_map.reshape(-1), absorb...  57 us
    gather x2, local copies, waits for them, and re-layouts, on_device(): face_absorb = absorb[patch_map]  51 us
    ppermute x8, starting transfers between devices, extended(): lax.ppermute(tail, axis, [(i, (i + 1) % count) for i in range(ends)])  48.2 us
    psum x1, blocking collectives, on_device(): energy = lax.psum(local_energy, 'gx') / all_cells  34.5 us
    unnamed x1, blocking collectives  31.2 us
    concatenate x8, other arithmetic, extended(): jnp.concatenate([lax.ppermute(tail, axis, [(i, (i + 1) % count) for i in...  25.3 us
    unnamed x77, local copies, waits for them, and re-layouts  23.1 us
    reduce_sum x4, other arithmetic, on_device(): local_energy = jnp.stack([jnp.sum(field * field) for field in states[2:]])  14.2 us
  transfers between devices with their start and end apart: 16, of which 4 were waited for; matrix products, arithmetic and copies ran while one was open for 36% of the time, Pallas kernels for 0%

commit v1 on v0

v1 whole, which is shorter than its diff:
```python
import functools

import jax
import jax.numpy as jnp
from jax import lax
from jax.experimental import pallas as pl
from jax.experimental.pallas import tpu as pltpu
from jax.sharding import PartitionSpec as P

STEPS = 4
PATCH_CELLS = 819
CHUNK = 32
LANES = 128
F32 = jnp.float32
VMEM = pltpu.VMEM
in_vmem = pl.BlockSpec(memory_space=pltpu.VMEM)
in_smem = pl.BlockSpec(memory_space=pltpu.SMEM)
in_hbm = pl.BlockSpec(memory_space=pltpu.HBM)


def end_layer(parity, side, depth, cx):
    high = 1 - parity if side == 0 else parity
    return high * (cx - 1 - depth) + (1 - high) * depth


def layer(ref, x):
    return lambda row, count: ref[x, pl.ds(row, count), :]


def flat(ref, base):
    return lambda row, count: ref[pl.ds(base + row, count), :]


def chunks(side_cells):
    return [(row, CHUNK) for row in range(0, side_cells, CHUNK)]


def beside(field, row, count, side_cells):
    v = field(row, count)
    sub = lax.broadcasted_iota(jnp.int32, v.shape, 0)
    lane = lax.broadcasted_iota(jnp.int32, v.shape, 1)
    if row == 0:
        above = jnp.where(sub == 0, 0.0, pltpu.roll(v, 1, 0))
    else:
        above = field(row - 1, count)
    if row + count == side_cells:
        below = jnp.where(sub == count - 1, 0.0, pltpu.roll(v, count - 1, 0))
    else:
        below = field(row + 1, count)
    left = jnp.where(lane == 0, 0.0, pltpu.roll(v, 1, 1))
    right = jnp.where(lane == v.shape[1] - 1, 0.0, pltpu.roll(v, v.shape[1] - 1, 1))
    return v, (above + below) + (left + right)


def forward(now, prior, courant, inverse, sides, row, count, side_cells):
    v, total = beside(now, row, count, side_cells)
    for other in sides:
        total = total + other(row, count)
    p = prior(row, count)
    c, i = courant(row, count), inverse(row, count)
    return i * (2.0 * (v - p) + c * (total - 6.0 * v)) + p


def backward(product, w, later, inverse, source, sides, row, count, side_cells):
    q, total = beside(product, row, count, side_cells)
    for other in sides:
        total = total + other(row, count)
    fresh = total - 6.0 * q + source
    i = inverse(row, count)
    if later is None:
        return i * (2.0 * w + fresh)
    return i * (2.0 * (w - later) + fresh) + later


def sweep(low, high, body):
    def turn(x, carry):
        body(x)
        return carry

    lax.fori_loop(low, high, turn, 0)


def x_sides(ref, x, cx):
    return [layer(ref, k) for k in (x - 1, x + 1) if not isinstance(k, int) or 0 <= k < cx]


def fold(values):
    total = values[0:8]
    for row in range(8, values.shape[0], 8):
        total = total + values[row : row + 8]
    return total


def start_kernel(parity_ref, u_hbm, a_ref, b_ref, sems):
    cx = u_hbm.shape[0]
    copies = []
    for side, out in enumerate((a_ref, b_ref)):
        x = end_layer(parity_ref[0], side, 0, cx)
        copies.append(pltpu.make_async_copy(u_hbm.at[x], out, sems.at[side]))
    for copy in copies:
        copy.start()
    for copy in copies:
        copy.wait()


def lookup(maps, absorb_ref):
    def turn(p, got):
        return jnp.where(maps == p, absorb_ref[p], got)

    return lax.fori_loop(0, absorb_ref.shape[0], turn, jnp.zeros(maps.shape, F32))


def put_column(acc_ref, spot, tile, lane_from):
    side_cells = acc_ref.shape[0]
    for row, count in chunks(side_cells):
        values = pltpu.roll(tile(row, count), (spot - lane_from) % LANES, 1)
        lane = lax.broadcasted_iota(jnp.int32, values.shape, 1)
        acc_ref[pl.ds(row, count), :] = jnp.where(
            lane == spot, values, acc_ref[pl.ds(row, count), :]
        )


def low_tile(field):
    return lambda row, count: field(row, count)[:, :LANES]


def high_tile(field):
    return lambda row, count: field(row, count)[:, -LANES:]


def setup_kernel(
    parity_ref, absorb_ref, map_ref, u_hbm, up_hbm, c_hbm,
    u, up, c, s, inv, pay_a, pay_b,
    maps, found, turned, columns, sems,
):
    cx, side_cells = u.shape[0], u.shape[1]
    copies = [
        pltpu.make_async_copy(src, dst, sems.at[k])
        for k, (src, dst) in enumerate(((u_hbm, u), (up_hbm, up), (c_hbm, c)))
    ]
    for copy in copies:
        copy.start()
    for x in range(cx):
        maps[4 * x : 4 * x + 4, :] = map_ref[x]
    found[...] = lookup(maps[...], absorb_ref)
    turned[...] = jnp.zeros_like(turned)
    for x in range(cx):
        turned[x : x + 1, :] = found[4 * x + 2 : 4 * x + 3, :]
        turned[cx + x : cx + x + 1, :] = found[4 * x + 3 : 4 * x + 4, :]
    columns[...] = jnp.transpose(turned[...])

    def spread(x, carry):
        for row, count in chunks(side_cells):
            tile = columns[pl.ds(row, count), :]
            lane = lax.broadcasted_iota(jnp.int32, tile.shape, 1)
            near = jnp.where(lane == 0, pltpu.roll(tile, lax.rem(LANES - x, LANES), 1), 0.0)
            far = jnp.where(lane == LANES - 1, pltpu.roll(tile, LANES - 1 - cx - x, 1), 0.0)
            mid = [jnp.zeros_like(near)] * (side_cells // LANES - 2)
            field = jnp.concatenate([near, *mid, far], axis=1)
            sub = lax.broadcasted_iota(jnp.int32, field.shape, 0)
            if row == 0:
                field = field + jnp.where(sub == 0, found[pl.ds(4 * x, 1), :], 0.0)
            if row + count == side_cells:
                field = field + jnp.where(sub == count - 1, found[pl.ds(4 * x + 1, 1), :], 0.0)
            s[x, pl.ds(row, count), :] = field
            inv[x, pl.ds(row, count), :] = 1.0 / (1.0 + field)
        return carry

    lax.fori_loop(0, cx, spread, 0)
    for copy in copies:
        copy.wait()
    columns[...] = jnp.zeros_like(columns)
    for side, pay in enumerate((pay_a, pay_b)):
        x0 = end_layer(parity_ref[0], side, 0, cx)
        x1 = end_layer(parity_ref[0], side, 1, cx)
        for row, count in chunks(side_cells):
            pay[pl.ds(row, count), :] = forward(
                layer(u, x0), layer(up, x0), layer(c, x0), layer(inv, x0), [layer(u, x1)],
                row, count, side_cells,
            )
            pay[pl.ds(side_cells + row, count), :] = (
                c[x0, pl.ds(row, count), :] * inv[x0, pl.ds(row, count), :]
            )
        put_column(columns, 2 * side, low_tile(layer(up, x0)), 0)
        put_column(columns, 2 * side + 1, high_tile(layer(up, x0)), LANES - 1)
    rows = jnp.transpose(columns[...])
    for side, pay in enumerate((pay_a, pay_b)):
        x0 = end_layer(parity_ref[0], side, 0, cx)
        base = 2 * side_cells
        pay[base : base + 1, :] = up[x0, 0:1, :]
        pay[base + 1 : base + 2, :] = up[x0, side_cells - 1 : side_cells, :]
        pay[base + 2 : base + 4, :] = rows[2 * side : 2 * side + 2, :]
        pay[base + 4 : base + 8, :] = map_ref[x0].astype(F32)


def ahead_kernel(u, up, c, inv, u1, u2):
    cx, side_cells = u.shape[0], u.shape[1]

    def first(x):
        for row, count in chunks(side_cells):
            u1[x, pl.ds(row, count), :] = forward(
                layer(u, x), layer(up, x), layer(c, x), layer(inv, x), x_sides(u, x, cx),
                row, count, side_cells,
            )

    def second(x):
        for row, count in chunks(side_cells):
            u2[x, pl.ds(row, count), :] = forward(
                layer(u1, x), layer(u, x), layer(c, x), layer(inv, x), x_sides(u1, x, cx),
                row, count, side_cells,
            )

    first(0)
    sweep(1, cx - 1, first)
    first(cx - 1)
    sweep(2, cx - 2, second)


def finish_step(x0, now, fresh, c, inv, got_now, got_part, got_b, halo, side_cells):
    for row, count in chunks(side_cells):
        b = c[x0, pl.ds(row, count), :] * inv[x0, pl.ds(row, count), :]
        fresh[x0, pl.ds(row, count), :] += b * got_now(row, count)
        halo[pl.ds(row, count), :] = got_part(row, count) + got_b(row, count) * now[
            x0, pl.ds(row, count), :
        ]


def join_first_kernel(
    parity_ref, u, c, inv, near_a, near_b, got_a, got_b, u1_in, u2_in,
    u1, u2, halo_a, halo_b, pay_a, pay_b,
):
    cx, side_cells = u.shape[0], u.shape[1]
    for side, (near, got, halo, pay) in enumerate(
        ((near_a, got_a, halo_a, pay_a), (near_b, got_b, halo_b, pay_b))
    ):
        x0, x1, x2 = (end_layer(parity_ref[0], side, k, cx) for k in range(3))
        finish_step(
            x0, u, u1, c, inv, flat(near, 0), flat(got, 0), flat(got, side_cells), halo, side_cells
        )
        for row, count in chunks(side_cells):
            value = forward(
                layer(u1, x0), layer(u, x0), layer(c, x0), layer(inv, x0),
                [layer(u1, x1), flat(halo, 0)], row, count, side_cells,
            )
            u2[x0, pl.ds(row, count), :] = value
            pay[pl.ds(row, count), :] = value
            u2[x1, pl.ds(row, count), :] = forward(
                layer(u1, x1), layer(u, x1), layer(c, x1), layer(inv, x1),
                [layer(u1, x0), layer(u1, x2)], row, count, side_cells,
            )
        for row, count in chunks(side_cells):
            pay[pl.ds(side_cells + row, count), :] = forward(
                layer(u2, x0), layer(u1, x0), layer(c, x0), layer(inv, x0), [layer(u2, x1)],
                row, count, side_cells,
            )


def ahead_again_kernel(u1, u2, c, inv, u3, u4, energy):
    cx, side_cells = u1.shape[0], u1.shape[1]
    energy[...] = jnp.zeros_like(energy)

    def first(x, inner):
        for row, count in chunks(side_cells):
            value = forward(
                layer(u2, x), layer(u1, x), layer(c, x), layer(inv, x), x_sides(u2, x, cx),
                row, count, side_cells,
            )
            u3[x, pl.ds(row, count), :] = value
            energy[0] += fold(u1[x, pl.ds(row, count), :] ** 2)
            energy[1] += fold(u2[x, pl.ds(row, count), :] ** 2)
            if inner:
                energy[2] += fold(value * value)

    def second(x):
        for row, count in chunks(side_cells):
            value = forward(
                layer(u3, x), layer(u2, x), layer(c, x), layer(inv, x), x_sides(u3, x, cx),
                row, count, side_cells,
            )
            u4[x, pl.ds(row, count), :] = value
            energy[3] += fold(value * value)

    first(0, False)
    sweep(1, cx - 1, lambda x: first(x, True))
    first(cx - 1, False)
    sweep(2, cx - 2, second)


def join_second_kernel(
    parity_ref, u2, c, inv, energy_in, got_a, got_b, b_a, b_b, u3_in, u4_in,
    u3, u4, halo_a, halo_b, pay_a, pay_b, energy_rows, energy,
):
    cx, side_cells = u2.shape[0], u2.shape[1]
    energy[...] = energy_in[...]
    for side, (got, b, halo, pay) in enumerate(
        ((got_a, b_a, halo_a, pay_a), (got_b, b_b, halo_b, pay_b))
    ):
        x0, x1, x2 = (end_layer(parity_ref[0], side, k, cx) for k in range(3))
        finish_step(
            x0, u2, u3, c, inv, flat(got, 0), flat(got, side_cells), flat(b, side_cells), halo,
            side_cells,
        )
        for row, count in chunks(side_cells):
            energy[2] += fold(u3[x0, pl.ds(row, count), :] ** 2)
            value = forward(
                layer(u3, x0), layer(u2, x0), layer(c, x0), layer(inv, x0),
                [layer(u3, x1), flat(halo, 0)], row, count, side_cells,
            )
            u4[x0, pl.ds(row, count), :] = value
            pay[pl.ds(row, count), :] = (
                2.0 * c[x0, pl.ds(row, count), :] * inv[x0, pl.ds(row, count), :] * value
            )
            other = forward(
                layer(u3, x1), layer(u2, x1), layer(c, x1), layer(inv, x1),
                [layer(u3, x0), layer(u3, x2)], row, count, side_cells,
            )
            u4[x1, pl.ds(row, count), :] = other
            energy[3] += fold(value * value + other * other)

        def inner(row, count):
            at = pl.ds(row, count)
            return 2.0 * c[x1, at, :] * inv[x1, at, :] * u4[x1, at, :]

        for row, count in chunks(side_cells):
            at = pl.ds(row, count)
            w = 2.0 * inv[x0, at, :] * u4[x0, at, :]
            part = backward(
                flat(pay, 0), w, None, layer(inv, x0), 0.0, [inner], row, count, side_cells
            )
            pay[pl.ds(side_cells + row, count), :] = c[x0, at, :] * part
    lane = lax.broadcasted_iota(jnp.int32, energy_rows.shape, 1)
    rows = jnp.zeros(energy_rows.shape, F32)
    for n in range(STEPS):
        total = jnp.sum(jnp.sum(energy[n], axis=0, keepdims=True), axis=1, keepdims=True)
        rows = jnp.where(lane == n, total, rows)
    energy_rows[...] = rows


def adjoint_kernel(
    all_cells, checkpoint_ref, target_ref, tail_ref, sums, u2, u3, u4, c, inv,
    weights, w3, q3, w2, q2, q4,
):
    cx, side_cells = u2.shape[0], u2.shape[1]
    totals = jnp.sum(sums[...], axis=0, keepdims=True) / all_cells
    lane = lax.broadcasted_iota(jnp.int32, totals.shape, 1)
    start = jnp.clip(checkpoint_ref[0], 0, target_ref.shape[0] - STEPS)
    weight = jnp.zeros((1, 1), F32)
    g = []
    for n in range(STEPS):
        rest = jnp.where(jnp.logical_and(lane >= n, lane < STEPS), totals, 0.0)
        schroeder = tail_ref[0] + jnp.sum(rest, axis=1, keepdims=True)
        weight = weight + 2.0 * (jnp.log(schroeder) - target_ref[start + n]) / schroeder
        g.append(weight)
        weights[n : n + 1, :] = jnp.broadcast_to(weight, (1, LANES))
    twice = [2.0 * one for one in g]

    def zeroth(x):
        for row, count in chunks(side_cells):
            at = pl.ds(row, count)
            q4[x, at, :] = (twice[3] * c[x, at, :]) * (inv[x, at, :] * u4[x, at, :])

    def first(x):
        for row, count in chunks(side_cells):
            at = pl.ds(row, count)
            w = twice[3] * (inv[x, at, :] * u4[x, at, :])
            value = backward(
                layer(q4, x), w, None, layer(inv, x), twice[2] * u3[x, at, :],
                x_sides(q4, x, cx), row, count, side_cells,
            )
            w3[x, at, :] = value
            q3[x, at, :] = c[x, at, :] * value

    def second(x):
        for row, count in chunks(side_cells):
            at = pl.ds(row, count)
            later = twice[3] * (inv[x, at, :] * u4[x, at, :])
            value = backward(
                layer(q3, x), w3[x, at, :], later, layer(inv, x), twice[1] * u2[x, at, :],
                x_sides(q3, x, cx), row, count, side_cells,
            )
            w2[x, at, :] = value
            q2[x, at, :] = c[x, at, :] * value

    sweep(0, cx, zeroth)
    first(0)
    sweep(1, cx - 1, first)
    first(cx - 1)
    sweep(2, cx - 2, second)


def join_third_kernel(
    parity_ref, weights, u1, u2, u4, c, inv, u3h_a, u3h_b, got_a, got_b, b_a, b_b,
    w3_in, q3_in, w2_in, q2_in,
    w3, q3, w2, q2, pay_a, pay_b, halo,
):
    cx, side_cells = u2.shape[0], u2.shape[1]
    g = [weights[n : n + 1, 0:1] for n in range(STEPS)]
    for side, (u3h, got, b, pay) in enumerate(
        ((u3h_a, got_a, b_a, pay_a), (u3h_b, got_b, b_b, pay_b))
    ):
        x0, x1, x2 = (end_layer(parity_ref[0], side, k, cx) for k in range(3))
        for row, count in chunks(side_cells):
            at = pl.ds(row, count)
            i, cc = inv[x0, at, :], c[x0, at, :]
            value = w3[x0, at, :] + g[3] * (i * got[at, :])
            w3[x0, at, :] = value
            q3[x0, at, :] = cc * value
            own = 2.0 * cc * i * u4[x0, at, :]
            bh = b[pl.ds(side_cells + row, count), :]
            halo[at, :] = g[3] * (got[pl.ds(side_cells + row, count), :] + bh * own) + (
                2.0 * g[2]
            ) * (bh * u3h[at, :])
        for x, others in ((x0, [layer(q3, x1), flat(halo, 0)]), (x1, [layer(q3, x0), layer(q3, x2)])):
            for row, count in chunks(side_cells):
                at = pl.ds(row, count)
                later = (2.0 * g[3]) * (inv[x, at, :] * u4[x, at, :])
                value = backward(
                    layer(q3, x), w3[x, at, :], later, layer(inv, x),
                    (2.0 * g[1]) * u2[x, at, :], others, row, count, side_cells,
                )
                w2[x, at, :] = value
                q2[x, at, :] = c[x, at, :] * value
        for row, count in chunks(side_cells):
            at = pl.ds(row, count)
            pay[at, :] = q2[x0, at, :]
            pay[pl.ds(side_cells + row, count), :] = c[x0, at, :] * backward(
                layer(q2, x0), w2[x0, at, :], w3[x0, at, :], layer(inv, x0),
                (2.0 * g[0]) * u1[x0, at, :], [layer(q2, x1)], row, count, side_cells,
            )


def last_step(w1, q1, w2, s, x, at, sides, row, count, side_cells):
    q, total = beside(q1, row, count, side_cells)
    for other in sides:
        total = total + other(row, count)
    return 2.0 * w1(row, count) + total - 6.0 * q - (1.0 - s[x, at, :]) * w2[x, at, :]


def adjoint_end_kernel(weights, u1, w2, w3, q2, c, inv, s, w1, q1, cur_hbm, prev_hbm, cur, prev, sems):
    cx, side_cells = u1.shape[0], u1.shape[1]
    g0 = 2.0 * weights[0:1, 0:1]

    def first(x, inner):
        for row, count in chunks(side_cells):
            at = pl.ds(row, count)
            value = backward(
                layer(q2, x), w2[x, at, :], w3[x, at, :], layer(inv, x), g0 * u1[x, at, :],
                x_sides(q2, x, cx), row, count, side_cells,
            )
            w1[x, at, :] = value
            q1[x, at, :] = c[x, at, :] * value
            if inner:
                prev[x, at, :] = (s[x, at, :] - 1.0) * value

    def second(x):
        for row, count in chunks(side_cells):
            at = pl.ds(row, count)
            cur[x, at, :] = last_step(
                layer(w1, x), layer(q1, x), w2, s, x, at, x_sides(q1, x, cx), row, count, side_cells
            )

    first(0, False)
    sweep(1, cx - 1, lambda x: first(x, True))
    first(cx - 1, False)
    out_prev = pltpu.make_async_copy(
        prev.at[pl.ds(1, cx - 2)], prev_hbm.at[pl.ds(1, cx - 2)], sems.at[0]
    )
    out_prev.start()
    sweep(2, cx - 2, second)
    out_cur = pltpu.make_async_copy(
        cur.at[pl.ds(2, cx - 4)], cur_hbm.at[pl.ds(2, cx - 4)], sems.at[1]
    )
    out_cur.start()
    out_prev.wait()
    out_cur.wait()


def patch_kernel(
    own, absorb_ref, parity_ref, weights, map_ref, up, u, u1, u2, u3, u4, w3, w2, w1, q2, inv,
    u1h_a, u1h_b, got_a, got_b,
    sums, maps, values, columns,
):
    cx, side_cells = u.shape[0], u.shape[1]
    last = side_cells - 1
    g3 = 2.0 * weights[3:4, 0:1]
    columns[...] = jnp.zeros_like(columns)

    def field(x, at, lanes):
        k = (x, at, lanes)
        return (
            g3 * (inv[k] * u4[k]) * (u2[k] - u4[k])
            + w3[k] * (u1[k] - u3[k])
            + w2[k] * (u[k] - u2[k])
            + w1[k] * (up[k] - u1[k])
        )

    everything = pl.ds(0, side_cells)
    for x in range(cx):
        maps[4 * x : 4 * x + 4, :] = map_ref[x]
        values[4 * x : 4 * x + 1, :] = field(x, pl.ds(0, 8), everything)[0:1]
        values[4 * x + 1 : 4 * x + 2, :] = field(x, pl.ds(last - 7, 8), everything)[7:8]
        near = lambda row, count: field(x, pl.ds(row, count), pl.ds(0, LANES))
        far = lambda row, count: field(x, pl.ds(row, count), pl.ds(side_cells - LANES, LANES))
        put_column(columns, 2 * x, near, 0)
        put_column(columns, 2 * x + 1, far, LANES - 1)
    base = 2 * cx
    halves = ((u1h_a, got_a), (u1h_b, got_b))
    for side, (u1h, got) in enumerate(halves):
        x0 = end_layer(parity_ref[0], side, 0, cx)
        put_column(columns, base + 4 * side, low_tile(layer(q2, x0)), 0)
        put_column(columns, base + 4 * side + 1, high_tile(layer(q2, x0)), LANES - 1)
        put_column(columns, base + 4 * side + 2, low_tile(flat(u1h, 0)), 0)
        put_column(columns, base + 4 * side + 3, high_tile(flat(u1h, 0)), LANES - 1)
    rows = jnp.transpose(columns[...])
    for x in range(cx):
        values[4 * x + 2 : 4 * x + 4, :] = rows[2 * x : 2 * x + 2, :]
    for side, (u1h, got) in enumerate(halves):
        x0 = end_layer(parity_ref[0], side, 0, cx)
        extra = 2 * side_cells
        theirs = got[extra + 4 : extra + 8, :].astype(jnp.int32)
        damping = lookup(theirs, absorb_ref)
        lane = lax.broadcasted_iota(jnp.int32, (1, side_cells), 1)

        def corners(low, high):
            return jnp.where(lane == 0, low, 0.0) + jnp.where(lane == last, high, 0.0)

        d = [damping[f : f + 1] for f in range(4)]
        total = jnp.concatenate(
            [
                d[0] + corners(d[2][:, 0:1], d[3][:, 0:1]),
                d[1] + corners(d[2][:, last:], d[3][:, last:]),
                d[2] + corners(d[0][:, 0:1], d[1][:, 0:1]),
                d[3] + corners(d[0][:, last:], d[1][:, last:]),
            ],
            axis=0,
        )
        at = base + 4 * side
        mine = jnp.concatenate(
            [q2[x0, 0:1, :], q2[x0, last : last + 1, :], rows[at : at + 2, :]], axis=0
        )
        now = jnp.concatenate([u1h[0:1, :], u1h[last : last + 1, :], rows[at + 2 : at + 4, :]], axis=0)
        spot = 4 * cx + 4 * side
        values[spot : spot + 4, :] = mine * (got[extra : extra + 4, :] - now) / (1.0 + total)
        maps[spot : spot + 4, :] = theirs
    lane = lax.broadcasted_iota(jnp.int32, (1, LANES), 1)
    all_maps, all_values = maps[...], values[...]

    def owner(d, carry):
        row = jnp.zeros((1, LANES), F32)
        for j in range(own):
            picked = fold(jnp.where(all_maps == d * own + j, all_values, 0.0))
            half = picked[:, :LANES]
            for k in range(LANES, side_cells, LANES):
                half = half + picked[:, k : k + LANES]
            total = jnp.sum(jnp.sum(half, axis=0, keepdims=True), axis=1, keepdims=True)
            row = jnp.where(lane == j, total, row)
        sums[pl.ds(d, 1), :] = row
        return carry

    lax.fori_loop(0, sums.shape[0], owner, 0)


def join_last_kernel(
    parity_ref, w1, q1, w2, q2, c, inv, s, got_a, got_b, b_a, b_b, cur_in, prev_in,
    cur_hbm, prev_hbm, we, qe, halo, cur, prev, sems,
):
    cx, side_cells = w1.shape[0], w1.shape[1]
    copies = []
    for side, (got, b) in enumerate(((got_a, b_a), (got_b, b_b))):
        x0, x1, x2 = (end_layer(parity_ref[0], side, k, cx) for k in range(3))
        for row, count in chunks(side_cells):
            at = pl.ds(row, count)
            value = w1[x0, at, :] + inv[x0, at, :] * got[at, :]
            we[side, at, :] = value
            qe[side, at, :] = c[x0, at, :] * value
            prev[side, at, :] = (s[x0, at, :] - 1.0) * value
            below = pl.ds(side_cells + row, count)
            halo[at, :] = got[below, :] + b[below, :] * q2[x0, at, :]
        copies.append(pltpu.make_async_copy(prev.at[side], prev_hbm.at[x0], sems.at[3 * side]))
        copies[-1].start()
        for k, (x, w, q, others) in enumerate(
            (
                (x0, layer(we, side), layer(qe, side), [layer(q1, x1), flat(halo, 0)]),
                (x1, layer(w1, x1), layer(q1, x1), [layer(qe, side), layer(q1, x2)]),
            )
        ):
            for row, count in chunks(side_cells):
                at = pl.ds(row, count)
                cur[2 * side + k, at, :] = last_step(
                    w, q, w2, s, x, at, others, row, count, side_cells
                )
            copies.append(
                pltpu.make_async_copy(
                    cur.at[2 * side + k], cur_hbm.at[x], sems.at[3 * side + 1 + k]
                )
            )
            copies[-1].start()
    for copy in copies:
        copy.wait()


def call(kernel, ins, outs, scratch=(), aliases=None, name=None):
    kinds = {"v": in_vmem, "s": in_smem, "h": in_hbm}
    got = pl.pallas_call(
        kernel,
        out_shape=[
            pltpu.VMEM(shape, F32) if kind == "v" else jax.ShapeDtypeStruct(shape, F32)
            for kind, shape in outs
        ],
        in_specs=[kinds[kind] for kind, _ in ins],
        out_specs=[kinds[kind] for kind, _ in outs],
        scratch_shapes=list(scratch),
        input_output_aliases=aliases or {},
        compiler_params=pltpu.CompilerParams(vmem_limit_bytes=12 * 2**20),
        name=name,
    )(*[value for _, value in ins])
    return got


def on_device(u_prev, u_cur, courant_sq, patch_map, absorb, checkpoint, target_curve, tail_energy):
    cx, side = u_cur.shape[0], u_cur.shape[1]
    count = lax.axis_size("gx")
    patches = absorb.shape[0]
    own = patches // count
    all_cells = float(cx * count * side * side)
    field, plane = (cx, side, side), (side, side)
    double, triple = (2 * side, side), (2 * side + 8, side)
    parity = lax.rem(lax.axis_index("gx"), 2).astype(jnp.int32).reshape(1)
    within = [(i, i ^ 1) for i in range(count)]
    across = [(i, i + 1) for i in range(1, count - 1, 2)]
    across = across + [(j, i) for i, j in across]

    def swap(a, b):
        b = lax.ppermute(b, "gx", across)
        return lax.ppermute(a, "gx", within), b

    def deal(rows):
        return lax.all_to_all(rows, "gx", 0, 0, tiled=True)

    dma = pltpu.SemaphoreType.DMA
    sp, ab = ("s", parity), ("s", absorb)
    v = lambda *arrays: [("v", a) for a in arrays]
    near = call(
        start_kernel, [sp, ("h", u_cur)], [("v", plane)] * 2, [dma((2,))], name="edges"
    )
    near = swap(*near)
    u, up, c, s, inv, pay_a, pay_b = call(
        setup_kernel,
        [sp, ab, ("v", patch_map), ("h", u_cur), ("h", u_prev), ("h", courant_sq)],
        [("v", field)] * 5 + [("v", triple)] * 2,
        [
            VMEM((4 * cx, side), jnp.int32),
            VMEM((4 * cx, side), F32),
            VMEM((LANES, side), F32),
            VMEM((side, LANES), F32),
            dma((3,)),
        ],
        name="damping",
    )
    first = swap(pay_a, pay_b)
    u1, u2 = call(ahead_kernel, v(u, up, c, inv), [("v", field)] * 2, name="forward_1_2")
    u1, u2, u1h_a, u1h_b, pay_a, pay_b = call(
        join_first_kernel,
        [sp] + v(u, c, inv, *near, *first, u1, u2),
        [("v", field)] * 2 + [("v", plane)] * 2 + [("v", double)] * 2,
        aliases={8: 0, 9: 1},
        name="edges_1_2",
    )
    second = swap(pay_a, pay_b)
    u3, u4, energy = call(
        ahead_again_kernel,
        v(u1, u2, c, inv),
        [("v", field)] * 2 + [("v", (STEPS, 8, side))],
        name="forward_3_4",
    )
    u3, u4, u3h_a, u3h_b, pay_a, pay_b, energy_rows = call(
        join_second_kernel,
        [sp] + v(u2, c, inv, energy, *second, *first, u3, u4),
        [("v", field)] * 2 + [("v", plane)] * 2 + [("v", double)] * 2 + [("v", (count, LANES))],
        [VMEM((STEPS, 8, side), F32)],
        aliases={9: 0, 10: 1},
        name="edges_3_4",
    )
    third = swap(pay_a, pay_b)
    sums = deal(energy_rows)
    weights, w3, q3, w2, q2 = call(
        functools.partial(adjoint_kernel, all_cells),
        [("s", checkpoint), ("s", target_curve), ("s", tail_energy)] + v(sums, u2, u3, u4, c, inv),
        [("v", (8, LANES))] + [("v", field)] * 4,
        [VMEM(field, F32)],
        name="adjoint_3_2",
    )
    w3, q3, w2, q2, pay_a, pay_b = call(
        join_third_kernel,
        [sp] + v(weights, u1, u2, u4, c, inv, u3h_a, u3h_b, *third, *first, w3, q3, w2, q2),
        [("v", field)] * 4 + [("v", double)] * 2,
        [VMEM(plane, F32)],
        aliases={13: 0, 14: 1, 15: 2, 16: 3},
        name="edges_adjoint_3_2",
    )
    fourth = swap(pay_a, pay_b)
    w1, q1, cur, prev = call(
        adjoint_end_kernel,
        v(weights, u1, w2, w3, q2, c, inv, s),
        [("v", field)] * 2 + [("h", field)] * 2,
        [VMEM(field, F32), VMEM(field, F32), dma((2,))],
        name="adjoint_1_0",
    )
    (partial,) = call(
        functools.partial(patch_kernel, own),
        [ab, sp]
        + v(weights, patch_map, up, u, u1, u2, u3, u4, w3, w2, w1, q2, inv, u1h_a, u1h_b, *first),
        [("v", (count, LANES))],
        [
            VMEM((4 * cx + 8, side), jnp.int32),
            VMEM((4 * cx + 8, side), F32),
            VMEM((side, LANES), F32),
        ],
        name="patch_sums",
    )
    grad_absorb = jnp.sum(deal(partial), axis=0)[:own] / float(PATCH_CELLS)
    cur, prev = call(
        join_last_kernel,
        [sp] + v(w1, q1, w2, q2, c, inv, s, *fourth, *first) + [("h", cur), ("h", prev)],
        [("h", field)] * 2,
        [
            VMEM((2, side, side), F32),
            VMEM((2, side, side), F32),
            VMEM(plane, F32),
            VMEM((4, side, side), F32),
            VMEM((2, side, side), F32),
            dma((6,)),
        ],
        aliases={12: 0, 13: 1},
        name="edges_adjoint_1_0",
    )
    return prev, cur, grad_absorb


def solution(mesh):
    bricks = P(("groups", "gx"), None, None)
    return jax.shard_map(
        on_device,
        mesh=mesh,
        in_specs=(bricks, bricks, bricks, bricks, P("groups"), P("groups"), P("groups"), P("groups")),
        out_specs=(bricks, bricks, P(("groups", "gx"))),
        check_vma=False,
    )
```

time: 345 us -> 133 us (0.39)
  other arithmetic: 123 us -> 0.55 us
  local copies, waits for them, and re-layouts: 87.3 us -> 26.3 us
  blocking collectives: 65.8 us -> 14.6 us
  Pallas kernels: 0 us -> 40.7 us
  starting transfers between devices: 58.5 us -> 42.6 us
    scatter-add x1 -> x0, other arithmetic: 57 us -> none  [on_device(): jax.ops.segment_sum(faces_grad.reshape(-1), patch_map.reshape(-1), absorb...]
    gather x2 -> x0, local copies, waits for them, and re-layouts: 51 us -> none  [on_device(): face_absorb = absorb[patch_map]]
    pallas_call x0 -> x11, Pallas kernels: none -> 40.7 us  [call(): pl.pallas_call(kernel, out_shape=[pltpu.VMEM(shape, F32) if kind == 'v' e...]
    psum x1 -> x0, blocking collectives: 34.5 us -> none  [on_device(): energy = lax.psum(local_energy, 'gx') / all_cells]
    unnamed x1 -> x0, blocking collectives: 31.2 us -> none
    concatenate x8 -> x0, other arithmetic: 25.3 us -> none  [extended(): jnp.concatenate([lax.ppermute(tail, axis, [(i, (i + 1) % count) for i in...]
    ppermute x16 -> x10, starting transfers between devices: 58.5 us -> 34.6 us  [the longest x5 29.7 us: swap(): return (lax.ppermute(a, 'gx', within), b)]
    all_to_all x0 -> x1, blocking collectives: none -> 14.6 us  [deal(): return lax.all_to_all(rows, 'gx', 0, 0, tiled=True)]
  transfers between devices with their start and end apart: 16 -> 11, of which waited for: 4 -> 1; matrix products, arithmetic and copies ran while one was open for 36% -> 0% of each run, Pallas kernels for 0% -> 18%
where the time goes in v1:
time: 133 us; the launch traced here: 132 us
  starting transfers between devices  42.6 us (32%)
  Pallas kernels  40.7 us (31%)
  local copies, waits for them, and re-layouts  26.3 us (20%)
  blocking collectives  14.6 us (11%)
  waiting for transfers between devices  5.13 us (4%)
  between operations  2.58 us (2%)
    pallas_call x11, Pallas kernels, call(): pl.pallas_call(kernel, out_shape=[pltpu.VMEM(shape, F32) if kind == 'v' e...  40.7 us
    ppermute x5, starting transfers between devices, swap(): return (lax.ppermute(a, 'gx', within), b)  29.7 us
    unnamed x90, local copies, waits for them, and re-layouts  26.3 us
    all_to_all x1, blocking collectives, deal(): return lax.all_to_all(rows, 'gx', 0, 0, tiled=True)  14.6 us
    all_to_all x1, starting transfers between devices, deal(): return lax.all_to_all(rows, 'gx', 0, 0, tiled=True)  7.98 us
    all_to_all x1, waiting for transfers between devices, deal(): return lax.all_to_all(rows, 'gx', 0, 0, tiled=True)  5.11 us
    ppermute x5, starting transfers between devices, swap(): b = lax.ppermute(b, 'gx', across)  4.96 us
  transfers between devices with their start and end apart: 11, of which 1 were waited for; matrix products, arithmetic and copies ran while one was open for 0% of the time, Pallas kernels for 18%

profile of v1, /device:TPU:0, one launch (start us, length us, event | category | flops | bytes accessed | tf_op | source)
XLA Modules:
  0.0 132.5 jit_solution(10244356683732592114)
XLA Ops:
  0.6 1.6 %copy-done.21 = f32[8,256,256]{2,1,0:T(8,128)S(1)} copy-done((f32[8,256,256]{2,1,0:T(8,128)S(1)}, f32[8,256,256]{2,1,0:T(8,128)}, u32[]{:S(2)}) %copy-start.21) | copy-done | bytes 2097176
  2.2 1.6 %copy-done.30 = f32[8,256,256]{2,1,0:T(8,128)S(1)} copy-done((f32[8,256,256]{2,1,0:T(8,128)S(1)}, f32[8,256,256]{2,1,0:T(8,128)}, u32[]{:S(2)}) %copy-start.30) | copy-done | bytes 2097176
  3.8 1.6 %copy-done.31 = f32[8,256,256]{2,1,0:T(8,128)S(1)} copy-done((f32[8,256,256]{2,1,0:T(8,128)S(1)}, f32[8,256,256]{2,1,0:T(8,128)}, u32[]{:S(2)}) %copy-start.31) | copy-done | bytes 2097176
  6.9 4.0 %damping.1 = (f32[8,256,256]{2,1,0:T(8,128)S(1)}, f32[8,256,256]{2,1,0:T(8,128)S(1)}, f32[8,256,256]{2,1,0:T(8,128)S(1)}, f32[8,256,256]{2,1,0:T(8,128)S(1)}, f3...) custom-call(s32[1]{0:T(128)} %bitcast.parity_ref, f32[160]{0:T(256)S(1)} %copy-done.42, ...), custom_call_target="tpu_custom_call" | custom-call | tf_op jit(solution)/shard_map/damping/pallas_call | solution.py:604
  12.2 3.9 %collective-permute-start = (f32[256,256]{1,0:T(8,128)S(1)}, f32[256,256]{1,0:T(8,128)S(1)}, u32[]{:S(2)}, u32[]{:S(2)}) collective-permute-start(f32[256,256]{1,0:T(8,128)S(1)} %get-tuple-element.49), channel_id=1, source_target_pairs={{0,1},{1,0},{2,3},{3,2},{4,5},{5,4},{6,7},{7,6},{8,9},{9,8},{10,11... | collective-permute-start | bytes 786440 | tf_op jit(solution)/shard_map/ppermute | solution.py:635
  16.8 3.5 %forward_1_2.1 = (f32[8,256,256]{2,1,0:T(8,128)S(1)}, f32[8,256,256]{2,1,0:T(8,128)S(1)}) custom-call(f32[8,256,256]{2,1,0:T(8,128)S(1)} %get-tuple-element.46.u, f32[8,256,256]{2,1,0:T(8,128)S(1)} %get-tuple-element.53.up, f32[8,256,256]{2,1,0:T(8,128)S(1)} %get-tuple-element.47.c, f32[8,256,256]{2,1,0:T(8,128)S(1)} %get-tuple-element.48.inv), custom_call_target="tpu_custom_call" | custom-call | tf_op jit(solution)/shard_map/forward_1_2/pallas_call | solution.py:604
  20.4 1.8 %edges_1_2.1 = (f32[8,256,256]{2,1,0:T(8,128)S(1)}, f32[8,256,256]{2,1,0:T(8,128)S(1)}, f32[256,256]{1,0:T(8,128)S(1)}, f32[256,256]{1,0:T(8,128)S(1)}, f32[512,256]{1,0:T(8,128)S(1)}, /*index=5*/f32[512,256]{1,0:T(8,128)S(1)}) custom-call(s32[1]{0:T(128)} %bitcast.parity_ref, ...), custom_call_target="tpu_custom_call", output_to_operand_aliasing={{0}: (8, {}), {1}: (9, {})} | custom-call | tf_op jit(solution)/shard_map/edges_1_2/pallas_call | solution.py:604
  22.2 13.2 %collective-permute-start.4 = (f32[512,256]{1,0:T(8,128)S(1)}, f32[512,256]{1,0:T(8,128)S(1)}, u32[]{:S(2)}, u32[]{:S(2)}) collective-permute-start(f32[512,256]{1,0:T(8,128)S(1)} %get-tuple-element.59), channel_id=1, source_target_pairs={{0,1},{1,0},{2,3},{3,2},{4,5},{5,4},{6,7},{7,6},{8,9},{9,8},{10,11... | collective-permute-start | bytes 1572872 | tf_op jit(solution)/shard_map/ppermute | solution.py:635
  36.1 4.0 %forward_3_4.1 = (f32[8,256,256]{2,1,0:T(8,128)S(1)}, f32[8,256,256]{2,1,0:T(8,128)S(1)}, f32[4,8,256]{2,1,0:T(8,128)S(1)}) custom-call(f32[8,256,256]{2,1,0:T(8,128)S(1)} %get-tuple-element.57.u1, f32[8,256,256]{2,1,0:T(8,128)S(1)} %get-tuple-element.56.u2, f32[8,256,256]{2,1,0:T(8,128)S(1)} %get-tuple-element.47.c, f32[8,256,256]{2,1,0:T(8,128)S(1)} %get-tuple-element.48.inv), custom_call_target="tpu_custom_call" | custom-call | tf_op jit(solution)/shard_map/forward_3_4/pallas_call | solution.py:604
  40.2 3.0 %edges_3_4.1 = (f32[8,256,256]{2,1,0:T(8,128)S(1)}, f32[8,256,256]{2,1,0:T(8,128)S(1)}, f32[256,256]{1,0:T(8,128)S(1)}, f32[256,256]{1,0:T(8,128)S(1)}, f32[512,...) custom-call(s32[1]{0:T(128)} %bitcast.parity_ref, ...), custom_call_target="tpu_custom_call", output_to_operand_aliasing={{0}: (9, {}), {1}: (10, {})} | custom-call | tf_op jit(solution)/shard_map/edges_3_4/pallas_call | solution.py:604
  44.5 1.3 copy-done.16
  47.2 11.3 %collective-permute-start.6 = (f32[512,256]{1,0:T(8,128)}, f32[512,256]{1,0:T(8,128)}, u32[]{:S(2)}, u32[]{:S(2)}) collective-permute-start(f32[512,256]{1,0:T(8,128)} %get-tuple-element.69), channel_id=1, source_target_pairs={{0,1},{1,0},{2,3},{3,2},{4,5},{5,4},{6,7},{7,6},{8,9},{9,8},{10,11... | collective-permute-start | bytes 1572872 | tf_op jit(solution)/shard_map/ppermute | solution.py:635
  58.6 1.5 %collective-permute-start.7 = (f32[512,256]{1,0:T(8,128)}, f32[512,256]{1,0:T(8,128)}, u32[]{:S(2)}, u32[]{:S(2)}) collective-permute-start(f32[512,256]{1,0:T(8,128)} %get-tuple-element.70), channel_id=1, source_target_pairs={{1,2},{3,4},{5,6},{7,8},{9,10},{11,12},{13,14},{2,1},{4,3},{6,5},{... | collective-permute-start | bytes 1572872 | tf_op jit(solution)/shard_map/ppermute | solution.py:634
  60.0 8.0 %all-to-all-start = ((f32[16,1,128]{2,1,0:T(1,128)}), f32[16,1,128]{2,1,0:T(1,128)S(1)}, u32[]{:S(2)}, u32[]{:S(2)}) async-start(f32[16,1,128]{2,1,0:T(1,128)} %bitcast.2), calls=%async_computation | async-start | bytes 16384 | tf_op jit(solution)/shard_map/all_to_all | solution.py:638
  69.3 5.1 %all-to-all-done = f32[16,1,128]{2,1,0:T(1,128)S(1)} async-done(((f32[16,1,128]{2,1,0:T(1,128)}), f32[16,1,128]{2,1,0:T(1,128)S(1)}, u32[]{:S(2)}, u32[]{:S(2)}) %all-to-all-start) | async-done | bytes 8224 | tf_op jit(solution)/shard_map/all_to_all | solution.py:638
  74.4 1.6 %copy-done.1 = f32[8,256,256]{2,1,0:T(8,128)S(1)} copy-done((f32[8,256,256]{2,1,0:T(8,128)S(1)}, f32[8,256,256]{2,1,0:T(8,128)}, u32[]{:S(2)}) %copy-start.1) | copy-done | bytes 2097176
  76.0 1.6 %copy-done.5 = f32[8,256,256]{2,1,0:T(8,128)S(1)} copy-done((f32[8,256,256]{2,1,0:T(8,128)S(1)}, f32[8,256,256]{2,1,0:T(8,128)}, u32[]{:S(2)}) %copy-start.5) | copy-done | bytes 2097176
  77.6 1.6 %copy-done.10 = f32[8,256,256]{2,1,0:T(8,128)S(1)} copy-done((f32[8,256,256]{2,1,0:T(8,128)S(1)}, f32[8,256,256]{2,1,0:T(8,128)}, u32[]{:S(2)}) %copy-start.10) | copy-done | bytes 2097176
  79.2 1.6 %copy-done.17 = f32[8,256,256]{2,1,0:T(8,128)S(1)} copy-done((f32[8,256,256]{2,1,0:T(8,128)S(1)}, f32[8,256,256]{2,1,0:T(8,128)}, u32[]{:S(2)}) %copy-start.17) | copy-done | bytes 2097176
  80.8 5.0 %adjoint_3_2.1 = (f32[8,128]{1,0:T(8,128)S(1)}, f32[8,256,256]{2,1,0:T(8,128)S(1)}, f32[8,256,256]{2,1,0:T(8,128)S(1)}, f32[8,256,256]{2,1,0:T(8,128)S(1)}, f32[8,256,256]{2,1,0:T(8,128)S(1)}) custom-call(s32[1]{0:T(128)S(6)} %copy.33.checkpoint_ref, f32[64]{0:T(128)S(1)} %copy-done.44, f32[1]{0:T(128)S(6)} %copy.34.tail_ref, f32[16,128]{1,0:T(8,128)S(1)} %bitcast.9, ...), custom_call_target="tpu_custom_call" | custom-call | tf_op jit(solution)/shard_map/adjoint_3_2/pallas_call | solution.py:604
  85.9 4.6 %edges_adjoint_3_2.1 = (f32[8,256,256]{2,1,0:T(8,128)S(1)}, f32[8,256,256]{2,1,0:T(8,128)S(1)}, f32[8,256,256]{2,1,0:T(8,128)S(1)}, f32[8,256,256]{2,1,0:T(8,128...) custom-call(s32[1]{0:T(128)} %bitcast.parity_ref, ...), custom_call_target="tpu_custom_call", output_to_operand_aliasing={{0}: (13, {}), {1}: (14, {}), {2}: (15, {}), {3}: (16, {})} | custom-call | tf_op jit(solution)/shard_map/edges_adjoint_3_2/pallas_call | solution.py:604
  91.1 1.5 %collective-permute-start.9 = (f32[512,256]{1,0:T(8,128)}, f32[512,256]{1,0:T(8,128)}, u32[]{:S(2)}, u32[]{:S(2)}) collective-permute-start(f32[512,256]{1,0:T(8,128)} %get-tuple-element.82), channel_id=1, source_target_pairs={{1,2},{3,4},{5,6},{7,8},{9,10},{11,12},{13,14},{2,1},{4,3},{6,5},{... | collective-permute-start | bytes 1572872 | tf_op jit(solution)/shard_map/ppermute | solution.py:634
  92.6 5.1 %adjoint_1_0.1 = (f32[8,256,256]{2,1,0:T(8,128)S(1)}, f32[8,256,256]{2,1,0:T(8,128)S(1)}, f32[8,256,256]{2,1,0:T(8,128)}, f32[8,256,256]{2,1,0:T(8,128)}) custom-call(f32[8,128]{1,0:T(8,128)S(1)} %get-tuple-element.66.weights, f32[8,256,256]{2,1,0:T(8,128)S(1)} %copy-done.8, f32[8,256,256]{2,1,0:T(8,128)S(1)} %get-tuple-element.75.w2, ...), custom_call_target="tpu_custom_call" | custom-call | tf_op jit(solution)/shard_map/adjoint_1_0/pallas_call | solution.py:604
  97.8 6.6 %patch_sums.1 = f32[16,128]{1,0:T(8,128)S(1)} custom-call(f32[160]{0:T(256)S(1)} %copy-done.43, s32[1]{0:T(128)} %bitcast.parity_ref, f32[8,128]{1,0:T(8,128)S(1)} %get-tuple-element.66.weights, s32[8,4,256]{2,1,0:T(4,128)S(1)} %copy-done.41, f32[8,256,256]{2,1,0:T(8,128)S(1)} %copy-done.24, f32[8,256,256]{2,1,0:T(8,128)S(1)} %copy-done.20, ...), custom_call_target="tpu_custom_call" | custom-call | tf_op jit(solution)/shard_map/patch_sums/pallas_call | solution.py:604
  104.4 14.6 %all_to_all.20 = f32[16,1,128]{2,1,0:T(1,128)S(1)} all-to-all(f32[16,1,128]{2,1,0:T(1,128)S(1)} %bitcast.8), channel_id=1, replica_groups=mesh['groups'=2,'gx'=16] {'gx'}, dimensions={0} | all-to-all | bytes 16384 | tf_op jit(solution)/shard_map/all_to_all | solution.py:638
  119.6 1.6 %copy-done.3 = f32[8,256,256]{2,1,0:T(8,128)S(1)} copy-done((f32[8,256,256]{2,1,0:T(8,128)S(1)}, f32[8,256,256]{2,1,0:T(8,128)}, u32[]{:S(2)}) %copy-start.3) | copy-done | bytes 2097176
  121.2 1.6 %copy-done.13 = f32[8,256,256]{2,1,0:T(8,128)S(1)} copy-done((f32[8,256,256]{2,1,0:T(8,128)S(1)}, f32[8,256,256]{2,1,0:T(8,128)}, u32[]{:S(2)}) %copy-start.13) | copy-done | bytes 2097176
  122.8 1.6 %copy-done.15 = f32[8,256,256]{2,1,0:T(8,128)S(1)} copy-done((f32[8,256,256]{2,1,0:T(8,128)S(1)}, f32[8,256,256]{2,1,0:T(8,128)}, u32[]{:S(2)}) %copy-start.15) | copy-done | bytes 2097176
  124.4 1.6 %copy-done.26 = f32[8,256,256]{2,1,0:T(8,128)S(1)} copy-done((f32[8,256,256]{2,1,0:T(8,128)S(1)}, f32[8,256,256]{2,1,0:T(8,128)}, u32[]{:S(2)}) %copy-start.26) | copy-done | bytes 2097176
  126.0 1.6 %copy-done.29 = f32[8,256,256]{2,1,0:T(8,128)S(1)} copy-done((f32[8,256,256]{2,1,0:T(8,128)S(1)}, f32[8,256,256]{2,1,0:T(8,128)}, u32[]{:S(2)}) %copy-start.29) | copy-done | bytes 2097176
  127.5 1.6 %copy-done.33 = f32[8,256,256]{2,1,0:T(8,128)S(1)} copy-done((f32[8,256,256]{2,1,0:T(8,128)S(1)}, f32[8,256,256]{2,1,0:T(8,128)}, u32[]{:S(2)}) %copy-start.33) | copy-done | bytes 2097176
  129.1 3.2 %edges_adjoint_1_0.1 = (f32[8,256,256]{2,1,0:T(8,128)}, f32[8,256,256]{2,1,0:T(8,128)}) custom-call(s32[1]{0:T(128)} %bitcast.parity_ref, f32[8,256,256]{2,1,0:T(8,128)S(1)} %copy-done.26, f32[8,256,256]{2,1,0:T(8,128)S(1)} %copy-done.33, f32[8,256,256]{2,1,0:T(8,128)S(1)} %copy-done.13, ...), custom_call_target="tpu_custom_call", output_to_operand_aliasing={{0}: (12, {}), {1}: (13, {})} | custom-call | tf_op jit(solution)/shard_map/edges_adjoint_1_0/pallas_call | solution.py:604
  (94 shorter events, 8.2 us)
Async XLA Ops:
  6.8 5.2 %copy-start.22 = (f32[8,256,256]{2,1,0:T(8,128)S(1)}, f32[8,256,256]{2,1,0:T(8,128)}, u32[]{:S(2)}) copy-start(f32[8,256,256]{2,1,0:T(8,128)} %u_hbm.3) | copy-start | bytes 6291460
  10.8 9.4 %copy-start.23 = (f32[8,256,256]{2,1,0:T(8,128)}, f32[8,256,256]{2,1,0:T(8,128)S(1)}, u32[]{:S(2)}) copy-start(f32[8,256,256]{2,1,0:T(8,128)S(1)} %get-tuple-element.53.up) | copy-start | bytes 6291460
  10.9 9.4 %copy-start.27 = (f32[8,256,256]{2,1,0:T(8,128)}, f32[8,256,256]{2,1,0:T(8,128)S(1)}, u32[]{:S(2)}) copy-start(f32[8,256,256]{2,1,0:T(8,128)S(1)} %get-tuple-element.78.s) | copy-start | bytes 6291460
  10.9 9.5 %copy-start.19 = (f32[8,256,256]{2,1,0:T(8,128)}, f32[8,256,256]{2,1,0:T(8,128)S(1)}, u32[]{:S(2)}) copy-start(f32[8,256,256]{2,1,0:T(8,128)S(1)} %get-tuple-element.46.u) | copy-start | bytes 6291460
  10.9 29.3 %copy-start = (f32[8,256,256]{2,1,0:T(8,128)}, f32[8,256,256]{2,1,0:T(8,128)S(1)}, u32[]{:S(2)}) copy-start(f32[8,256,256]{2,1,0:T(8,128)S(1)} %get-tuple-element.47.c) | copy-start | bytes 6291460
  10.9 9.4 %collective-permute-start.2 = (f32[520,256]{1,0:T(8,128)S(1)}, f32[520,256]{1,0:T(8,128)S(1)}, u32[]{:S(2)}, u32[]{:S(2)}) collective-permute-start(f32[520,256]{1,0:T(8,128)S(1)} %get-tuple-element.51), channel_id=1, source_target_pairs={{0,1},{1,0},{2,3},{3,2},{4,5},{5,4},{6,7},{7,6},{8,9},{9,8},{10,11... | collective-permute-start | bytes 1597448 | tf_op jit(solution)/shard_map/ppermute | solution.py:635
  11.4 8.9 %collective-permute-start.3 = (f32[520,256]{1,0:T(8,128)S(1)}, f32[520,256]{1,0:T(8,128)S(1)}, u32[]{:S(2)}, u32[]{:S(2)}) collective-permute-start(f32[520,256]{1,0:T(8,128)S(1)} %get-tuple-element.52), channel_id=1, source_target_pairs={{1,2},{3,4},{5,6},{7,8},{9,10},{11,12},{13,14},{2,1},{4,3},{6,5},{... | collective-permute-start | bytes 1597448 | tf_op jit(solution)/shard_map/ppermute | solution.py:634
  12.2 8.1 %collective-permute-start = (f32[256,256]{1,0:T(8,128)S(1)}, f32[256,256]{1,0:T(8,128)S(1)}, u32[]{:S(2)}, u32[]{:S(2)}) collective-permute-start(f32[256,256]{1,0:T(8,128)S(1)} %get-tuple-element.49), channel_id=1, source_target_pairs={{0,1},{1,0},{2,3},{3,2},{4,5},{5,4},{6,7},{7,6},{8,9},{9,8},{10,11... | collective-permute-start | bytes 786440 | tf_op jit(solution)/shard_map/ppermute | solution.py:635
  16.1 4.2 %collective-permute-start.1 = (f32[256,256]{1,0:T(8,128)S(1)}, f32[256,256]{1,0:T(8,128)S(1)}, u32[]{:S(2)}, u32[]{:S(2)}) collective-permute-start(f32[256,256]{1,0:T(8,128)S(1)} %get-tuple-element.50), channel_id=1, source_target_pairs={{1,2},{3,4},{5,6},{7,8},{9,10},{11,12},{13,14},{2,1},{4,3},{6,5},{... | collective-permute-start | bytes 786440 | tf_op jit(solution)/shard_map/ppermute | solution.py:634
  22.2 17.9 %copy-start.7 = (f32[8,256,256]{2,1,0:T(8,128)}, f32[8,256,256]{2,1,0:T(8,128)S(1)}, u32[]{:S(2)}) copy-start(f32[8,256,256]{2,1,0:T(8,128)S(1)} %get-tuple-element.57.u1) | copy-start | bytes 6291460
  22.2 17.9 %copy-start.34 = (f32[256,256]{1,0:T(8,128)}, f32[256,256]{1,0:T(8,128)S(1)}, u32[]{:S(2)}) copy-start(f32[256,256]{1,0:T(8,128)S(1)} %get-tuple-element.88.u1h_b) | copy-start | bytes 786436
  22.2 18.0 %copy-start.4 = (f32[8,256,256]{2,1,0:T(8,128)}, f32[8,256,256]{2,1,0:T(8,128)S(1)}, u32[]{:S(2)}) copy-start(f32[8,256,256]{2,1,0:T(8,128)S(1)} %get-tuple-element.56.u2) | copy-start | bytes 6291460
  22.2 17.9 %collective-permute-start.4 = (f32[512,256]{1,0:T(8,128)S(1)}, f32[512,256]{1,0:T(8,128)S(1)}, u32[]{:S(2)}, u32[]{:S(2)}) collective-permute-start(f32[512,256]{1,0:T(8,128)S(1)} %get-tuple-element.59), channel_id=1, source_target_pairs={{0,1},{1,0},{2,3},{3,2},{4,5},{5,4},{6,7},{7,6},{8,9},{9,8},{10,11... | collective-permute-start | bytes 1572872 | tf_op jit(solution)/shard_map/ppermute | solution.py:635
  35.4 4.7 %collective-permute-start.5 = (f32[512,256]{1,0:T(8,128)S(1)}, f32[512,256]{1,0:T(8,128)S(1)}, u32[]{:S(2)}, u32[]{:S(2)}) collective-permute-start(f32[512,256]{1,0:T(8,128)S(1)} %get-tuple-element.60), channel_id=1, source_target_pairs={{1,2},{3,4},{5,6},{7,8},{9,10},{11,12},{13,14},{2,1},{4,3},{6,5},{... | collective-permute-start | bytes 1572872 | tf_op jit(solution)/shard_map/ppermute | solution.py:634
  40.2 34.2 %copy-start.44 = (f32[64]{0:T(128)S(1)}, f32[64]{0:T(128)}, u32[]{:S(2)}) copy-start(f32[64]{0:T(128)} %target_ref.1) | copy-start | bytes 772
  47.2 38.5 %collective-permute-start.6 = (f32[512,256]{1,0:T(8,128)}, f32[512,256]{1,0:T(8,128)}, u32[]{:S(2)}, u32[]{:S(2)}) collective-permute-start(f32[512,256]{1,0:T(8,128)} %get-tuple-element.69), channel_id=1, source_target_pairs={{0,1},{1,0},{2,3},{3,2},{4,5},{5,4},{6,7},{7,6},{8,9},{9,8},{10,11... | collective-permute-start | bytes 1572872 | tf_op jit(solution)/shard_map/ppermute | solution.py:635
  58.6 27.2 %collective-permute-start.7 = (f32[512,256]{1,0:T(8,128)}, f32[512,256]{1,0:T(8,128)}, u32[]{:S(2)}, u32[]{:S(2)}) collective-permute-start(f32[512,256]{1,0:T(8,128)} %get-tuple-element.70), channel_id=1, source_target_pairs={{1,2},{3,4},{5,6},{7,8},{9,10},{11,12},{13,14},{2,1},{4,3},{6,5},{... | collective-permute-start | bytes 1572872 | tf_op jit(solution)/shard_map/ppermute | solution.py:634
  60.0 14.4 %all-to-all-start = ((f32[16,1,128]{2,1,0:T(1,128)}), f32[16,1,128]{2,1,0:T(1,128)S(1)}, u32[]{:S(2)}, u32[]{:S(2)}) async-start(f32[16,1,128]{2,1,0:T(1,128)} %bitcast.2), calls=%async_computation | async-start | bytes 16384 | tf_op jit(solution)/shard_map/all_to_all | solution.py:638
  80.8 5.0 %copy-start.37 = (f32[256,256]{1,0:T(8,128)S(1)}, f32[256,256]{1,0:T(8,128)}, u32[]{:S(2)}) copy-start(f32[256,256]{1,0:T(8,128)} %copy-done.36) | copy-start | bytes 786436
  85.9 6.7 %copy-start.28 = (f32[8,256,256]{2,1,0:T(8,128)S(1)}, f32[8,256,256]{2,1,0:T(8,128)}, u32[]{:S(2)}) copy-start(f32[8,256,256]{2,1,0:T(8,128)} %copy-done.27) | copy-start | bytes 6291460
  90.4 7.3 %copy-start.12 = (f32[8,256,256]{2,1,0:T(8,128)}, f32[8,256,256]{2,1,0:T(8,128)S(1)}, u32[]{:S(2)}) copy-start(f32[8,256,256]{2,1,0:T(8,128)S(1)} %get-tuple-element.75.w2) | copy-start | bytes 6291460
  90.4 7.3 %copy-start.14 = (f32[8,256,256]{2,1,0:T(8,128)}, f32[8,256,256]{2,1,0:T(8,128)S(1)}, u32[]{:S(2)}) copy-start(f32[8,256,256]{2,1,0:T(8,128)S(1)} %get-tuple-element.77.q2) | copy-start | bytes 6291460
  90.4 29.1 %collective-permute-start.8 = (f32[512,256]{1,0:T(8,128)}, f32[512,256]{1,0:T(8,128)}, u32[]{:S(2)}, u32[]{:S(2)}) collective-permute-start(f32[512,256]{1,0:T(8,128)} %get-tuple-element.81), channel_id=1, source_target_pairs={{0,1},{1,0},{2,3},{3,2},{4,5},{5,4},{6,7},{7,6},{8,9},{9,8},{10,11... | collective-permute-start | bytes 1572872 | tf_op jit(solution)/shard_map/ppermute | solution.py:635
  91.1 28.5 %collective-permute-start.9 = (f32[512,256]{1,0:T(8,128)}, f32[512,256]{1,0:T(8,128)}, u32[]{:S(2)}, u32[]{:S(2)}) collective-permute-start(f32[512,256]{1,0:T(8,128)} %get-tuple-element.82), channel_id=1, source_target_pairs={{1,2},{3,4},{5,6},{7,8},{9,10},{11,12},{13,14},{2,1},{4,3},{6,5},{... | collective-permute-start | bytes 1572872 | tf_op jit(solution)/shard_map/ppermute | solution.py:634
  92.6 5.2 %copy-start.18 = (f32[8,256,256]{2,1,0:T(8,128)S(1)}, f32[8,256,256]{2,1,0:T(8,128)}, u32[]{:S(2)}) copy-start(f32[8,256,256]{2,1,0:T(8,128)} %copy-done.16) | copy-start | bytes 6291460
  92.6 5.2 %copy-start.20 = (f32[8,256,256]{2,1,0:T(8,128)S(1)}, f32[8,256,256]{2,1,0:T(8,128)}, u32[]{:S(2)}) copy-start(f32[8,256,256]{2,1,0:T(8,128)} %copy-done.19) | copy-start | bytes 6291460
  92.6 5.2 %copy-start.24 = (f32[8,256,256]{2,1,0:T(8,128)S(1)}, f32[8,256,256]{2,1,0:T(8,128)}, u32[]{:S(2)}) copy-start(f32[8,256,256]{2,1,0:T(8,128)} %copy-done.23) | copy-start | bytes 6291460
  92.6 5.2 %copy-start.35 = (f32[256,256]{1,0:T(8,128)S(1)}, f32[256,256]{1,0:T(8,128)}, u32[]{:S(2)}) copy-start(f32[256,256]{1,0:T(8,128)} %copy-done.34) | copy-start | bytes 786436
  92.6 5.2 %copy-start.41 = (s32[8,4,256]{2,1,0:T(4,128)S(1)}, s32[8,4,256]{2,1,0:T(4,128)}, u32[]{:S(2)}) copy-start(s32[8,4,256]{2,1,0:T(4,128)} %map_ref.3) | copy-start | bytes 98308
  92.6 5.2 %copy-start.43 = (f32[160]{0:T(256)S(1)}, f32[160]{0:T(256)}, u32[]{:S(2)}) copy-start(f32[160]{0:T(256)} %absorb_ref.3) | copy-start | bytes 1924
  97.7 6.7 %copy-start.25 = (f32[8,256,256]{2,1,0:T(8,128)}, f32[8,256,256]{2,1,0:T(8,128)S(1)}, u32[]{:S(2)}) copy-start(f32[8,256,256]{2,1,0:T(8,128)S(1)} %get-tuple-element.79.w1) | copy-start | bytes 6291460
  97.7 6.7 %copy-start.32 = (f32[8,256,256]{2,1,0:T(8,128)}, f32[8,256,256]{2,1,0:T(8,128)S(1)}, u32[]{:S(2)}) copy-start(f32[8,256,256]{2,1,0:T(8,128)S(1)} %get-tuple-element.80.q1) | copy-start | bytes 6291460
  (24 other events, 51.4 us)

commit v2 on v0

v2 whole, which is shorter than its diff:
```python
import functools

import jax
import jax.numpy as jnp
from jax import lax
from jax.experimental import pallas as pl
from jax.experimental.pallas import tpu as pltpu
from jax.sharding import PartitionSpec as P

STEPS = 4
PATCH_CELLS = 819
CHUNK = 16
LANES = 128
GROUP = 32
F32 = jnp.float32
VMEM = pltpu.VMEM
in_vmem = pl.BlockSpec(memory_space=pltpu.VMEM)
in_smem = pl.BlockSpec(memory_space=pltpu.SMEM)
in_hbm = pl.BlockSpec(memory_space=pltpu.HBM)


def end_layer(parity, side, depth, cx):
    high = 1 - parity if side == 0 else parity
    return high * (cx - 1 - depth) + (1 - high) * depth


def layer(ref, x):
    return lambda row, count: ref[x, pl.ds(row, count), :]


def flat(ref, base):
    return lambda row, count: ref[pl.ds(base + row, count), :]


def chunks(side_cells):
    return [(row, CHUNK) for row in range(0, side_cells, CHUNK)]


def beside(field, row, count, side_cells):
    v = field(row, count)
    tiles = [v[k : k + 8] for k in range(0, count, 8)]
    sub = lax.broadcasted_iota(jnp.int32, tiles[0].shape, 0)
    zero = jnp.zeros_like(tiles[0])
    before = pltpu.roll(field(row - 8, 8), 1, 0) if row else zero
    after = pltpu.roll(field(row + count, 8), 7, 0) if row + count < side_cells else zero
    down = [before] + [pltpu.roll(tile, 1, 0) for tile in tiles]
    up = [pltpu.roll(tile, 7, 0) for tile in tiles] + [after]
    total = jnp.concatenate(
        [
            jnp.where(sub == 0, down[k], down[k + 1]) + jnp.where(sub == 7, up[k + 1], up[k])
            for k in range(len(tiles))
        ],
        axis=0,
    )
    parts = [v[:, k : k + LANES] for k in range(0, side_cells, LANES)]
    lane = lax.broadcasted_iota(jnp.int32, parts[0].shape, 1)
    zero = jnp.zeros_like(parts[0])
    right = [zero] + [pltpu.roll(part, 1, 1) for part in parts]
    left = [pltpu.roll(part, LANES - 1, 1) for part in parts] + [zero]
    across = jnp.concatenate(
        [
            jnp.where(lane == 0, right[k], right[k + 1])
            + jnp.where(lane == LANES - 1, left[k + 1], left[k])
            for k in range(len(parts))
        ],
        axis=1,
    )
    return v, total + across


def forward(now, prior, courant, inverse, sides, row, count, side_cells):
    v, total = beside(now, row, count, side_cells)
    for other in sides:
        total = total + other(row, count)
    p = prior(row, count)
    c, i = courant(row, count), inverse(row, count)
    return i * (2.0 * (v - p) + c * (total - 6.0 * v)) + p


def backward(product, w, later, inverse, source, sides, row, count, side_cells):
    q, total = beside(product, row, count, side_cells)
    for other in sides:
        total = total + other(row, count)
    fresh = total - 6.0 * q + source
    i = inverse(row, count)
    if later is None:
        return i * (2.0 * w + fresh)
    return i * (2.0 * (w - later) + fresh) + later


def sweep(low, high, body):
    def turn(x, carry):
        body(x)
        return carry

    lax.fori_loop(low, high, turn, 0)


def x_sides(ref, x, cx):
    return [layer(ref, k) for k in (x - 1, x + 1) if not isinstance(k, int) or 0 <= k < cx]


def fold(values):
    total = values[0:8]
    for row in range(8, values.shape[0], 8):
        total = total + values[row : row + 8]
    return total


def spread_weight(weights, n, count):
    tile = weights[8 * n : 8 * n + 8, :]
    return jnp.concatenate([tile] * (count // 8), axis=0)


def start_kernel(parity_ref, u_hbm, a_ref, b_ref, sems):
    cx = u_hbm.shape[0]
    copies = []
    for side, out in enumerate((a_ref, b_ref)):
        x = end_layer(parity_ref[0], side, 0, cx)
        copies.append(pltpu.make_async_copy(u_hbm.at[x], out, sems.at[side]))
    for copy in copies:
        copy.start()
    for copy in copies:
        copy.wait()


def lookup(maps, absorb_ref):
    def turn(p, got):
        return jnp.where(maps == p, absorb_ref[p], got)

    return lax.fori_loop(0, absorb_ref.shape[0], turn, jnp.zeros(maps.shape, F32), unroll=8)


def to_lane(tile, spot, lane_from):
    return pltpu.roll(tile, (spot - lane_from) % LANES, 1)


def damping_at(x, cx, columns, found, row, count, side_cells):
    tile = columns[pl.ds(row, count), :]
    lane = lax.broadcasted_iota(jnp.int32, tile.shape, 1)
    near = jnp.where(lane == 0, pltpu.roll(tile, lax.rem(LANES - x, LANES), 1), 0.0)
    far = jnp.where(lane == LANES - 1, pltpu.roll(tile, LANES - 1 - cx - x, 1), 0.0)
    mid = [jnp.zeros_like(near)] * (side_cells // LANES - 2)
    field = jnp.concatenate([near, *mid, far], axis=1)
    sub = lax.broadcasted_iota(jnp.int32, field.shape, 0)
    if row == 0:
        field = field + jnp.where(sub == 0, found[pl.ds(4 * x, 1), :], 0.0)
    if row + count == side_cells:
        field = field + jnp.where(sub == count - 1, found[pl.ds(4 * x + 1, 1), :], 0.0)
    return field


def setup_kernel(
    parity_ref, absorb_ref, checkpoint_ref, target_ref, tail_ref, map_ref, e_a, e_b,
    u_hbm, up_hbm, c_hbm,
    pay_a, pay_b, columns, found, params,
    maps, turned, deep, prior, courant, inv, turned_back, sems,
):
    cx, side_cells = u_hbm.shape[0], u_hbm.shape[1]
    copies = []
    for side in range(2):
        x0 = end_layer(parity_ref[0], side, 0, cx)
        x1 = end_layer(parity_ref[0], side, 1, cx)
        for src, x, dst in ((up_hbm, x0, prior), (c_hbm, x0, courant), (u_hbm, x1, deep)):
            copies.append(
                pltpu.make_async_copy(src.at[x], dst.at[side], sems.at[len(copies)])
            )
            copies[-1].start()
    lane = lax.broadcasted_iota(jnp.int32, params.shape, 1)
    start = jnp.clip(checkpoint_ref[0], 0, target_ref.shape[0] - STEPS)
    row = jnp.where(lane == STEPS, tail_ref[0], 0.0)
    for n in range(STEPS):
        row = jnp.where(lane == n, target_ref[start + n], row)
    params[...] = row
    for x in range(cx):
        maps[4 * x : 4 * x + 4, :] = map_ref[x]
    found[...] = lookup(maps[...], absorb_ref)
    turned[...] = jnp.zeros_like(turned)
    for x in range(cx):
        turned[x : x + 1, :] = found[4 * x + 2 : 4 * x + 3, :]
        turned[cx + x : cx + x + 1, :] = found[4 * x + 3 : 4 * x + 4, :]
    columns[...] = jnp.transpose(turned[...])
    for side in range(2):
        x0 = end_layer(parity_ref[0], side, 0, cx)
        for row, count in chunks(side_cells):
            inv[side, pl.ds(row, count), :] = 1.0 / (
                1.0 + damping_at(x0, cx, columns, found, row, count, side_cells)
            )
    for copy in copies:
        copy.wait()
    for side, (edge, pay) in enumerate(((e_a, pay_a), (e_b, pay_b))):
        for row, count in chunks(side_cells):
            pay[pl.ds(row, count), :] = forward(
                flat(edge, 0), layer(prior, side), layer(courant, side), layer(inv, side),
                [layer(deep, side)], row, count, side_cells,
            )
            pay[pl.ds(side_cells + row, count), :] = (
                courant[side, pl.ds(row, count), :] * inv[side, pl.ds(row, count), :]
            )
    spot = lax.broadcasted_iota(jnp.int32, (CHUNK, LANES), 1)
    for row, count in chunks(side_cells):
        total = jnp.zeros((count, LANES), F32)
        for side in range(2):
            values = prior[side, pl.ds(row, count), :]
            total = jnp.where(spot == 2 * side, to_lane(values[:, :LANES], 2 * side, 0), total)
            total = jnp.where(
                spot == 2 * side + 1, to_lane(values[:, -LANES:], 2 * side + 1, LANES - 1), total
            )
        turned_back[pl.ds(row, count), :] = total
    rows = jnp.transpose(turned_back[...])
    base = 2 * side_cells
    for side, pay in enumerate((pay_a, pay_b)):
        x0 = end_layer(parity_ref[0], side, 0, cx)
        pay[base : base + 1, :] = prior[side, 0:1, :]
        pay[base + 1 : base + 2, :] = prior[side, side_cells - 1 : side_cells, :]
        pay[base + 2 : base + 4, :] = rows[2 * side : 2 * side + 2, :]
        pay[base + 4 : base + 8, :] = map_ref[x0].astype(F32)


def ahead_kernel(columns, found, u_hbm, up_hbm, c_hbm, u, up, c, s, inv, u1, u2, sems):
    cx, side_cells = u.shape[0], u.shape[1]
    copies = [
        pltpu.make_async_copy(src, dst, sems.at[k])
        for k, (src, dst) in enumerate(((u_hbm, u), (up_hbm, up), (c_hbm, c)))
    ]
    for copy in copies:
        copy.start()

    def spread(x):
        for row, count in chunks(side_cells):
            field = damping_at(x, cx, columns, found, row, count, side_cells)
            s[x, pl.ds(row, count), :] = field
            inv[x, pl.ds(row, count), :] = 1.0 / (1.0 + field)

    def first(x):
        for row, count in chunks(side_cells):
            u1[x, pl.ds(row, count), :] = forward(
                layer(u, x), layer(up, x), layer(c, x), layer(inv, x), x_sides(u, x, cx),
                row, count, side_cells,
            )

    def second(x):
        for row, count in chunks(side_cells):
            u2[x, pl.ds(row, count), :] = forward(
                layer(u1, x), layer(u, x), layer(c, x), layer(inv, x), x_sides(u1, x, cx),
                row, count, side_cells,
            )

    sweep(0, cx, spread)
    for copy in copies:
        copy.wait()
    for body in (first, second):
        body(0)
        sweep(1, cx - 1, body)
        body(cx - 1)


def join_forward(x0, x1, edge, mid, last, c, inv, got_now, got_part, got_b, b, halo, delta, side_cells):
    for row, count in chunks(side_cells):
        at = pl.ds(row, count)
        change = b(row, count) * got_now(row, count)
        delta[at, :] = change
        mid[x0, at, :] += change
        halo[at, :] = got_part(row, count) + got_b(row, count) * edge(row, count)
        last[x1, at, :] += (c[x1, at, :] * inv[x1, at, :]) * change
    for row, count in chunks(side_cells):
        at = pl.ds(row, count)
        v, total = beside(flat(delta, 0), row, count, side_cells)
        last[x0, at, :] += (2.0 * inv[x0, at, :]) * v + b(row, count) * (
            total - 6.0 * v + halo[at, :]
        )


def join_first_kernel(
    parity_ref, c, inv, e_a, e_b, near_a, near_b, own_a, own_b, got_a, got_b, u1_in, u2_in,
    u1, u2, halo_a, halo_b, pay_a, pay_b, delta,
):
    cx, side_cells = c.shape[0], c.shape[1]
    for side, (edge, near, own, got, halo, pay) in enumerate(
        ((e_a, near_a, own_a, got_a, halo_a, pay_a), (e_b, near_b, own_b, got_b, halo_b, pay_b))
    ):
        x0, x1 = (end_layer(parity_ref[0], side, k, cx) for k in range(2))
        join_forward(
            x0, x1, flat(edge, 0), u1, u2, c, inv, flat(near, 0), flat(got, 0),
            flat(got, side_cells), flat(own, side_cells), halo, delta, side_cells,
        )
        for row, count in chunks(side_cells):
            pay[pl.ds(row, count), :] = u2[x0, pl.ds(row, count), :]
            pay[pl.ds(side_cells + row, count), :] = forward(
                layer(u2, x0), layer(u1, x0), layer(c, x0), layer(inv, x0), [layer(u2, x1)],
                row, count, side_cells,
            )


def halo_walls(absorb_ref, map_ref, halves, maps, wall_gain, columns):
    cx, side_cells = map_ref.shape[0], columns.shape[0]
    last, extra = side_cells - 1, 2 * side_cells
    for x in range(cx):
        maps[4 * x : 4 * x + 4, :] = map_ref[x]
    for side, (_, got) in enumerate(halves):
        maps[4 * (cx + side) : 4 * (cx + side) + 4, :] = got[extra + 4 : extra + 8, :].astype(
            jnp.int32
        )
    damping = lookup(maps[4 * cx : 4 * cx + 8, :], absorb_ref)
    spot = lax.broadcasted_iota(jnp.int32, (CHUNK, LANES), 1)
    for row, count in chunks(side_cells):
        total = jnp.zeros((count, LANES), F32)
        for side, (u1h, _) in enumerate(halves):
            values = u1h[pl.ds(row, count), :]
            total = jnp.where(spot == 2 * side, to_lane(values[:, :LANES], 2 * side, 0), total)
            total = jnp.where(
                spot == 2 * side + 1, to_lane(values[:, -LANES:], 2 * side + 1, LANES - 1), total
            )
        columns[pl.ds(row, count), :] = total
    rows = jnp.transpose(columns[...])
    lane = lax.broadcasted_iota(jnp.int32, (1, side_cells), 1)

    def corners(one, two):
        return jnp.where(lane == 0, one, 0.0) + jnp.where(lane == last, two, 0.0)

    for side, (u1h, got) in enumerate(halves):
        d = [damping[4 * side + f : 4 * side + f + 1] for f in range(4)]
        total = jnp.concatenate(
            [
                d[0] + corners(d[2][:, 0:1], d[3][:, 0:1]),
                d[1] + corners(d[2][:, last:], d[3][:, last:]),
                d[2] + corners(d[0][:, 0:1], d[1][:, 0:1]),
                d[3] + corners(d[0][:, last:], d[1][:, last:]),
            ],
            axis=0,
        )
        now = jnp.concatenate(
            [u1h[0:1, :], u1h[last : last + 1, :], rows[2 * side : 2 * side + 2, :]], axis=0
        )
        wall_gain[4 * side : 4 * side + 4, :] = (got[extra : extra + 4, :] - now) / (1.0 + total)


def ahead_again_kernel(
    absorb_ref, map_ref, u1, u2, c, inv, u1h_a, u1h_b, got_a, got_b,
    u3, u4, energy, maps, wall_gain, columns,
):
    cx, side_cells = u1.shape[0], u1.shape[1]
    halo_walls(absorb_ref, map_ref, ((u1h_a, got_a), (u1h_b, got_b)), maps, wall_gain, columns)
    energy[...] = jnp.zeros_like(energy)

    def first(x, inner):
        sums = [jnp.zeros((8, side_cells), F32)] * 3
        for row, count in chunks(side_cells):
            value = forward(
                layer(u2, x), layer(u1, x), layer(c, x), layer(inv, x), x_sides(u2, x, cx),
                row, count, side_cells,
            )
            u3[x, pl.ds(row, count), :] = value
            sums[0] = sums[0] + fold(u1[x, pl.ds(row, count), :] ** 2)
            sums[1] = sums[1] + fold(u2[x, pl.ds(row, count), :] ** 2)
            sums[2] = sums[2] + fold(value * value)
        for k in range(3 if inner else 2):
            energy[k] += sums[k]

    def second(x, inner):
        total = jnp.zeros((8, side_cells), F32)
        for row, count in chunks(side_cells):
            value = forward(
                layer(u3, x), layer(u2, x), layer(c, x), layer(inv, x), x_sides(u3, x, cx),
                row, count, side_cells,
            )
            u4[x, pl.ds(row, count), :] = value
            total = total + fold(value * value)
        if inner:
            energy[3] += total

    first(0, False)
    sweep(1, cx - 1, lambda x: first(x, True))
    first(cx - 1, False)
    second(0, False)
    second(1, False)
    sweep(2, cx - 2, lambda x: second(x, True))
    second(cx - 2, False)
    second(cx - 1, False)


def join_second_kernel(
    parity_ref, c, inv, energy, edge_a, edge_b, own_a, own_b, got_a, got_b, b_a, b_b, u3_in, u4_in,
    u3, u4, halo_a, halo_b, pay_a, pay_b, energy_rows, delta,
):
    cx, side_cells = c.shape[0], c.shape[1]
    third = energy[2]
    fourth = energy[3]
    for side, (edge, own, got, gb, halo, pay) in enumerate(
        ((edge_a, own_a, got_a, b_a, halo_a, pay_a), (edge_b, own_b, got_b, b_b, halo_b, pay_b))
    ):
        x0, x1 = (end_layer(parity_ref[0], side, k, cx) for k in range(2))
        b = flat(own, side_cells)
        join_forward(
            x0, x1, flat(edge, 0), u3, u4, c, inv, flat(got, 0), flat(got, side_cells),
            flat(gb, side_cells), b, halo, delta, side_cells,
        )
        for row, count in chunks(side_cells):
            at = pl.ds(row, count)
            value, other = u4[x0, at, :], u4[x1, at, :]
            pay[at, :] = 2.0 * b(row, count) * value
            third = third + fold(u3[x0, at, :] ** 2)
            fourth = fourth + fold(value * value + other * other)
        for row, count in chunks(side_cells):
            at = pl.ds(row, count)
            q, total = beside(flat(pay, 0), row, count, side_cells)
            total = total + 2.0 * (c[x1, at, :] * inv[x1, at, :]) * u4[x1, at, :]
            pay[pl.ds(side_cells + row, count), :] = b(row, count) * (
                4.0 * (inv[x0, at, :] * u4[x0, at, :]) + total - 6.0 * q
            )
    lane = lax.broadcasted_iota(jnp.int32, energy_rows.shape, 1)
    rows = jnp.zeros(energy_rows.shape, F32)
    for n, part in enumerate((energy[0], energy[1], third, fourth)):
        total = jnp.sum(jnp.sum(part, axis=0, keepdims=True), axis=1, keepdims=True)
        rows = jnp.where(lane == n, total, rows)
    energy_rows[...] = rows


def adjoint_kernel(all_cells, params, sums, u2, u3, u4, c, inv, weights, w4, w3, w2, q2, q4, q3):
    cx, side_cells = u2.shape[0], u2.shape[1]
    totals = jnp.sum(sums[...], axis=0, keepdims=True) / all_cells
    lane = lax.broadcasted_iota(jnp.int32, totals.shape, 1)
    weight = jnp.zeros((1, 1), F32)
    for n in range(STEPS):
        rest = jnp.where(jnp.logical_and(lane >= n, lane < STEPS), totals, 0.0)
        schroeder = params[0:1, STEPS : STEPS + 1] + jnp.sum(rest, axis=1, keepdims=True)
        weight = weight + 2.0 * (jnp.log(schroeder) - params[0:1, n : n + 1]) / schroeder
        weights[8 * n : 8 * n + 8, :] = jnp.broadcast_to(2.0 * weight, (8, side_cells))

    def zeroth(x):
        for row, count in chunks(side_cells):
            at = pl.ds(row, count)
            value = spread_weight(weights, 3, count) * (inv[x, at, :] * u4[x, at, :])
            w4[x, at, :] = value
            q4[x, at, :] = c[x, at, :] * value

    def first(x):
        for row, count in chunks(side_cells):
            at = pl.ds(row, count)
            value = backward(
                layer(q4, x), w4[x, at, :], None, layer(inv, x),
                spread_weight(weights, 2, count) * u3[x, at, :],
                x_sides(q4, x, cx), row, count, side_cells,
            )
            w3[x, at, :] = value
            q3[x, at, :] = c[x, at, :] * value

    def second(x):
        for row, count in chunks(side_cells):
            at = pl.ds(row, count)
            value = backward(
                layer(q3, x), w3[x, at, :], w4[x, at, :], layer(inv, x),
                spread_weight(weights, 1, count) * u2[x, at, :],
                x_sides(q3, x, cx), row, count, side_cells,
            )
            w2[x, at, :] = value
            q2[x, at, :] = c[x, at, :] * value

    sweep(0, cx, zeroth)
    for body in (first, second):
        body(0)
        sweep(1, cx - 1, body)
        body(cx - 1)


def join_third_kernel(
    parity_ref, weights, u1, c, inv, u3h_a, u3h_b, own_a, own_b, got_a, got_b, b_a, b_b,
    w3_in, w2_in, q2_in,
    w3, w2, q2, pay_a, pay_b, halo, delta,
):
    cx, side_cells = c.shape[0], c.shape[1]
    g = [spread_weight(weights, n, CHUNK) for n in range(STEPS)]
    for side, (u3h, own, got, b, pay) in enumerate(
        ((u3h_a, own_a, got_a, b_a, pay_a), (u3h_b, own_b, got_b, b_b, pay_b))
    ):
        x0, x1 = (end_layer(parity_ref[0], side, k, cx) for k in range(2))
        for row, count in chunks(side_cells):
            at, below = pl.ds(row, count), pl.ds(side_cells + row, count)
            change = (0.5 * g[3]) * (inv[x0, at, :] * got[at, :])
            w3[x0, at, :] += change
            change = c[x0, at, :] * change
            delta[at, :] = change
            bh = b[below, :]
            halo[at, :] = (0.5 * g[3]) * (got[below, :] + bh * own[at, :]) + g[2] * (bh * u3h[at, :])
            value = w2[x1, at, :] + inv[x1, at, :] * change
            w2[x1, at, :] = value
            q2[x1, at, :] = c[x1, at, :] * value
        for row, count in chunks(side_cells):
            at = pl.ds(row, count)
            v, total = beside(flat(delta, 0), row, count, side_cells)
            i = inv[x0, at, :]
            value = w2[x0, at, :] + i * (
                g[3] * (i * got[at, :]) + total - 6.0 * v + halo[at, :]
            )
            w2[x0, at, :] = value
            value = c[x0, at, :] * value
            q2[x0, at, :] = value
            pay[at, :] = value
        for row, count in chunks(side_cells):
            at = pl.ds(row, count)
            pay[pl.ds(side_cells + row, count), :] = c[x0, at, :] * backward(
                flat(pay, 0), w2[x0, at, :], w3[x0, at, :], layer(inv, x0),
                g[0] * u1[x0, at, :], [layer(q2, x1)], row, count, side_cells,
            )


def adjoint_end_kernel(weights, u1, w2, w3, q2, c, inv, w1, q1):
    cx, side_cells = u1.shape[0], u1.shape[1]
    g0 = spread_weight(weights, 0, CHUNK)

    def first(x):
        for row, count in chunks(side_cells):
            at = pl.ds(row, count)
            value = backward(
                layer(q2, x), w2[x, at, :], w3[x, at, :], layer(inv, x), g0 * u1[x, at, :],
                x_sides(q2, x, cx), row, count, side_cells,
            )
            w1[x, at, :] = value
            q1[x, at, :] = c[x, at, :] * value

    first(0)
    sweep(1, cx - 1, first)
    first(cx - 1)


def result_kernel(w1, q1, w2, s, dealt, cur_hbm, prev_hbm, cur_ends, mine, cur, prev, sems):
    cx, side_cells = w1.shape[0], w1.shape[1]
    mine[...] = jnp.sum(dealt[...], axis=0, keepdims=True) / float(PATCH_CELLS)

    def send_cur(x):
        return pltpu.make_async_copy(cur.at[x], cur_hbm.at[x], sems.at[0, x])

    def send_prev(x):
        return pltpu.make_async_copy(prev.at[x], prev_hbm.at[x], sems.at[1, x])

    def turn(x, ends=None):
        for row, count in chunks(side_cells):
            at = pl.ds(row, count)
            q, total = beside(layer(q1, x), row, count, side_cells)
            for other in x_sides(q1, x, cx):
                total = total + other(row, count)
            w, keep = w1[x, at, :], s[x, at, :] - 1.0
            value = 2.0 * w + total - 6.0 * q + keep * w2[x, at, :]
            if ends is None:
                cur[x, at, :] = value
            else:
                cur_ends[ends, at, :] = value
            prev[x, at, :] = keep * w
        if ends is None:
            send_cur(x).start()
        if ends in (None, 1, 2):
            send_prev(x).start()

    turn(1, 1)
    turn(cx - 2, 2)
    sweep(2, cx - 2, turn)
    turn(0, 0)
    turn(cx - 1, 3)
    sweep(1, cx - 1, lambda x: send_prev(x).wait())
    sweep(2, cx - 2, lambda x: send_cur(x).wait())


def patch_kernel(
    own, parity_ref, maps, wall_gain, up, u, u1, u2, u3, u4, w4, w3, w2, w1, q2,
    sums, values, columns, totals,
):
    cx, side_cells = u.shape[0], u.shape[1]
    last = side_cells - 1
    ends = [end_layer(parity_ref[0], side, 0, cx) for side in range(2)]

    def field(x, at, lanes):
        k = (x, at, lanes)
        return (
            w4[k] * (u2[k] - u4[k])
            + w3[k] * (u1[k] - u3[k])
            + (w2[k] * (u[k] - u2[k]) + w1[k] * (up[k] - u1[k]))
        )

    everything = pl.ds(0, side_cells)
    low, high = pl.ds(0, LANES), pl.ds(side_cells - LANES, LANES)
    for x in range(cx):
        values[4 * x : 4 * x + 1, :] = field(x, pl.ds(0, 8), everything)[0:1]
        values[4 * x + 1 : 4 * x + 2, :] = field(x, pl.ds(last - 7, 8), everything)[7:8]
    base = 2 * cx
    spot = lax.broadcasted_iota(jnp.int32, (CHUNK, LANES), 1)

    def gather(k, carry):
        at = pl.ds(pl.multiple_of(k * CHUNK, CHUNK), CHUNK)
        total = jnp.zeros((CHUNK, LANES), F32)
        for x in range(cx):
            for j, (lanes, lane_from) in enumerate(((low, 0), (high, LANES - 1))):
                tile = to_lane(field(x, at, lanes), 2 * x + j, lane_from)
                total = jnp.where(spot == 2 * x + j, tile, total)
        for side in range(2):
            for j, (lanes, lane_from) in enumerate(((low, 0), (high, LANES - 1))):
                place = base + 2 * side + j
                total = jnp.where(
                    spot == place, to_lane(q2[ends[side], at, lanes], place, lane_from), total
                )
        columns[at, :] = total
        return carry

    lax.fori_loop(0, side_cells // CHUNK, gather, 0)
    rows = jnp.transpose(columns[...])
    for x in range(cx):
        values[4 * x + 2 : 4 * x + 4, :] = rows[2 * x : 2 * x + 2, :]
    for side in range(2):
        at, place = base + 2 * side, 4 * (cx + side)
        theirs = jnp.concatenate(
            [q2[ends[side], 0:1, :], q2[ends[side], last : last + 1, :], rows[at : at + 2, :]], axis=0
        )
        values[place : place + 4, :] = theirs * wall_gain[4 * side : 4 * side + 4, :]
    all_maps, all_values = maps[...], values[...]

    def patch(k, carry):
        for m in range(GROUP // 8):
            block = []
            for j in range(8):
                picked = fold(jnp.where(all_maps == GROUP * k + 8 * m + j, all_values, 0.0))
                half = picked[:, :LANES]
                for first in range(LANES, side_cells, LANES):
                    half = half + picked[:, first : first + LANES]
                block.append(jnp.sum(half, axis=0, keepdims=True))
            total = jnp.sum(jnp.concatenate(block, axis=0), axis=1, keepdims=True)
            totals[pl.ds(pl.multiple_of(GROUP * k + 8 * m, 8), 8), :] = jnp.broadcast_to(
                total, (8, LANES)
            )
        return carry

    lax.fori_loop(0, totals.shape[0] // GROUP, patch, 0)
    every = totals[...]
    ahead = lax.broadcasted_iota(jnp.int32, every.shape, 0) - lax.broadcasted_iota(
        jnp.int32, every.shape, 1
    )
    ahead = jnp.where(lax.broadcasted_iota(jnp.int32, every.shape, 1) < own, ahead, -1)

    def owner(d, carry):
        for k in range(4):
            mine = jnp.where(ahead == (4 * d + k) * own, every, 0.0)
            sums[pl.ds(4 * d + k, 1), :] = jnp.sum(mine, axis=0, keepdims=True)
        return carry

    lax.fori_loop(0, sums.shape[0] // 4, owner, 0)


def join_last_kernel(
    parity_ref, w1, q2, c, inv, s, got_a, got_b, b_a, b_b, cur_ends, cur_in, prev_in,
    cur_hbm, prev_hbm, delta, cur, prev, sems,
):
    cx, side_cells = w1.shape[0], w1.shape[1]
    copies = []

    def send(src, dst, x):
        copies.append(pltpu.make_async_copy(src, dst.at[x], sems.at[len(copies)]))
        copies[-1].start()

    for side, (got, b) in enumerate(((got_a, b_a), (got_b, b_b))):
        x0, x1 = (end_layer(parity_ref[0], side, k, cx) for k in range(2))
        e0, e1 = (end_layer(parity_ref[0], side, k, 4) for k in range(2))
        for row, count in chunks(side_cells):
            at = pl.ds(row, count)
            change = inv[x0, at, :] * got[at, :]
            prev[side, at, :] = (s[x0, at, :] - 1.0) * (w1[x0, at, :] + change)
            change = c[x0, at, :] * change
            delta[at, :] = change
            cur[2 * side + 1, at, :] = cur_ends[e1, at, :] + change
        send(prev.at[side], prev_hbm, x0)
        send(cur.at[2 * side + 1], cur_hbm, x1)
        for row, count in chunks(side_cells):
            at, below = pl.ds(row, count), pl.ds(side_cells + row, count)
            v, total = beside(flat(delta, 0), row, count, side_cells)
            cur[2 * side, at, :] = (
                cur_ends[e0, at, :]
                + 2.0 * (inv[x0, at, :] * got[at, :])
                + (total - 6.0 * v)
                + (got[below, :] + b[below, :] * q2[x0, at, :])
            )
        send(cur.at[2 * side], cur_hbm, x0)
    for copy in copies:
        copy.wait()


def call(kernel, ins, outs, scratch=(), aliases=None, name=None, us=2.0):
    kinds = {"v": in_vmem, "s": in_smem, "h": in_hbm}
    return pl.pallas_call(
        kernel,
        out_shape=[
            (pltpu.VMEM if kind == "v" else pltpu.HBM)(shape, *(dtype or [F32]))
            for kind, shape, *dtype in outs
        ],
        in_specs=[kinds[kind] for kind, _ in ins],
        out_specs=[kinds[kind] for kind, *_ in outs],
        scratch_shapes=list(scratch),
        input_output_aliases=aliases or {},
        compiler_params=pltpu.CompilerParams(vmem_limit_bytes=12 * 2**20),
        cost_estimate=pl.CostEstimate(flops=0, transcendentals=0, bytes_accessed=int(us * 3.0e6)),
        name=name,
    )(*[value for _, value in ins])


def on_device(u_prev, u_cur, courant_sq, patch_map, absorb, checkpoint, target_curve, tail_energy):
    cx, side = u_cur.shape[0], u_cur.shape[1]
    count = lax.axis_size("gx")
    patches = absorb.shape[0]
    own = patches // count
    all_cells = float(cx * count * side * side)
    field, plane = (cx, side, side), (side, side)
    double, triple = (2 * side, side), (2 * side + 8, side)
    parity = lax.rem(lax.axis_index("gx"), 2).astype(jnp.int32).reshape(1)
    within = [(i, i ^ 1) for i in range(count)]
    across = [(i, i + 1) for i in range(1, count - 1, 2)]
    across = across + [(j, i) for i, j in across]

    def swap(a, b):
        b = lax.ppermute(b, "gx", across)
        return lax.ppermute(a, "gx", within), b

    def deal(rows):
        return lax.all_to_all(rows, "gx", 0, 0, tiled=True)

    dma = pltpu.SemaphoreType.DMA
    sp, ab = ("s", parity), ("s", absorb)
    v = lambda *arrays: [("v", a) for a in arrays]
    raw = [
        ("h", pltpu.with_memory_space_constraint(a, pltpu.HBM))
        for a in (u_cur, u_prev, courant_sq)
    ]
    edge = call(start_kernel, [sp, raw[0]], [("v", plane)] * 2, [dma((2,))], name="edges", us=1.0)
    near = swap(*edge)
    *pays, columns, found, params = call(
        setup_kernel,
        [sp, ab, ("s", checkpoint), ("s", target_curve), ("s", tail_energy)]
        + v(patch_map, *edge)
        + raw,
        [("v", triple)] * 2
        + [("v", (side, LANES)), ("v", (4 * cx, side)), ("v", (8, LANES))],
        [
            VMEM((4 * cx, side), jnp.int32),
            VMEM((LANES, side), F32),
            VMEM((2, side, side), F32),
            VMEM((2, side, side), F32),
            VMEM((2, side, side), F32),
            VMEM((2, side, side), F32),
            VMEM((side, LANES), F32),
            dma((6,)),
        ],
        name="damping",
        us=2.6,
    )
    first = swap(*pays)
    u, up, c, s, inv, u1, u2 = call(
        ahead_kernel, v(columns, found) + raw, [("v", field)] * 7, [dma((3,))], name="forward_1_2", us=7.0
    )
    u1, u2, u1h_a, u1h_b, *edge_2 = call(
        join_first_kernel,
        [sp] + v(c, inv, *edge, *near, *pays, *first, u1, u2),
        [("v", field)] * 2 + [("v", plane)] * 2 + [("v", double)] * 2,
        [VMEM(plane, F32)],
        aliases={11: 0, 12: 1},
        name="edges_1_2",
    )
    second = swap(*edge_2)
    u3, u4, energy, maps, wall_gain = call(
        ahead_again_kernel,
        [ab] + v(patch_map, u1, u2, c, inv, u1h_a, u1h_b, *first),
        [("v", field)] * 2
        + [("v", (STEPS, 8, side)), ("v", (4 * cx + 8, side), jnp.int32), ("v", (8, side))],
        [VMEM((side, LANES), F32)],
        name="forward_3_4",
        us=5.5,
    )
    u3, u4, u3h_a, u3h_b, *edge_4, energy_rows = call(
        join_second_kernel,
        [sp] + v(c, inv, energy, *edge_2, *pays, *second, *first, u3, u4),
        [("v", field)] * 2 + [("v", plane)] * 2 + [("v", double)] * 2 + [("v", (count, LANES))],
        [VMEM(plane, F32)],
        aliases={12: 0, 13: 1},
        name="edges_3_4",
    )
    third = swap(*edge_4)
    sums = deal(energy_rows)
    weights, w4, w3, w2, q2 = call(
        functools.partial(adjoint_kernel, all_cells),
        v(params, sums, u2, u3, u4, c, inv),
        [("v", (8 * STEPS, side))] + [("v", field)] * 4,
        [VMEM(field, F32), VMEM(field, F32)],
        name="adjoint_3_2",
        us=5.0,
    )
    w3, w2, q2, *edge_2 = call(
        join_third_kernel,
        [sp] + v(weights, u1, c, inv, u3h_a, u3h_b, *edge_4, *third, *first, w3, w2, q2),
        [("v", field)] * 3 + [("v", double)] * 2,
        [VMEM(plane, F32), VMEM(plane, F32)],
        aliases={13: 0, 14: 1, 15: 2},
        name="edges_adjoint_3_2",
    )
    fourth = swap(*edge_2)
    w1, q1 = call(
        adjoint_end_kernel, v(weights, u1, w2, w3, q2, c, inv), [("v", field)] * 2, name="adjoint_1"
    )
    (partial,) = call(
        functools.partial(patch_kernel, own),
        [sp] + v(maps, wall_gain, up, u, u1, u2, u3, u4, w4, w3, w2, w1, q2),
        [("v", (count, LANES))],
        [
            VMEM((4 * cx + 8, side), F32),
            VMEM((side, LANES), F32),
            VMEM((-(-patches // GROUP) * GROUP, LANES), F32),
        ],
        name="patch_sums",
    )
    cur, prev, cur_ends, mine = call(
        result_kernel,
        v(w1, q1, w2, s, deal(partial)),
        [("h", field)] * 2 + [("v", (4, side, side)), ("v", (1, LANES))],
        [VMEM(field, F32), VMEM(field, F32), dma((2, cx))],
        name="adjoint_0",
    )
    grad_absorb = mine[0, :own]
    cur, prev = call(
        join_last_kernel,
        [sp] + v(w1, q2, c, inv, s, *fourth, *first, cur_ends) + [("h", cur), ("h", prev)],
        [("h", field)] * 2,
        [VMEM(plane, F32), VMEM((4, side, side), F32), VMEM((2, side, side), F32), dma((6,))],
        aliases={11: 0, 12: 1},
        name="edges_adjoint_1_0",
    )
    return prev, cur, grad_absorb


def solution(mesh):
    bricks = P(("groups", "gx"), None, None)
    return jax.shard_map(
        on_device,
        mesh=mesh,
        in_specs=(bricks, bricks, bricks, bricks, P("groups"), P("groups"), P("groups"), P("groups")),
        out_specs=(bricks, bricks, P(("groups", "gx"))),
        check_vma=False,
    )
```

time: 345 us -> 96.4 us (0.28)
  other arithmetic: 123 us -> 0 us
  local copies, waits for them, and re-layouts: 87.3 us -> 0.53 us
  blocking collectives: 65.8 us -> 30.3 us
  Pallas kernels: 0 us -> 33.8 us
  starting transfers between devices: 58.5 us -> 29.1 us
  between operations: 5.71 us -> 2.17 us
    scatter-add x1 -> x0, other arithmetic: 57 us -> none  [on_device(): jax.ops.segment_sum(faces_grad.reshape(-1), patch_map.reshape(-1), absorb...]
    gather x2 -> x0, local copies, waits for them, and re-layouts: 51 us -> none  [on_device(): face_absorb = absorb[patch_map]]
    psum x1 -> x0, blocking collectives: 34.5 us -> none  [on_device(): energy = lax.psum(local_energy, 'gx') / all_cells]
    pallas_call x0 -> x12, Pallas kernels: none -> 33.8 us  [call(): pl.pallas_call(kernel, out_shape=[(pltpu.VMEM if kind == 'v' else pltpu.H...]
    unnamed x1 -> x0, blocking collectives: 31.2 us -> none
    all_to_all x0 -> x2, blocking collectives: none -> 30.3 us  [deal(): return lax.all_to_all(rows, 'gx', 0, 0, tiled=True)]
    ppermute x16 -> x10, starting transfers between devices: 58.5 us -> 29.1 us  [the longest x5 25.7 us: swap(): return (lax.ppermute(a, 'gx', within), b)]
    concatenate x8 -> x0, other arithmetic: 25.3 us -> none  [extended(): jnp.concatenate([lax.ppermute(tail, axis, [(i, (i + 1) % count) for i in...]
  transfers between devices with their start and end apart: 16 -> 10, of which waited for: 4 -> 0; matrix products, arithmetic and copies ran while one was open for 36% -> 1% of each run, Pallas kernels for 0% -> 26%
where the time goes in v2:
time: 96.4 us; the launch traced here: 96 us
  Pallas kernels  33.8 us (35%)
  blocking collectives  30.3 us (31%)
  starting transfers between devices  29.1 us (30%)
  between operations  2.17 us (2%)
    pallas_call x12, Pallas kernels, call(): pl.pallas_call(kernel, out_shape=[(pltpu.VMEM if kind == 'v' else pltpu.H...  33.8 us
    all_to_all x2, blocking collectives, deal(): return lax.all_to_all(rows, 'gx', 0, 0, tiled=True)  30.3 us
    ppermute x5, starting transfers between devices, swap(): return (lax.ppermute(a, 'gx', within), b)  25.7 us
    ppermute x5, starting transfers between devices, swap(): b = lax.ppermute(b, 'gx', across)  3.39 us
  transfers between devices with their start and end apart: 10, of which 0 were waited for; matrix products, arithmetic and copies ran while one was open for 1% of the time, Pallas kernels for 26%

profile of v2, /device:TPU:0, one launch (start us, length us, event | category | flops | bytes accessed | tf_op | source)
XLA Modules:
  0.0 96.0 jit_solution(13194825224049488237)
XLA Ops:
  2.0 1.0 %edges.1 = (f32[256,256]{1,0:T(8,128)S(1)}, f32[256,256]{1,0:T(8,128)S(1)}) custom-call(s32[1]{0:T(128)} %bitcast.parity_ref, f32[8,256,256]{2,1,0:T(8,128)} %u_hbm.5), custom_call_target="tpu_custom_call" | custom-call | bytes 3000000 | tf_op jit(solution)/shard_map/edges/pallas_call | solution.py:685
  3.1 2.5 %damping.1 = (f32[520,256]{1,0:T(8,128)S(1)}, f32[520,256]{1,0:T(8,128)S(1)}, f32[256,128]{1,0:T(8,128)S(1)}, f32[32,256]{1,0:T(8,128)S(1)}, f32[8,128]{1,0:T(8,128)S(1)}) custom-call(s32[1]{0:T(128)} %bitcast.parity_ref, f32[160]{0:T(256)S(1)} %copy-done.1, s32[1]{0:T(128)S(6)} %copy.31.checkpoint_ref, f32[64]{0:T(128)S(1)} %copy-done.2, ...), custom_call_target="tpu_custom_call" | custom-call | bytes 7800000 | tf_op jit(solution)/shard_map/damping/pallas_call | solution.py:685
  5.6 0.5 collective-permute-start.2
  6.1 0.7 collective-permute-start.3
  6.8 3.9 %collective-permute-start = (f32[256,256]{1,0:T(8,128)S(1)}, f32[256,256]{1,0:T(8,128)S(1)}, u32[]{:S(2)}, u32[]{:S(2)}) collective-permute-start(f32[256,256]{1,0:T(8,128)S(1)} %get-tuple-element.53.e_a), channel_id=1, source_target_pairs={{0,1},{1,0},{2,3},{3,2},{4,5},{5,4},{6,7},{7,6},{8,9},{9,8},{10,11... | collective-permute-start | bytes 786440 | tf_op jit(solution)/shard_map/ppermute | solution.py:716
  10.8 0.7 collective-permute-start.1
  11.4 6.7 %forward_1_2.1 = (f32[8,256,256]{2,1,0:T(8,128)S(1)}, f32[8,256,256]{2,1,0:T(8,128)S(1)}, f32[8,256,256]{2,1,0:T(8,128)S(1)}, f32[8,256,256]{2,1,0:T(8,128)S(1)}...) custom-call(f32[256,128]{1,0:T(8,128)S(1)} %get-tuple-element.56.columns, ...), custom_call_target="tpu_custom_call" | custom-call | bytes 21000000 | tf_op jit(solution)/shard_map/forward_1_2/pallas_call | solution.py:685
  18.1 0.0 collective-permute-done.near_a
  18.2 0.0 collective-permute-done.1.near_b
  18.2 0.0 collective-permute-done.2.got_a.b_a
  18.2 0.0 collective-permute-done.3.got_b.b_b
  18.2 1.0 %edges_1_2.1 = (f32[8,256,256]{2,1,0:T(8,128)S(1)}, f32[8,256,256]{2,1,0:T(8,128)S(1)}, f32[256,256]{1,0:T(8,128)S(1)}, f32[256,256]{1,0:T(8,128)S(1)}, f32[512,256]{1,0:T(8,128)S(1)}, /*index=5*/f32[512,256]{1,0:T(8,128)S(1)}) custom-call(s32[1]{0:T(128)} %bitcast.parity_ref, ...), custom_call_target="tpu_custom_call", output_to_operand_aliasing={{0}: (11, {}), {1}: (12, {})} | custom-call | bytes 6000000 | tf_op jit(solution)/shard_map/edges_1_2/pallas_call | solution.py:685
  19.2 10.1 %collective-permute-start.4 = (f32[512,256]{1,0:T(8,128)S(1)}, f32[512,256]{1,0:T(8,128)S(1)}, u32[]{:S(2)}, u32[]{:S(2)}) collective-permute-start(f32[512,256]{1,0:T(8,128)S(1)} %get-tuple-element.69.edge_a), channel_id=1, source_target_pairs={{0,1},{1,0},{2,3},{3,2},{4,5},{5,4},{6,7},{7,6},{8,9},{9,8},{10,11... | collective-permute-start | bytes 1572872 | tf_op jit(solution)/shard_map/ppermute | solution.py:716
  29.3 0.7 collective-permute-start.5
  30.0 5.0 %forward_3_4.1 = (f32[8,256,256]{2,1,0:T(8,128)S(1)}, f32[8,256,256]{2,1,0:T(8,128)S(1)}, f32[4,8,256]{2,1,0:T(8,128)S(1)}, s32[40,256]{1,0:T(8,128)S(1)}, f32[8,256]{1,0:T(8,128)S(1)}) custom-call(f32[160]{0:T(256)S(1)} %copy-done.1, s32[8,4,256]{2,1,0:T(4,128)S(1)} %copy-done, f32[8,256,256]{2,1,0:T(8,128)S(1)} %get-tuple-element.64.u1, ...), custom_call_target="tpu_custom_call" | custom-call | bytes 16500000 | tf_op jit(solution)/shard_map/forward_3_4/pallas_call | solution.py:685
  35.0 0.0 collective-permute-done.4.got_a
  35.0 1.2 %edges_3_4.1 = (f32[8,256,256]{2,1,0:T(8,128)S(1)}, f32[8,256,256]{2,1,0:T(8,128)S(1)}, f32[256,256]{1,0:T(8,128)S(1)}, f32[256,256]{1,0:T(8,128)S(1)}, f32[512,...) custom-call(s32[1]{0:T(128)} %bitcast.parity_ref, ...), custom_call_target="tpu_custom_call", output_to_operand_aliasing={{0}: (12, {}), {1}: (13, {})} | custom-call | bytes 6000000 | tf_op jit(solution)/shard_map/edges_3_4/pallas_call | solution.py:685
  36.2 10.5 %collective-permute-start.6 = (f32[512,256]{1,0:T(8,128)S(1)}, f32[512,256]{1,0:T(8,128)S(1)}, u32[]{:S(2)}, u32[]{:S(2)}) collective-permute-start(f32[512,256]{1,0:T(8,128)S(1)} %get-tuple-element.79.own_a), channel_id=1, source_target_pairs={{0,1},{1,0},{2,3},{3,2},{4,5},{5,4},{6,7},{7,6},{8,9},{9,8},{10,11... | collective-permute-start | bytes 1572872 | tf_op jit(solution)/shard_map/ppermute | solution.py:716
  46.7 0.7 collective-permute-start.7
  47.4 14.9 %all_to_all.22 = f32[16,1,128]{2,1,0:T(1,128)S(1)} all-to-all(f32[16,1,128]{2,1,0:T(1,128)S(1)} %bitcast.14), channel_id=1, replica_groups=mesh['groups'=2,'gx'=16] {'gx'}, dimensions={0} | all-to-all | bytes 16384 | tf_op jit(solution)/shard_map/all_to_all | solution.py:719
  62.3 4.9 %adjoint_3_2.1 = (f32[32,256]{1,0:T(8,128)S(1)}, f32[8,256,256]{2,1,0:T(8,128)S(1)}, f32[8,256,256]{2,1,0:T(8,128)S(1)}, f32[8,256,256]{2,1,0:T(8,128)S(1)}, f32[8,256,256]{2,1,0:T(8,128)S(1)}) custom-call(f32[8,128]{1,0:T(8,128)S(1)} %get-tuple-element.55.params, f32[16,128]{1,0:T(8,128)S(1)} %bitcast.13, f32[8,256,256]{2,1,0:T(8,128)S(1)} %get-tuple-element.65.u2, ...), custom_call_target="tpu_custom_call" | custom-call | bytes 15000000 | tf_op jit(solution)/shard_map/adjoint_3_2/pallas_call | solution.py:685
  67.2 1.2 %edges_adjoint_3_2.1 = (f32[8,256,256]{2,1,0:T(8,128)S(1)}, f32[8,256,256]{2,1,0:T(8,128)S(1)}, f32[8,256,256]{2,1,0:T(8,128)S(1)}, f32[512,256]{1,0:T(8,128)S(1)}, f32[512,256]{1,0:T(8,128)S(1)}) custom-call(s32[1]{0:T(128)} %bitcast.parity_ref, ...), custom_call_target="tpu_custom_call", output_to_operand_aliasing={{0}: (13, {}), {1}: (14, {}), {2}: (15, {})} | custom-call | bytes 6000000 | tf_op jit(solution)/shard_map/edges_adjoint_3_2/pallas_call | solution.py:685
  68.4 0.7 collective-permute-start.8
  69.2 0.7 collective-permute-start.9
  69.8 2.1 %adjoint_1.1 = (f32[8,256,256]{2,1,0:T(8,128)S(1)}, f32[8,256,256]{2,1,0:T(8,128)S(1)}) custom-call(f32[32,256]{1,0:T(8,128)S(1)} %get-tuple-element.76.weights, f32[8,256,256]{2,1,0:T(8,128)S(1)} %get-tuple-element.64.u1, f32[8,256,256]{2,1,0:T(8,128)S(1)} %get-tuple-element.84.w2, f32[8,256,256]{2,1,0:T(8,128)S(1)} %get-tuple-element.85.w3, ...), custom_call_target="tpu_custom_call" | custom-call | bytes 6000000 | tf_op jit(solution)/shard_map/adjoint_1/pallas_call | solution.py:685
  72.0 4.2 %patch_sums.1 = f32[16,128]{1,0:T(8,128)S(1)} custom-call(s32[1]{0:T(128)} %bitcast.parity_ref, s32[40,256]{1,0:T(8,128)S(1)} %get-tuple-element.92.maps, f32[8,256]{1,0:T(8,128)S(1)} %get-tuple-element.93.wall_gain, f32[8,256,256]{2,1,0:T(8,128)S(1)} %get-tuple-element.94.up, f32[8,256,256]{2,1,0:T(8,128)S(1)} %get-tuple-element.95.u, ...), custom_call_target="tpu_custom_call" | custom-call | bytes 6000000 | tf_op jit(solution)/shard_map/patch_sums/pallas_call | solution.py:685
  76.2 15.4 %all_to_all.23 = f32[16,1,128]{2,1,0:T(1,128)S(1)} all-to-all(f32[16,1,128]{2,1,0:T(1,128)S(1)} %bitcast.11), channel_id=1, replica_groups=mesh['groups'=2,'gx'=16] {'gx'}, dimensions={0} | all-to-all | bytes 16384 | tf_op jit(solution)/shard_map/all_to_all | solution.py:719
  91.6 2.5 %adjoint_0.1 = (f32[8,256,256]{2,1,0:T(8,128)}, f32[8,256,256]{2,1,0:T(8,128)}, f32[4,256,256]{2,1,0:T(8,128)S(1)}, f32[1,128]{1,0:T(1,128)S(1)}) custom-call(f32[8,256,256]{2,1,0:T(8,128)S(1)} %get-tuple-element.87.w1, f32[8,256,256]{2,1,0:T(8,128)S(1)} %get-tuple-element.91.q1, f32[8,256,256]{2,1,0:T(8,128)S(1)} %get-tuple-element.84.w2, ...), custom_call_target="tpu_custom_call" | custom-call | bytes 6000000 | tf_op jit(solution)/shard_map/adjoint_0/pallas_call | solution.py:685
  94.1 0.5 slice_bitcast_fusion
  94.6 0.0 collective-permute-done.8.got_a
  94.6 0.0 collective-permute-done.9.got_b
  94.6 1.4 %edges_adjoint_1_0.1 = (f32[8,256,256]{2,1,0:T(8,128)}, f32[8,256,256]{2,1,0:T(8,128)}) custom-call(s32[1]{0:T(128)} %bitcast.parity_ref, f32[8,256,256]{2,1,0:T(8,128)S(1)} %get-tuple-element.87.w1, f32[8,256,256]{2,1,0:T(8,128)S(1)} %get-tuple-element.86.q2, ...), custom_call_target="tpu_custom_call", output_to_operand_aliasing={{0}: (11, {}), {1}: (12, {})} | custom-call | bytes 6000000 | tf_op jit(solution)/shard_map/edges_adjoint_1_0/pallas_call | solution.py:685
  (9 shorter events, 0.0 us)
Async XLA Ops:
  0.6 2.4 %copy-start.1 = (f32[160]{0:T(256)S(1)}, f32[160]{0:T(256)}, u32[]{:S(2)}) copy-start(f32[160]{0:T(256)} %absorb_ref.3) | copy-start | bytes 1924
  0.6 2.4 %copy-start = (s32[8,4,256]{2,1,0:T(4,128)S(1)}, s32[8,4,256]{2,1,0:T(4,128)}, u32[]{:S(2)}) copy-start(s32[8,4,256]{2,1,0:T(4,128)} %map_ref.3) | copy-start | bytes 98308
  0.7 2.4 %copy-start.2 = (f32[64]{0:T(128)S(1)}, f32[64]{0:T(128)}, u32[]{:S(2)}) copy-start(f32[64]{0:T(128)} %target_ref.1) | copy-start | bytes 772
  5.6 12.5 %collective-permute-start.2 = (f32[520,256]{1,0:T(8,128)S(1)}, f32[520,256]{1,0:T(8,128)S(1)}, u32[]{:S(2)}, u32[]{:S(2)}) collective-permute-start(f32[520,256]{1,0:T(8,128)S(1)} %get-tuple-element.60.own_a), channel_id=1, source_target_pairs={{0,1},{1,0},{2,3},{3,2},{4,5},{5,4},{6,7},{7,6},{8,9},{9,8},{10,11... | collective-permute-start | bytes 1597448 | tf_op jit(solution)/shard_map/ppermute | solution.py:716
  6.1 12.0 %collective-permute-start.3 = (f32[520,256]{1,0:T(8,128)S(1)}, f32[520,256]{1,0:T(8,128)S(1)}, u32[]{:S(2)}, u32[]{:S(2)}) collective-permute-start(f32[520,256]{1,0:T(8,128)S(1)} %get-tuple-element.61.own_b), channel_id=1, source_target_pairs={{1,2},{3,4},{5,6},{7,8},{9,10},{11,12},{13,14},{2,1},{4,3},{6,5},{... | collective-permute-start | bytes 1597448 | tf_op jit(solution)/shard_map/ppermute | solution.py:715
  6.8 11.3 %collective-permute-start = (f32[256,256]{1,0:T(8,128)S(1)}, f32[256,256]{1,0:T(8,128)S(1)}, u32[]{:S(2)}, u32[]{:S(2)}) collective-permute-start(f32[256,256]{1,0:T(8,128)S(1)} %get-tuple-element.53.e_a), channel_id=1, source_target_pairs={{0,1},{1,0},{2,3},{3,2},{4,5},{5,4},{6,7},{7,6},{8,9},{9,8},{10,11... | collective-permute-start | bytes 786440 | tf_op jit(solution)/shard_map/ppermute | solution.py:716
  10.8 7.4 %collective-permute-start.1 = (f32[256,256]{1,0:T(8,128)S(1)}, f32[256,256]{1,0:T(8,128)S(1)}, u32[]{:S(2)}, u32[]{:S(2)}) collective-permute-start(f32[256,256]{1,0:T(8,128)S(1)} %get-tuple-element.54.e_b), channel_id=1, source_target_pairs={{1,2},{3,4},{5,6},{7,8},{9,10},{11,12},{13,14},{2,1},{4,3},{6,5},{... | collective-permute-start | bytes 786440 | tf_op jit(solution)/shard_map/ppermute | solution.py:715
  19.2 15.8 %collective-permute-start.4 = (f32[512,256]{1,0:T(8,128)S(1)}, f32[512,256]{1,0:T(8,128)S(1)}, u32[]{:S(2)}, u32[]{:S(2)}) collective-permute-start(f32[512,256]{1,0:T(8,128)S(1)} %get-tuple-element.69.edge_a), channel_id=1, source_target_pairs={{0,1},{1,0},{2,3},{3,2},{4,5},{5,4},{6,7},{7,6},{8,9},{9,8},{10,11... | collective-permute-start | bytes 1572872 | tf_op jit(solution)/shard_map/ppermute | solution.py:716
  29.3 5.7 %collective-permute-start.5 = (f32[512,256]{1,0:T(8,128)S(1)}, f32[512,256]{1,0:T(8,128)S(1)}, u32[]{:S(2)}, u32[]{:S(2)}) collective-permute-start(f32[512,256]{1,0:T(8,128)S(1)} %get-tuple-element.70.edge_b), channel_id=1, source_target_pairs={{1,2},{3,4},{5,6},{7,8},{9,10},{11,12},{13,14},{2,1},{4,3},{6,5},{... | collective-permute-start | bytes 1572872 | tf_op jit(solution)/shard_map/ppermute | solution.py:715
  36.2 31.0 %collective-permute-start.6 = (f32[512,256]{1,0:T(8,128)S(1)}, f32[512,256]{1,0:T(8,128)S(1)}, u32[]{:S(2)}, u32[]{:S(2)}) collective-permute-start(f32[512,256]{1,0:T(8,128)S(1)} %get-tuple-element.79.own_a), channel_id=1, source_target_pairs={{0,1},{1,0},{2,3},{3,2},{4,5},{5,4},{6,7},{7,6},{8,9},{9,8},{10,11... | collective-permute-start | bytes 1572872 | tf_op jit(solution)/shard_map/ppermute | solution.py:716
  46.7 20.5 %collective-permute-start.7 = (f32[512,256]{1,0:T(8,128)S(1)}, f32[512,256]{1,0:T(8,128)S(1)}, u32[]{:S(2)}, u32[]{:S(2)}) collective-permute-start(f32[512,256]{1,0:T(8,128)S(1)} %get-tuple-element.80.own_b), channel_id=1, source_target_pairs={{1,2},{3,4},{5,6},{7,8},{9,10},{11,12},{13,14},{2,1},{4,3},{6,5},{... | collective-permute-start | bytes 1572872 | tf_op jit(solution)/shard_map/ppermute | solution.py:715
  68.4 26.2 %collective-permute-start.8 = (f32[512,256]{1,0:T(8,128)S(1)}, f32[512,256]{1,0:T(8,128)S(1)}, u32[]{:S(2)}, u32[]{:S(2)}) collective-permute-start(f32[512,256]{1,0:T(8,128)S(1)} %get-tuple-element.89), channel_id=1, source_target_pairs={{0,1},{1,0},{2,3},{3,2},{4,5},{5,4},{6,7},{7,6},{8,9},{9,8},{10,11... | collective-permute-start | bytes 1572872 | tf_op jit(solution)/shard_map/ppermute | solution.py:716
  69.2 25.5 %collective-permute-start.9 = (f32[512,256]{1,0:T(8,128)S(1)}, f32[512,256]{1,0:T(8,128)S(1)}, u32[]{:S(2)}, u32[]{:S(2)}) collective-permute-start(f32[512,256]{1,0:T(8,128)S(1)} %get-tuple-element.90), channel_id=1, source_target_pairs={{1,2},{3,4},{5,6},{7,8},{9,10},{11,12},{13,14},{2,1},{4,3},{6,5},{... | collective-permute-start | bytes 1572872 | tf_op jit(solution)/shard_map/ppermute | solution.py:715

commit v3 on v2

v3 whole, which is shorter than its diff:
```python
import functools

import jax
import jax.numpy as jnp
from jax import lax
from jax.experimental import pallas as pl
from jax.experimental.pallas import tpu as pltpu
from jax.sharding import PartitionSpec as P

STEPS = 4
PATCH_CELLS = 819
CHUNK = 16
LANES = 128
GROUP = 80
F32 = jnp.float32
VMEM = pltpu.VMEM
in_vmem = pl.BlockSpec(memory_space=pltpu.VMEM)
in_smem = pl.BlockSpec(memory_space=pltpu.SMEM)
in_hbm = pl.BlockSpec(memory_space=pltpu.HBM)


def end_layer(parity, side, depth, cx):
    high = 1 - parity if side == 0 else parity
    return high * (cx - 1 - depth) + (1 - high) * depth


def own_parity():
    return lax.rem(lax.axis_index("gx"), 2)


def layer(ref, x):
    return lambda row, count: ref[x, pl.ds(row, count), :]


def flat(ref, base):
    return lambda row, count: ref[pl.ds(base + row, count), :]


def chunks(side_cells):
    return [(row, CHUNK) for row in range(0, side_cells, CHUNK)]


def beside(field, row, count, side_cells):
    v = field(row, count)
    tiles = [v[k : k + 8] for k in range(0, count, 8)]
    sub = lax.broadcasted_iota(jnp.int32, tiles[0].shape, 0)
    zero = jnp.zeros_like(tiles[0])
    before = pltpu.roll(field(row - 8, 8), 1, 0) if row else zero
    after = pltpu.roll(field(row + count, 8), 7, 0) if row + count < side_cells else zero
    down = [before] + [pltpu.roll(tile, 1, 0) for tile in tiles]
    up = [pltpu.roll(tile, 7, 0) for tile in tiles] + [after]
    total = jnp.concatenate(
        [
            jnp.where(sub == 0, down[k], down[k + 1]) + jnp.where(sub == 7, up[k + 1], up[k])
            for k in range(len(tiles))
        ],
        axis=0,
    )
    parts = [v[:, k : k + LANES] for k in range(0, side_cells, LANES)]
    lane = lax.broadcasted_iota(jnp.int32, parts[0].shape, 1)
    zero = jnp.zeros_like(parts[0])
    right = [zero] + [pltpu.roll(part, 1, 1) for part in parts]
    left = [pltpu.roll(part, LANES - 1, 1) for part in parts] + [zero]
    across = jnp.concatenate(
        [
            jnp.where(lane == 0, right[k], right[k + 1])
            + jnp.where(lane == LANES - 1, left[k + 1], left[k])
            for k in range(len(parts))
        ],
        axis=1,
    )
    return v, total + across


def forward(now, prior, courant, inverse, sides, row, count, side_cells):
    v, total = beside(now, row, count, side_cells)
    for other in sides:
        total = total + other(row, count)
    p = prior(row, count)
    c, i = courant(row, count), inverse(row, count)
    return i * (2.0 * (v - p) + c * (total - 6.0 * v)) + p


def backward(product, w, later, inverse, source, sides, row, count, side_cells):
    q, total = beside(product, row, count, side_cells)
    for other in sides:
        total = total + other(row, count)
    fresh = total - 6.0 * q + source
    i = inverse(row, count)
    if later is None:
        return i * (2.0 * w + fresh)
    return i * (2.0 * (w - later) + fresh) + later


def sweep(low, high, body):
    def turn(x, carry):
        body(x)
        return carry

    lax.fori_loop(low, high, turn, 0)


def x_sides(ref, x, cx):
    return [layer(ref, k) for k in (x - 1, x + 1) if not isinstance(k, int) or 0 <= k < cx]


def fold(values):
    total = values[0:8]
    for row in range(8, values.shape[0], 8):
        total = total + values[row : row + 8]
    return total


def spread_weight(weights, n, count):
    tile = weights[8 * n : 8 * n + 8, :]
    return jnp.concatenate([tile] * (count // 8), axis=0)


def start_kernel(map_hbm, u_hbm, c_hbm, c_a, u_b, c_b, maps, sems):
    cx, side_cells = u_hbm.shape[0], u_hbm.shape[1]
    copies = []
    ends = [end_layer(own_parity(), side, 0, cx) for side in range(2)]
    u_a = c_a.at[pl.ds(side_cells + 8, side_cells)]
    for side, (u, c) in enumerate(((u_a, c_a), (u_b, c_b))):
        x0 = ends[side]
        for k, (src, dst) in enumerate(
            ((map_hbm, maps.at[side]), (u_hbm, u), (c_hbm, c.at[pl.ds(0, side_cells)]))
        ):
            copies.append(pltpu.make_async_copy(src.at[x0], dst, sems.at[k, side]))
    for copy in copies:
        copy.start()
    for side, c in enumerate((c_a, c_b)):
        copies[3 * side].wait()
        c[side_cells : side_cells + 4, :] = maps[side].astype(F32)
        c[side_cells + 4 : side_cells + 8, :] = jnp.zeros((4, side_cells), F32)
    for k, copy in enumerate(copies):
        if k % 3:
            copy.wait()


def lookup(maps, absorb_ref):
    def turn(p, got):
        return jnp.where(maps == p, absorb_ref[p], got)

    return lax.fori_loop(0, absorb_ref.shape[0], turn, jnp.zeros(maps.shape, F32), unroll=8)


def to_lane(tile, spot, lane_from):
    return pltpu.roll(tile, (spot - lane_from) % LANES, 1)


def wall_fields(columns, gains, low, high, top, bottom, row, count, side_cells):
    lane = lax.broadcasted_iota(jnp.int32, (count, LANES), 1)

    def place(ref, other):
        tile = ref[pl.ds(row, count), :]
        near = pltpu.roll(tile, lax.rem(LANES - low, LANES), 1)
        far = pltpu.roll(tile, LANES - 1 - high, 1)
        mid = [jnp.full((count, LANES), other, F32)] * (side_cells // LANES - 2)
        return jnp.concatenate(
            [
                jnp.where(lane == 0, near, other),
                *mid,
                jnp.where(lane == LANES - 1, far, other),
            ],
            axis=1,
        )

    field = place(columns, 0.0)
    if 0 < row and row + count < side_cells:
        return field, place(gains, 1.0)
    sub = lax.broadcasted_iota(jnp.int32, field.shape, 0)
    if row == 0:
        field = field + jnp.where(sub == 0, top, 0.0)
    if row + count == side_cells:
        field = field + jnp.where(sub == count - 1, bottom, 0.0)
    return field, 1.0 / (1.0 + field)


def ahead_one_kernel(
    absorb_ref, checkpoint, target, tail, map_hbm, u_hbm, up_hbm, c_hbm,
    u, up, c, s, inv, u1, params, map_ref,
    maps, found, turned, columns, gains, sems,
):
    cx, side_cells = u.shape[0], u.shape[1]
    copies = [
        pltpu.make_async_copy(src, dst, sems.at[k])
        for k, (src, dst) in enumerate(
            ((map_hbm, map_ref), (u_hbm, u), (up_hbm, up), (c_hbm, c))
        )
    ]
    for copy in copies:
        copy.start()
    copies[0].wait()
    for x in range(cx):
        maps[4 * x : 4 * x + 4, :] = map_ref[x]
    found[...] = lookup(maps[...], absorb_ref)
    turned[...] = jnp.zeros_like(turned)
    for x in range(cx):
        turned[x : x + 1, :] = found[4 * x + 2 : 4 * x + 3, :]
        turned[cx + x : cx + x + 1, :] = found[4 * x + 3 : 4 * x + 4, :]
    columns[...] = jnp.transpose(turned[...])
    gains[...] = 1.0 / (1.0 + columns[...])

    def spread(x):
        for row, count in chunks(side_cells):
            at = pl.ds(row, count)
            field, gain = wall_fields(
                columns, gains, x, cx + x, found[pl.ds(4 * x, 1), :], found[pl.ds(4 * x + 1, 1), :],
                row, count, side_cells,
            )
            s[x, at, :] = field
            inv[x, at, :] = gain

    def first(x):
        for row, count in chunks(side_cells):
            u1[x, pl.ds(row, count), :] = forward(
                layer(u, x), layer(up, x), layer(c, x), layer(inv, x), x_sides(u, x, cx),
                row, count, side_cells,
            )

    sweep(0, cx, spread)
    for copy in copies[1:]:
        copy.wait()
    history = target.shape[1]
    lane = lax.broadcasted_iota(jnp.int32, params.shape, 1)
    spot = lax.broadcasted_iota(jnp.int32, target.shape, 1)
    start = jnp.clip(checkpoint[...], 0, history - STEPS)
    row = jnp.where(lane == STEPS, tail[...], 0.0)
    for n in range(STEPS):
        value = jnp.sum(jnp.where(spot == start + n, target[...], 0.0), axis=1, keepdims=True)
        row = jnp.where(lane == n, value, row)
    params[...] = row
    first(0)
    sweep(1, cx - 1, first)
    first(cx - 1)


def join_one_kernel(c, inv, near_a, near_b, u1_in, u1, edge_a, edge_b):
    cx, side_cells = c.shape[0], c.shape[1]
    near_a = near_a.at[pl.ds(side_cells + 8, side_cells)]
    for side, (near, edge) in enumerate(((near_a, edge_a), (near_b, edge_b))):
        x0 = end_layer(own_parity(), side, 0, cx)
        for row, count in chunks(side_cells):
            at = pl.ds(row, count)
            value = u1[x0, at, :] + (c[x0, at, :] * inv[x0, at, :]) * near[at, :]
            u1[x0, at, :] = value
            edge[at, :] = value


def wall_rows(plane, columns, side_cells):
    last = side_cells - 1
    spot = lax.broadcasted_iota(jnp.int32, (CHUNK, LANES), 1)
    low, high = pl.ds(0, LANES), pl.ds(side_cells - LANES, LANES)
    for row, count in chunks(side_cells):
        at = pl.ds(row, count)
        far = to_lane(plane(at, high), 1, LANES - 1)
        columns[at, :] = jnp.where(spot == 0, plane(at, low), jnp.where(spot == 1, far, 0.0))
    rows = jnp.transpose(columns[...])
    every = pl.ds(0, side_cells)
    return jnp.concatenate([plane(pl.ds(0, 1), every), plane(pl.ds(last, 1), every), rows[0:2]], axis=0)


def ahead_two_kernel(
    absorb_ref, map_ref, u, up, c, inv, u1, got_a, got_b,
    u2, own_a, own_b, b_a, b_b, maps, wall_gain, wall_prior, columns, gains, turned,
):
    cx, side_cells = u.shape[0], u.shape[1]
    last = side_cells - 1
    ends = [end_layer(own_parity(), side, 0, cx) for side in range(2)]
    for x in range(cx):
        maps[4 * x : 4 * x + 4, :] = map_ref[x]
    for side, got in enumerate((got_a, got_b)):
        maps[4 * (cx + side) : 4 * (cx + side) + 4, :] = got[
            side_cells : side_cells + 4, :
        ].astype(jnp.int32)
    damping = lookup(maps[4 * cx : 4 * cx + 8, :], absorb_ref)
    turned[...] = jnp.zeros_like(turned)
    for side in range(2):
        turned[2 * side : 2 * side + 2, :] = damping[4 * side + 2 : 4 * side + 4]
    columns[...] = jnp.transpose(turned[...])
    gains[...] = 1.0 / (1.0 + columns[...])
    lane = lax.broadcasted_iota(jnp.int32, (1, side_cells), 1)

    def corners(one, two):
        return jnp.where(lane == 0, one, 0.0) + jnp.where(lane == last, two, 0.0)

    for side, (got, own, b) in enumerate(((got_a, own_a, b_a), (got_b, own_b, b_b))):
        d = [damping[4 * side + f : 4 * side + f + 1] for f in range(4)]
        for row, count in chunks(side_cells):
            at = pl.ds(row, count)
            own[at, :] = c[ends[side], at, :] * inv[ends[side], at, :]
            _, gain = wall_fields(
                columns, gains, 2 * side, 2 * side + 1, d[0], d[1], row, count, side_cells
            )
            b[at, :] = got[at, :] * gain
        total = jnp.concatenate(
            [
                d[0] + corners(d[2][:, 0:1], d[3][:, 0:1]),
                d[1] + corners(d[2][:, last:], d[3][:, last:]),
                d[2] + corners(d[0][:, 0:1], d[1][:, 0:1]),
                d[3] + corners(d[0][:, last:], d[1][:, last:]),
            ],
            axis=0,
        )
        wall_gain[4 * side : 4 * side + 4, :] = 1.0 / (1.0 + total)
    for side in range(2):
        wall_prior[4 * side : 4 * side + 4, :] = wall_rows(
            lambda at, lanes, x=ends[side]: up[x, at, lanes], columns, side_cells
        )

    def second(x):
        for row, count in chunks(side_cells):
            u2[x, pl.ds(row, count), :] = forward(
                layer(u1, x), layer(u, x), layer(c, x), layer(inv, x), x_sides(u1, x, cx),
                row, count, side_cells,
            )

    second(0)
    sweep(1, cx - 1, second)
    second(cx - 1)


def join_two_kernel(
    c, inv, own_a, own_b, near_a, near_b, wall_prior, u1, u2_in, u2, pay_a, pay_b
):
    cx, side_cells = c.shape[0], c.shape[1]
    for side, (own, near, pay) in enumerate(((own_a, near_a, pay_a), (own_b, near_b, pay_b))):
        x0, x1 = (end_layer(own_parity(), side, k, cx) for k in range(2))
        for row, count in chunks(side_cells):
            at = pl.ds(row, count)
            value = u2[x0, at, :] + own[at, :] * near[at, :]
            u2[x0, at, :] = value
            pay[at, :] = value
        pay[2 * side_cells : 2 * side_cells + 4, :] = wall_prior[4 * side : 4 * side + 4, :]
        pay[2 * side_cells + 4 : 2 * side_cells + 8, :] = jnp.zeros((4, side_cells), F32)
        for row, count in chunks(side_cells):
            pay[pl.ds(side_cells + row, count), :] = forward(
                flat(pay, 0), layer(u1, x0), layer(c, x0), layer(inv, x0), [layer(u2, x1)],
                row, count, side_cells,
            )


def join_forward(x0, x1, edge, mid, last, c, inv, got_now, got_part, got_b, b, halo, delta, side_cells):
    for row, count in chunks(side_cells):
        at = pl.ds(row, count)
        change = b(row, count) * got_now(row, count)
        delta[at, :] = change
        mid[x0, at, :] += change
        halo[at, :] = got_part(row, count) + got_b(row, count) * edge(row, count)
        last[x1, at, :] += (c[x1, at, :] * inv[x1, at, :]) * change
    for row, count in chunks(side_cells):
        at = pl.ds(row, count)
        v, total = beside(flat(delta, 0), row, count, side_cells)
        last[x0, at, :] += (2.0 * inv[x0, at, :]) * v + b(row, count) * (
            total - 6.0 * v + halo[at, :]
        )


def ahead_again_kernel(u1, u2, c, inv, u1h_a, u1h_b, u3, u4, energy, wall_now, columns):
    cx, side_cells = u1.shape[0], u1.shape[1]
    for side, u1h in enumerate((u1h_a, u1h_b)):
        wall_now[4 * side : 4 * side + 4, :] = wall_rows(
            lambda at, lanes, u1h=u1h: u1h[at, lanes], columns, side_cells
        )
    energy[...] = jnp.zeros_like(energy)

    def first(x, inner):
        sums = [jnp.zeros((8, side_cells), F32)] * 3
        for row, count in chunks(side_cells):
            value = forward(
                layer(u2, x), layer(u1, x), layer(c, x), layer(inv, x), x_sides(u2, x, cx),
                row, count, side_cells,
            )
            u3[x, pl.ds(row, count), :] = value
            sums[0] = sums[0] + fold(u1[x, pl.ds(row, count), :] ** 2)
            sums[1] = sums[1] + fold(u2[x, pl.ds(row, count), :] ** 2)
            sums[2] = sums[2] + fold(value * value)
        for k in range(3 if inner else 2):
            energy[k] += sums[k]

    def second(x, inner):
        total = jnp.zeros((8, side_cells), F32)
        for row, count in chunks(side_cells):
            value = forward(
                layer(u3, x), layer(u2, x), layer(c, x), layer(inv, x), x_sides(u3, x, cx),
                row, count, side_cells,
            )
            u4[x, pl.ds(row, count), :] = value
            total = total + fold(value * value)
        if inner:
            energy[3] += total

    first(0, False)
    sweep(1, cx - 1, lambda x: first(x, True))
    first(cx - 1, False)
    second(0, False)
    second(1, False)
    sweep(2, cx - 2, lambda x: second(x, True))
    second(cx - 2, False)
    second(cx - 1, False)


def join_second_kernel(
    c, inv, energy, edge_a, edge_b, own_a, own_b, got_a, got_b, b_a, b_b, u3_in, u4_in,
    u3, u4, halo_a, halo_b, pay_a, pay_b, energy_rows, delta,
):
    cx, side_cells = c.shape[0], c.shape[1]
    third = energy[2]
    fourth = energy[3]
    for side, (edge, own, got, gb, halo, pay) in enumerate(
        ((edge_a, own_a, got_a, b_a, halo_a, pay_a), (edge_b, own_b, got_b, b_b, halo_b, pay_b))
    ):
        x0, x1 = (end_layer(own_parity(), side, k, cx) for k in range(2))
        b = flat(own, 0)
        join_forward(
            x0, x1, flat(edge, 0), u3, u4, c, inv, flat(got, 0), flat(got, side_cells),
            flat(gb, 0), b, halo, delta, side_cells,
        )
        for row, count in chunks(side_cells):
            at = pl.ds(row, count)
            value, other = u4[x0, at, :], u4[x1, at, :]
            pay[at, :] = 2.0 * b(row, count) * value
            third = third + fold(u3[x0, at, :] ** 2)
            fourth = fourth + fold(value * value + other * other)
        for row, count in chunks(side_cells):
            at = pl.ds(row, count)
            q, total = beside(flat(pay, 0), row, count, side_cells)
            total = total + 2.0 * (c[x1, at, :] * inv[x1, at, :]) * u4[x1, at, :]
            pay[pl.ds(side_cells + row, count), :] = b(row, count) * (
                4.0 * (inv[x0, at, :] * u4[x0, at, :]) + total - 6.0 * q
            )
    lane = lax.broadcasted_iota(jnp.int32, energy_rows.shape, 1)
    rows = jnp.zeros(energy_rows.shape, F32)
    for n, part in enumerate((energy[0], energy[1], third, fourth)):
        total = jnp.sum(jnp.sum(part, axis=0, keepdims=True), axis=1, keepdims=True)
        rows = jnp.where(lane == n, total, rows)
    energy_rows[...] = rows


def adjoint_free_kernel(u4, c, inv, w4, w3, q4):
    cx, side_cells = u4.shape[0], u4.shape[1]

    def zeroth(x):
        for row, count in chunks(side_cells):
            at = pl.ds(row, count)
            value = 2.0 * (inv[x, at, :] * u4[x, at, :])
            w4[x, at, :] = value
            q4[x, at, :] = c[x, at, :] * value

    def first(x):
        for row, count in chunks(side_cells):
            at = pl.ds(row, count)
            w3[x, at, :] = backward(
                layer(q4, x), w4[x, at, :], None, layer(inv, x), 0.0,
                x_sides(q4, x, cx), row, count, side_cells,
            )

    sweep(0, cx, zeroth)
    first(0)
    sweep(1, cx - 1, first)
    first(cx - 1)


def adjoint_kernel(
    all_cells, params, sums, u2, u3, c, inv, w4_in, w3_in, weights, w4, w3, w2, q2, q3
):
    cx, side_cells = u2.shape[0], u2.shape[1]
    totals = jnp.sum(sums[...], axis=0, keepdims=True) / all_cells
    lane = lax.broadcasted_iota(jnp.int32, totals.shape, 1)
    weight = jnp.zeros((1, 1), F32)
    for n in range(STEPS):
        rest = jnp.where(jnp.logical_and(lane >= n, lane < STEPS), totals, 0.0)
        schroeder = params[0:1, STEPS : STEPS + 1] + jnp.sum(rest, axis=1, keepdims=True)
        weight = weight + 2.0 * (jnp.log(schroeder) - params[0:1, n : n + 1]) / schroeder
        weights[8 * n : 8 * n + 8, :] = jnp.broadcast_to(2.0 * weight, (8, side_cells))

    def first(x):
        for row, count in chunks(side_cells):
            at = pl.ds(row, count)
            g3 = 0.5 * spread_weight(weights, 3, count)
            w4[x, at, :] = g3 * w4[x, at, :]
            value = g3 * w3[x, at, :] + spread_weight(weights, 2, count) * (
                inv[x, at, :] * u3[x, at, :]
            )
            w3[x, at, :] = value
            q3[x, at, :] = c[x, at, :] * value

    def second(x):
        for row, count in chunks(side_cells):
            at = pl.ds(row, count)
            value = backward(
                layer(q3, x), w3[x, at, :], w4[x, at, :], layer(inv, x),
                spread_weight(weights, 1, count) * u2[x, at, :],
                x_sides(q3, x, cx), row, count, side_cells,
            )
            w2[x, at, :] = value
            q2[x, at, :] = c[x, at, :] * value

    sweep(0, cx, first)
    second(0)
    sweep(1, cx - 1, second)
    second(cx - 1)


def join_third_kernel(
    weights, u1, c, inv, u3h_a, u3h_b, own_a, own_b, got_a, got_b, b_a, b_b,
    w3_in, w2_in, q2_in,
    w3, w2, q2, pay_a, pay_b, halo, delta,
):
    cx, side_cells = c.shape[0], c.shape[1]
    g = [spread_weight(weights, n, CHUNK) for n in range(STEPS)]
    for side, (u3h, own, got, b, pay) in enumerate(
        ((u3h_a, own_a, got_a, b_a, pay_a), (u3h_b, own_b, got_b, b_b, pay_b))
    ):
        x0, x1 = (end_layer(own_parity(), side, k, cx) for k in range(2))
        for row, count in chunks(side_cells):
            at, below = pl.ds(row, count), pl.ds(side_cells + row, count)
            change = (0.5 * g[3]) * (inv[x0, at, :] * got[at, :])
            w3[x0, at, :] += change
            change = c[x0, at, :] * change
            delta[at, :] = change
            bh = b[at, :]
            halo[at, :] = (0.5 * g[3]) * (got[below, :] + bh * own[at, :]) + g[2] * (bh * u3h[at, :])
            value = w2[x1, at, :] + inv[x1, at, :] * change
            w2[x1, at, :] = value
            q2[x1, at, :] = c[x1, at, :] * value
        for row, count in chunks(side_cells):
            at = pl.ds(row, count)
            v, total = beside(flat(delta, 0), row, count, side_cells)
            i = inv[x0, at, :]
            value = w2[x0, at, :] + i * (
                g[3] * (i * got[at, :]) + total - 6.0 * v + halo[at, :]
            )
            w2[x0, at, :] = value
            value = c[x0, at, :] * value
            q2[x0, at, :] = value
            pay[at, :] = value
        for row, count in chunks(side_cells):
            at = pl.ds(row, count)
            pay[pl.ds(side_cells + row, count), :] = c[x0, at, :] * backward(
                flat(pay, 0), w2[x0, at, :], w3[x0, at, :], layer(inv, x0),
                g[0] * u1[x0, at, :], [layer(q2, x1)], row, count, side_cells,
            )


def result_kernel(w1, q1, w2, s, dealt, cur_hbm, prev_hbm, cur_ends, mine, cur, prev, sems):
    cx, side_cells = w1.shape[0], w1.shape[1]
    mine[...] = jnp.sum(dealt[...], axis=0, keepdims=True) / float(PATCH_CELLS)

    def send_cur(x):
        return pltpu.make_async_copy(cur.at[x], cur_hbm.at[x], sems.at[0, x])

    def send_prev(x):
        return pltpu.make_async_copy(prev.at[x], prev_hbm.at[x], sems.at[1, x])

    def turn(x, ends=None):
        for row, count in chunks(side_cells):
            at = pl.ds(row, count)
            q, total = beside(layer(q1, x), row, count, side_cells)
            for other in x_sides(q1, x, cx):
                total = total + other(row, count)
            w, keep = w1[x, at, :], s[x, at, :] - 1.0
            value = 2.0 * w + total - 6.0 * q + keep * w2[x, at, :]
            if ends is None:
                cur[x, at, :] = value
            else:
                cur_ends[ends, at, :] = value
            prev[x, at, :] = keep * w
        if ends is None:
            send_cur(x).start()
        if ends in (None, 1, 2):
            send_prev(x).start()

    turn(1, 1)
    turn(cx - 2, 2)
    sweep(2, cx - 2, turn)
    turn(0, 0)
    turn(cx - 1, 3)
    sweep(1, cx - 1, lambda x: send_prev(x).wait())
    sweep(2, cx - 2, lambda x: send_cur(x).wait())


def adjoint_end_kernel(weights, u1, w2, w3, q2, c, inv, w1, q1):
    cx, side_cells = u1.shape[0], u1.shape[1]
    g0 = spread_weight(weights, 0, CHUNK)

    def first(x):
        for row, count in chunks(side_cells):
            at = pl.ds(row, count)
            value = backward(
                layer(q2, x), w2[x, at, :], w3[x, at, :], layer(inv, x), g0 * u1[x, at, :],
                x_sides(q2, x, cx), row, count, side_cells,
            )
            w1[x, at, :] = value
            q1[x, at, :] = c[x, at, :] * value

    first(0)
    sweep(1, cx - 1, first)
    first(cx - 1)


def patch_kernel(
    own, maps, wall_gain, wall_now, got_a, got_b, up, u, u1, u2, u3, u4, w4, w3, w2, w1, q2,
    sums, values, columns, totals,
):
    cx, side_cells = u.shape[0], u.shape[1]
    last = side_cells - 1
    ends = [end_layer(own_parity(), side, 0, cx) for side in range(2)]

    def field(x, at, lanes):
        k = (x, at, lanes)
        return (
            w4[k] * (u2[k] - u4[k])
            + w3[k] * (u1[k] - u3[k])
            + (w2[k] * (u[k] - u2[k]) + w1[k] * (up[k] - u1[k]))
        )

    everything = pl.ds(0, side_cells)
    low, high = pl.ds(0, LANES), pl.ds(side_cells - LANES, LANES)
    for x in range(cx):
        values[4 * x : 4 * x + 1, :] = field(x, pl.ds(0, 8), everything)[0:1]
        values[4 * x + 1 : 4 * x + 2, :] = field(x, pl.ds(last - 7, 8), everything)[7:8]
    base = 2 * cx
    tall = 2 * CHUNK
    spot = lax.broadcasted_iota(jnp.int32, (tall, LANES), 1)

    def gather(k, carry):
        at = pl.ds(pl.multiple_of(k * tall, tall), tall)
        total = jnp.zeros((tall, LANES), F32)
        for x in range(cx):
            for j, (lanes, lane_from) in enumerate(((low, 0), (high, LANES - 1))):
                tile = to_lane(field(x, at, lanes), 2 * x + j, lane_from)
                total = jnp.where(spot == 2 * x + j, tile, total)
        for side in range(2):
            for j, (lanes, lane_from) in enumerate(((low, 0), (high, LANES - 1))):
                place = base + 2 * side + j
                total = jnp.where(
                    spot == place, to_lane(q2[ends[side], at, lanes], place, lane_from), total
                )
        columns[at, :] = total
        return carry

    lax.fori_loop(0, side_cells // tall, gather, 0)
    rows = jnp.transpose(columns[...])
    for x in range(cx):
        values[4 * x + 2 : 4 * x + 4, :] = rows[2 * x : 2 * x + 2, :]
    for side in range(2):
        at, place = base + 2 * side, 4 * (cx + side)
        theirs = jnp.concatenate(
            [q2[ends[side], 0:1, :], q2[ends[side], last : last + 1, :], rows[at : at + 2, :]], axis=0
        )
        faces = slice(4 * side, 4 * side + 4)
        prior = (got_a, got_b)[side][2 * side_cells : 2 * side_cells + 4, :]
        values[place : place + 4, :] = theirs * (wall_gain[faces, :] * (prior - wall_now[faces, :]))
    all_maps, all_values = maps[...], values[...]

    def patch(k, carry):
        for m in range(GROUP // 8):
            block = []
            for j in range(8):
                picked = fold(jnp.where(all_maps == GROUP * k + 8 * m + j, all_values, 0.0))
                half = picked[:, :LANES]
                for first in range(LANES, side_cells, LANES):
                    half = half + picked[:, first : first + LANES]
                block.append(jnp.sum(half, axis=0, keepdims=True))
            total = jnp.sum(jnp.concatenate(block, axis=0), axis=1, keepdims=True)
            totals[pl.ds(pl.multiple_of(GROUP * k + 8 * m, 8), 8), :] = jnp.broadcast_to(
                total, (8, LANES)
            )
        return carry

    totals[totals.shape[0] - LANES :, :] = jnp.zeros((LANES, LANES), F32)
    lax.fori_loop(0, (totals.shape[0] - LANES) // GROUP, patch, 0)
    tall = -(-own // 8) * 8
    sub = lax.broadcasted_iota(jnp.int32, (tall, LANES), 0)
    diagonal = sub == lax.broadcasted_iota(jnp.int32, (tall, LANES), 1)

    def owner(d, carry):
        mine = jnp.where(diagonal, totals[pl.ds(d * own, tall), :], 0.0)
        sums[pl.ds(d, 1), :] = jnp.sum(mine, axis=0, keepdims=True)
        return carry

    lax.fori_loop(0, sums.shape[0], owner, 0, unroll=8)


def join_last_kernel(
    w1, q2, c, inv, s, got_a, got_b, b_a, b_b, cur_ends, cur_in, prev_in,
    cur_hbm, prev_hbm, delta, cur, prev, sems,
):
    cx, side_cells = w1.shape[0], w1.shape[1]
    copies = []

    def send(src, dst, x):
        copies.append(pltpu.make_async_copy(src, dst.at[x], sems.at[len(copies)]))
        copies[-1].start()

    for side, (got, b) in enumerate(((got_a, b_a), (got_b, b_b))):
        x0, x1 = (end_layer(own_parity(), side, k, cx) for k in range(2))
        e0, e1 = (end_layer(own_parity(), side, k, 4) for k in range(2))
        for row, count in chunks(side_cells):
            at = pl.ds(row, count)
            change = inv[x0, at, :] * got[at, :]
            prev[side, at, :] = (s[x0, at, :] - 1.0) * (w1[x0, at, :] + change)
            change = c[x0, at, :] * change
            delta[at, :] = change
            cur[2 * side + 1, at, :] = cur_ends[e1, at, :] + change
        send(prev.at[side], prev_hbm, x0)
        send(cur.at[2 * side + 1], cur_hbm, x1)
        for row, count in chunks(side_cells):
            at, below = pl.ds(row, count), pl.ds(side_cells + row, count)
            v, total = beside(flat(delta, 0), row, count, side_cells)
            cur[2 * side, at, :] = (
                cur_ends[e0, at, :]
                + 2.0 * (inv[x0, at, :] * got[at, :])
                + (total - 6.0 * v)
                + (got[below, :] + b[at, :] * q2[x0, at, :])
            )
        send(cur.at[2 * side], cur_hbm, x0)
    for copy in copies:
        copy.wait()


def call(kernel, ins, outs, scratch=(), aliases=None, name=None, us=2.0):
    kinds = {"v": in_vmem, "s": in_smem, "h": in_hbm}
    return pl.pallas_call(
        kernel,
        out_shape=[
            (pltpu.VMEM if kind == "v" else pltpu.HBM)(shape, *(dtype or [F32]))
            for kind, shape, *dtype in outs
        ],
        in_specs=[kinds[kind] for kind, _ in ins],
        out_specs=[kinds[kind] for kind, *_ in outs],
        scratch_shapes=list(scratch),
        input_output_aliases=aliases or {},
        compiler_params=pltpu.CompilerParams(vmem_limit_bytes=12 * 2**20),
        cost_estimate=pl.CostEstimate(flops=0, transcendentals=0, bytes_accessed=int(us * 3.0e6)),
        name=name,
    )(*[value for _, value in ins])


def on_device(u_prev, u_cur, courant_sq, patch_map, absorb, checkpoint, target_curve, tail_energy):
    cx, side = u_cur.shape[0], u_cur.shape[1]
    count = lax.axis_size("gx")
    patches = absorb.shape[0]
    own = patches // count
    all_cells = float(cx * count * side * side)
    field, plane = (cx, side, side), (side, side)
    double, tall = (2 * side, side), (side + 8, side)
    within = [(i, i ^ 1) for i in range(count)]
    across = [(i, i + 1) for i in range(1, count - 1, 2)]
    across = across + [(j, i) for i, j in across]

    def swap(a, b):
        a = lax.ppermute(a, "gx", within)
        return a, lax.ppermute(b, "gx", across)

    def deal(rows):
        return lax.all_to_all(rows, "gx", 0, 0, tiled=True)

    dma = pltpu.SemaphoreType.DMA
    ab = ("s", absorb)
    v = lambda *arrays: [("v", a) for a in arrays]
    small = (checkpoint.reshape(1, 1), target_curve.reshape(1, -1), tail_energy.reshape(1, 1))
    raw = [
        ("h", pltpu.with_memory_space_constraint(a, pltpu.HBM))
        for a in (patch_map, u_cur, u_prev, courant_sq)
    ]
    c_a, u_b, c_b = call(
        start_kernel,
        [raw[0], raw[1], raw[3]],
        [("v", (2 * side + 8, side)), ("v", plane), ("v", tall)],
        [VMEM((2, 4, side), jnp.int32), dma((3, 2))],
        name="edges",
        us=1.0,
    )
    near_a = lax.ppermute(c_a, "gx", within)
    near = (near_a, lax.ppermute(u_b, "gx", across))
    got_c = (near_a, lax.ppermute(c_b, "gx", across))
    u, up, c, s, inv, u1, params, own_maps = call(
        ahead_one_kernel,
        [ab] + v(*small) + raw,
        [("v", field)] * 6 + [("v", (8, LANES)), ("v", (cx, 4, side), jnp.int32)],
        [
            VMEM((4 * cx, side), jnp.int32),
            VMEM((4 * cx, side), F32),
            VMEM((LANES, side), F32),
            VMEM((side, LANES), F32),
            VMEM((side, LANES), F32),
            dma((4,)),
        ],
        name="forward_1",
        us=6.0,
    )
    u1, *edge_1 = call(
        join_one_kernel,
        v(c, inv, *near, u1),
        [("v", field)] + [("v", plane)] * 2,
        aliases={4: 0},
        name="edges_1",
        us=0.5,
    )
    u1h_a, u1h_b = near = swap(*edge_1)
    u2, *own_b, b_a, b_b, maps, wall_gain, wall_prior = call(
        ahead_two_kernel,
        [ab] + v(own_maps, u, up, c, inv, u1, *got_c),
        [("v", field)]
        + [("v", plane)] * 4
        + [("v", (4 * cx + 8, side), jnp.int32), ("v", (8, side)), ("v", (8, side))],
        [VMEM((side, LANES), F32), VMEM((side, LANES), F32), VMEM((LANES, side), F32)],
        name="forward_2",
        us=3.5,
    )
    got_b = (b_a, b_b)
    u2, *edge_2 = call(
        join_two_kernel,
        v(c, inv, *own_b, *near, wall_prior, u1, u2),
        [("v", field)] + [("v", (2 * side + 8, side))] * 2,
        aliases={8: 0},
        name="edges_2",
        us=0.8,
    )
    second = swap(*edge_2)
    u3, u4, energy, wall_now = call(
        ahead_again_kernel,
        v(u1, u2, c, inv, u1h_a, u1h_b),
        [("v", field)] * 2 + [("v", (STEPS, 8, side)), ("v", (8, side))],
        [VMEM((side, LANES), F32)],
        name="forward_3_4",
        us=5.5,
    )
    u3, u4, u3h_a, u3h_b, *edge_4, energy_rows = call(
        join_second_kernel,
        v(c, inv, energy, *edge_2, *own_b, *second, *got_b, u3, u4),
        [("v", field)] * 2 + [("v", plane)] * 2 + [("v", double)] * 2 + [("v", (count, LANES))],
        [VMEM(plane, F32)],
        aliases={11: 0, 12: 1},
        name="edges_3_4",
    )
    third = swap(*edge_4)
    w4, w3 = call(
        adjoint_free_kernel,
        v(u4, c, inv),
        [("v", field)] * 2,
        [VMEM(field, F32)],
        name="adjoint_3",
        us=2.6,
    )
    energy_rows, w4, w3 = lax.optimization_barrier((energy_rows, w4, w3))
    sums = deal(energy_rows)
    weights, w4, w3, w2, q2 = call(
        functools.partial(adjoint_kernel, all_cells),
        v(params, sums, u2, u3, c, inv, w4, w3),
        [("v", (8 * STEPS, side))] + [("v", field)] * 4,
        [VMEM(field, F32)],
        aliases={6: 1, 7: 2},
        name="adjoint_2",
        us=3.0,
    )
    w3, w2, q2, *edge_2 = call(
        join_third_kernel,
        v(weights, u1, c, inv, u3h_a, u3h_b, *edge_4, *third, *got_b, w3, w2, q2),
        [("v", field)] * 3 + [("v", double)] * 2,
        [VMEM(plane, F32), VMEM(plane, F32)],
        aliases={12: 0, 13: 1, 14: 2},
        name="edges_adjoint_3_2",
    )
    fourth = swap(*edge_2)
    w1, q1 = call(
        adjoint_end_kernel, v(weights, u1, w2, w3, q2, c, inv), [("v", field)] * 2, name="adjoint_1"
    )
    (partial,) = call(
        functools.partial(patch_kernel, own),
        v(maps, wall_gain, wall_now, *second, up, u, u1, u2, u3, u4, w4, w3, w2, w1, q2),
        [("v", (count, LANES))],
        [
            VMEM((4 * cx + 8, side), F32),
            VMEM((side, LANES), F32),
            VMEM((-(-patches // GROUP) * GROUP + LANES, LANES), F32),
        ],
        name="patch_sums",
    )
    cur, prev, cur_ends, mine = call(
        result_kernel,
        v(w1, q1, w2, s, deal(partial)),
        [("h", field)] * 2 + [("v", (4, side, side)), ("v", (1, LANES))],
        [VMEM(field, F32), VMEM(field, F32), dma((2, cx))],
        name="adjoint_0",
    )
    grad_absorb = mine[0, :own]
    cur, prev = call(
        join_last_kernel,
        v(w1, q2, c, inv, s, *fourth, *got_b, cur_ends) + [("h", cur), ("h", prev)],
        [("h", field)] * 2,
        [VMEM(plane, F32), VMEM((4, side, side), F32), VMEM((2, side, side), F32), dma((6,))],
        aliases={10: 0, 11: 1},
        name="edges_adjoint_1_0",
    )
    return prev, cur, grad_absorb


def solution(mesh):
    bricks = P(("groups", "gx"), None, None)
    return jax.shard_map(
        on_device,
        mesh=mesh,
        in_specs=(bricks, bricks, bricks, bricks, P("groups"), P("groups"), P("groups"), P("groups")),
        out_specs=(bricks, bricks, P(("groups", "gx"))),
        check_vma=False,
    )
```

time: 96.4 us -> 91 us (0.944)
  Pallas kernels: 33.8 us -> 30.6 us
  blocking collectives: 30.3 us -> 28.6 us
    pallas_call x12 -> x14, Pallas kernels: 33.8 us -> 30.6 us  [call(): pl.pallas_call(kernel, out_shape=[(pltpu.VMEM if kind == 'v' else pltpu.H...]
    all_to_all x2, blocking collectives: 30.3 us -> 28.6 us  [deal(): return lax.all_to_all(rows, 'gx', 0, 0, tiled=True)]
    ppermute x10 -> x11, starting transfers between devices: 29.1 us -> 28.7 us  [the longest x4 24.1 us: swap(): a = lax.ppermute(a, 'gx', within)]
  transfers between devices with their start and end apart: 10 -> 11, of which waited for: 0 -> 0; matrix products, arithmetic and copies ran while one was open for 1% -> 1% of each run, Pallas kernels for 26% -> 28%
where the time goes in v3:
time: 91 us; the launch traced here: 90.7 us
  Pallas kernels  30.6 us (34%)
  starting transfers between devices  28.7 us (32%)
  blocking collectives  28.6 us (31%)
  between operations  2.16 us (2%)
    pallas_call x14, Pallas kernels, call(): pl.pallas_call(kernel, out_shape=[(pltpu.VMEM if kind == 'v' else pltpu.H...  30.6 us
    all_to_all x2, blocking collectives, deal(): return lax.all_to_all(rows, 'gx', 0, 0, tiled=True)  28.6 us
    ppermute x4, starting transfers between devices, swap(): a = lax.ppermute(a, 'gx', within)  24.1 us
    ppermute x4, starting transfers between devices, swap(): return (a, lax.ppermute(b, 'gx', across))  2.72 us
  transfers between devices with their start and end apart: 11, of which 0 were waited for; matrix products, arithmetic and copies ran while one was open for 1% of the time, Pallas kernels for 28%

profile of v3, /device:TPU:0, one launch (start us, length us, event | category | flops | bytes accessed | tf_op | source)
XLA Modules:
  0.0 90.7 jit_solution(1043100437108561953)
XLA Ops:
  0.7 1.3 %edges.1 = (f32[520,256]{1,0:T(8,128)S(1)}, f32[256,256]{1,0:T(8,128)S(1)}, f32[264,256]{1,0:T(8,128)S(1)}) custom-call(s32[8,4,256]{2,1,0:T(4,128)} %map_hbm.3, f32[8,256,256]{2,1,0:T(8,128)} %u_hbm.3, f32[8,256,256]{2,1,0:T(8,128)} %c_hbm.3), custom_call_target="tpu_custom_call" | custom-call | bytes 3000000 | tf_op jit(solution)/shard_map/edges/pallas_call | solution.py:726
  1.9 0.5 collective-permute-start
  2.5 0.7 collective-permute-start.1
  3.1 0.7 collective-permute-start.2
  5.1 5.3 %forward_1.1 = (f32[8,256,256]{2,1,0:T(8,128)S(1)}, f32[8,256,256]{2,1,0:T(8,128)S(1)}, f32[8,256,256]{2,1,0:T(8,128)S(1)}, f32[8,256,256]{2,1,0:T(8,128)S(1)}, ...) custom-call(f32[160]{0:T(256)S(1)} %copy-done, ...), custom_call_target="tpu_custom_call" | custom-call | bytes 18000000 | tf_op jit(solution)/shard_map/forward_1/pallas_call | solution.py:726
  10.5 0.0 collective-permute-done.1.near_b
  10.5 0.0 collective-permute-done.near_a.got_a
  10.5 0.1 edges_1.1
  10.6 5.6 %collective-permute-start.3 = (f32[256,256]{1,0:T(8,128)S(1)}, f32[256,256]{1,0:T(8,128)S(1)}, u32[]{:S(2)}, u32[]{:S(2)}) collective-permute-start(f32[256,256]{1,0:T(8,128)S(1)} %get-tuple-element.75), channel_id=1, source_target_pairs={{0,1},{1,0},{2,3},{3,2},{4,5},{5,4},{6,7},{7,6},{8,9},{9,8},{10,11... | collective-permute-start | bytes 786440 | tf_op jit(solution)/shard_map/ppermute | solution.py:755
  16.2 0.7 collective-permute-start.4
  16.9 3.0 %forward_2.1 = (f32[8,256,256]{2,1,0:T(8,128)S(1)}, f32[256,256]{1,0:T(8,128)S(1)}, f32[256,256]{1,0:T(8,128)S(1)}, f32[256,256]{1,0:T(8,128)S(1)}, f32[256,256]...) custom-call(f32[160]{0:T(256)S(1)} %copy-done, ...), custom_call_target="tpu_custom_call" | custom-call | bytes 10500000 | tf_op jit(solution)/shard_map/forward_2/pallas_call | solution.py:726
  19.9 0.5 edges_2.1
  20.4 7.1 %collective-permute-start.5 = (f32[520,256]{1,0:T(8,128)S(1)}, f32[520,256]{1,0:T(8,128)S(1)}, u32[]{:S(2)}, u32[]{:S(2)}) collective-permute-start(f32[520,256]{1,0:T(8,128)S(1)} %get-tuple-element.81.edge_a), channel_id=1, source_target_pairs={{0,1},{1,0},{2,3},{3,2},{4,5},{5,4},{6,7},{7,6},{8,9},{9,8},{10,11... | collective-permute-start | bytes 1597448 | tf_op jit(solution)/shard_map/ppermute | solution.py:755
  27.5 0.7 collective-permute-start.6
  28.2 4.2 %forward_3_4.1 = (f32[8,256,256]{2,1,0:T(8,128)S(1)}, f32[8,256,256]{2,1,0:T(8,128)S(1)}, f32[4,8,256]{2,1,0:T(8,128)S(1)}, f32[8,256]{1,0:T(8,128)S(1)}) custom-call(f32[8,256,256]{2,1,0:T(8,128)S(1)} %get-tuple-element.68.u1, f32[8,256,256]{2,1,0:T(8,128)S(1)} %get-tuple-element.79.u2, f32[8,256,256]{2,1,0:T(8,128)S(1)} %get-tuple-element.63.c, ...), custom_call_target="tpu_custom_call" | custom-call | bytes 16500000 | tf_op jit(solution)/shard_map/forward_3_4/pallas_call | solution.py:726
  32.4 0.0 collective-permute-done.5.got_a
  32.4 1.1 %edges_3_4.1 = (f32[8,256,256]{2,1,0:T(8,128)S(1)}, f32[8,256,256]{2,1,0:T(8,128)S(1)}, f32[256,256]{1,0:T(8,128)S(1)}, f32[256,256]{1,0:T(8,128)S(1)}, f32[512,...) custom-call(f32[8,256,256]{2,1,0:T(8,128)S(1)} %get-tuple-element.63, ...), custom_call_target="tpu_custom_call", output_to_operand_aliasing={{0}: (11, {}), {1}: (12, {})} | custom-call | bytes 6000000 | tf_op jit(solution)/shard_map/edges_3_4/pallas_call | solution.py:726
  33.6 11.4 %collective-permute-start.7 = (f32[512,256]{1,0:T(8,128)S(1)}, f32[512,256]{1,0:T(8,128)S(1)}, u32[]{:S(2)}, u32[]{:S(2)}) collective-permute-start(f32[512,256]{1,0:T(8,128)S(1)} %get-tuple-element.98.own_a), channel_id=1, source_target_pairs={{0,1},{1,0},{2,3},{3,2},{4,5},{5,4},{6,7},{7,6},{8,9},{9,8},{10,11... | collective-permute-start | bytes 1572872 | tf_op jit(solution)/shard_map/ppermute | solution.py:755
  45.0 0.7 collective-permute-start.8
  45.7 2.1 %adjoint_3.1 = (f32[8,256,256]{2,1,0:T(8,128)S(1)}, f32[8,256,256]{2,1,0:T(8,128)S(1)}) custom-call(f32[8,256,256]{2,1,0:T(8,128)S(1)} %get-tuple-element.88.u4, f32[8,256,256]{2,1,0:T(8,128)S(1)} %get-tuple-element.63.c, f32[8,256,256]{2,1,0:T(8,128)S(1)} %get-tuple-element.64.inv), custom_call_target="tpu_custom_call" | custom-call | bytes 7800000 | tf_op jit(solution)/shard_map/adjoint_3/pallas_call | solution.py:726
  47.8 14.8 %all_to_all.22 = f32[16,1,128]{2,1,0:T(1,128)S(1)} all-to-all(f32[16,1,128]{2,1,0:T(1,128)S(1)} %bitcast.18), channel_id=1, replica_groups=mesh['groups'=2,'gx'=16] {'gx'}, dimensions={0} | all-to-all | bytes 16384 | tf_op jit(solution)/shard_map/all_to_all | solution.py:759
  62.6 2.8 %adjoint_2.1 = (f32[32,256]{1,0:T(8,128)S(1)}, f32[8,256,256]{2,1,0:T(8,128)S(1)}, f32[8,256,256]{2,1,0:T(8,128)S(1)}, f32[8,256,256]{2,1,0:T(8,128)S(1)}, f32[8,256,256]{2,1,0:T(8,128)S(1)}) custom-call(f32[8,128]{1,0:T(8,128)S(1)} %get-tuple-element.62.params, f32[16,128]{1,0:T(8,128)S(1)} %bitcast.16, ...), custom_call_target="tpu_custom_call", output_to_operand_aliasing={{1}: (6, {}), {2}: (7, {})} | custom-call | bytes 9000000 | tf_op jit(solution)/shard_map/adjoint_2/pallas_call | solution.py:726
  65.3 0.0 collective-permute-done.7.got_a
  65.4 1.2 %edges_adjoint_3_2.1 = (f32[8,256,256]{2,1,0:T(8,128)S(1)}, f32[8,256,256]{2,1,0:T(8,128)S(1)}, f32[8,256,256]{2,1,0:T(8,128)S(1)}, f32[512,256]{1,0:T(8,128)S(1)}, f32[512,256]{1,0:T(8,128)S(1)}) custom-call(f32[32,256]{1,0:T(8,128)S(1)} %get-tuple-element.95.weights, ...), custom_call_target="tpu_custom_call", output_to_operand_aliasing={{0}: (12, {}), {1}: (13, {}), {2}: (14, {})} | custom-call | bytes 6000000 | tf_op jit(solution)/shard_map/edges_adjoint_3_2/pallas_call | solution.py:726
  66.6 0.1 collective-permute-start.9
  66.6 0.7 collective-permute-start.10
  67.3 2.2 %adjoint_1.1 = (f32[8,256,256]{2,1,0:T(8,128)S(1)}, f32[8,256,256]{2,1,0:T(8,128)S(1)}) custom-call(f32[32,256]{1,0:T(8,128)S(1)} %get-tuple-element.95.weights, f32[8,256,256]{2,1,0:T(8,128)S(1)} %get-tuple-element.68.u1, f32[8,256,256]{2,1,0:T(8,128)S(1)} %get-tuple-element.103.w2, f32[8,256,256]{2,1,0:T(8,128)S(1)} %get-tuple-element.104.w3, ...), custom_call_target="tpu_custom_call" | custom-call | bytes 6000000 | tf_op jit(solution)/shard_map/adjoint_1/pallas_call | solution.py:726
  69.5 3.0 %patch_sums.1 = f32[16,128]{1,0:T(8,128)S(1)} custom-call(s32[40,256]{1,0:T(8,128)S(1)} %get-tuple-element.111.maps, f32[8,256]{1,0:T(8,128)S(1)} %get-tuple-element.112.wall_gain, f32[8,256]{1,0:T(8,128)S(1)} %get-tuple-element.113.wall_now, f32[520,256]{1,0:T(8,128)S(1)} %collective-permute-done.5.got_a, f32[520,256]{1,0:T(8,128)S(1)} %collective-permute-done.6.got_b, ...), custom_call_target="tpu_custom_call" | custom-call | bytes 6000000 | tf_op jit(solution)/shard_map/patch_sums/pallas_call | solution.py:726
  72.6 13.9 %all_to_all.23 = f32[16,1,128]{2,1,0:T(1,128)S(1)} all-to-all(f32[16,1,128]{2,1,0:T(1,128)S(1)} %bitcast.15), channel_id=1, replica_groups=mesh['groups'=2,'gx'=16] {'gx'}, dimensions={0} | all-to-all | bytes 16384 | tf_op jit(solution)/shard_map/all_to_all | solution.py:759
  86.4 2.3 %adjoint_0.1 = (f32[8,256,256]{2,1,0:T(8,128)}, f32[8,256,256]{2,1,0:T(8,128)}, f32[4,256,256]{2,1,0:T(8,128)S(1)}, f32[1,128]{1,0:T(1,128)S(1)}) custom-call(f32[8,256,256]{2,1,0:T(8,128)S(1)} %get-tuple-element.106.w1, f32[8,256,256]{2,1,0:T(8,128)S(1)} %get-tuple-element.110.q1, f32[8,256,256]{2,1,0:T(8,128)S(1)} %get-tuple-element.103.w2, ...), custom_call_target="tpu_custom_call" | custom-call | bytes 6000000 | tf_op jit(solution)/shard_map/adjoint_0/pallas_call | solution.py:726
  88.8 0.5 slice_bitcast_fusion
  89.3 1.4 %edges_adjoint_1_0.1 = (f32[8,256,256]{2,1,0:T(8,128)}, f32[8,256,256]{2,1,0:T(8,128)}) custom-call(f32[8,256,256]{2,1,0:T(8,128)S(1)} %get-tuple-element.106.w1, f32[8,256,256]{2,1,0:T(8,128)S(1)} %get-tuple-element.105.q2, f32[8,256,256]{2,1,0:T(8,128)S(1)} %get-tuple-element.63.c, ...), custom_call_target="tpu_custom_call", output_to_operand_aliasing={{0}: (10, {}), {1}: (11, {})} | custom-call | bytes 6000000 | tf_op jit(solution)/shard_map/edges_adjoint_1_0/pallas_call | solution.py:726
  (11 shorter events, 0.0 us)
Async XLA Ops:
  0.6 4.5 %copy-start = (f32[160]{0:T(256)S(1)}, f32[160]{0:T(256)}, u32[]{:S(2)}) copy-start(f32[160]{0:T(256)} %absorb_ref.3) | copy-start | bytes 1924
  0.6 4.5 %copy-start.1 = (f32[64]{0:T(128)S(1)}, f32[64]{0:T(128)}, u32[]{:S(2)}) copy-start(f32[64]{0:T(128)} %param.14) | copy-start | bytes 772
  1.9 8.6 %collective-permute-start = (f32[520,256]{1,0:T(8,128)S(1)}, f32[520,256]{1,0:T(8,128)S(1)}, u32[]{:S(2)}, u32[]{:S(2)}) collective-permute-start(f32[520,256]{1,0:T(8,128)S(1)} %get-tuple-element.65), channel_id=1, source_target_pairs={{0,1},{1,0},{2,3},{3,2},{4,5},{5,4},{6,7},{7,6},{8,9},{9,8},{10,11... | collective-permute-start | bytes 1597448 | tf_op jit(solution)/shard_map/ppermute | solution.py:777
  2.5 8.0 %collective-permute-start.1 = (f32[256,256]{1,0:T(8,128)S(1)}, f32[256,256]{1,0:T(8,128)S(1)}, u32[]{:S(2)}, u32[]{:S(2)}) collective-permute-start(f32[256,256]{1,0:T(8,128)S(1)} %get-tuple-element.66), channel_id=1, source_target_pairs={{1,2},{3,4},{5,6},{7,8},{9,10},{11,12},{13,14},{2,1},{4,3},{6,5},{... | collective-permute-start | bytes 786440 | tf_op jit(solution)/shard_map/ppermute | solution.py:778
  3.1 13.8 %collective-permute-start.2 = (f32[264,256]{1,0:T(8,128)S(1)}, f32[264,256]{1,0:T(8,128)S(1)}, u32[]{:S(2)}, u32[]{:S(2)}) collective-permute-start(f32[264,256]{1,0:T(8,128)S(1)} %get-tuple-element.72), channel_id=1, source_target_pairs={{1,2},{3,4},{5,6},{7,8},{9,10},{11,12},{13,14},{2,1},{4,3},{6,5},{... | collective-permute-start | bytes 811016 | tf_op jit(solution)/shard_map/ppermute | solution.py:779
  10.6 9.3 %collective-permute-start.3 = (f32[256,256]{1,0:T(8,128)S(1)}, f32[256,256]{1,0:T(8,128)S(1)}, u32[]{:S(2)}, u32[]{:S(2)}) collective-permute-start(f32[256,256]{1,0:T(8,128)S(1)} %get-tuple-element.75), channel_id=1, source_target_pairs={{0,1},{1,0},{2,3},{3,2},{4,5},{5,4},{6,7},{7,6},{8,9},{9,8},{10,11... | collective-permute-start | bytes 786440 | tf_op jit(solution)/shard_map/ppermute | solution.py:755
  16.2 3.7 %collective-permute-start.4 = (f32[256,256]{1,0:T(8,128)S(1)}, f32[256,256]{1,0:T(8,128)S(1)}, u32[]{:S(2)}, u32[]{:S(2)}) collective-permute-start(f32[256,256]{1,0:T(8,128)S(1)} %get-tuple-element.76), channel_id=1, source_target_pairs={{1,2},{3,4},{5,6},{7,8},{9,10},{11,12},{13,14},{2,1},{4,3},{6,5},{... | collective-permute-start | bytes 786440 | tf_op jit(solution)/shard_map/ppermute | solution.py:756
  20.4 12.0 %collective-permute-start.5 = (f32[520,256]{1,0:T(8,128)S(1)}, f32[520,256]{1,0:T(8,128)S(1)}, u32[]{:S(2)}, u32[]{:S(2)}) collective-permute-start(f32[520,256]{1,0:T(8,128)S(1)} %get-tuple-element.81.edge_a), channel_id=1, source_target_pairs={{0,1},{1,0},{2,3},{3,2},{4,5},{5,4},{6,7},{7,6},{8,9},{9,8},{10,11... | collective-permute-start | bytes 1597448 | tf_op jit(solution)/shard_map/ppermute | solution.py:755
  27.5 4.9 %collective-permute-start.6 = (f32[520,256]{1,0:T(8,128)S(1)}, f32[520,256]{1,0:T(8,128)S(1)}, u32[]{:S(2)}, u32[]{:S(2)}) collective-permute-start(f32[520,256]{1,0:T(8,128)S(1)} %get-tuple-element.82.edge_b), channel_id=1, source_target_pairs={{1,2},{3,4},{5,6},{7,8},{9,10},{11,12},{13,14},{2,1},{4,3},{6,5},{... | collective-permute-start | bytes 1597448 | tf_op jit(solution)/shard_map/ppermute | solution.py:756
  33.6 31.7 %collective-permute-start.7 = (f32[512,256]{1,0:T(8,128)S(1)}, f32[512,256]{1,0:T(8,128)S(1)}, u32[]{:S(2)}, u32[]{:S(2)}) collective-permute-start(f32[512,256]{1,0:T(8,128)S(1)} %get-tuple-element.98.own_a), channel_id=1, source_target_pairs={{0,1},{1,0},{2,3},{3,2},{4,5},{5,4},{6,7},{7,6},{8,9},{9,8},{10,11... | collective-permute-start | bytes 1572872 | tf_op jit(solution)/shard_map/ppermute | solution.py:755
  45.0 20.3 %collective-permute-start.8 = (f32[512,256]{1,0:T(8,128)S(1)}, f32[512,256]{1,0:T(8,128)S(1)}, u32[]{:S(2)}, u32[]{:S(2)}) collective-permute-start(f32[512,256]{1,0:T(8,128)S(1)} %get-tuple-element.99.own_b), channel_id=1, source_target_pairs={{1,2},{3,4},{5,6},{7,8},{9,10},{11,12},{13,14},{2,1},{4,3},{6,5},{... | collective-permute-start | bytes 1572872 | tf_op jit(solution)/shard_map/ppermute | solution.py:756
  66.6 22.8 %collective-permute-start.9 = (f32[512,256]{1,0:T(8,128)S(1)}, f32[512,256]{1,0:T(8,128)S(1)}, u32[]{:S(2)}, u32[]{:S(2)}) collective-permute-start(f32[512,256]{1,0:T(8,128)S(1)} %get-tuple-element.108), channel_id=1, source_target_pairs={{0,1},{1,0},{2,3},{3,2},{4,5},{5,4},{6,7},{7,6},{8,9},{9,8},{10,11... | collective-permute-start | bytes 1572872 | tf_op jit(solution)/shard_map/ppermute | solution.py:755
  66.6 22.7 %collective-permute-start.10 = (f32[512,256]{1,0:T(8,128)S(1)}, f32[512,256]{1,0:T(8,128)S(1)}, u32[]{:S(2)}, u32[]{:S(2)}) collective-permute-start(f32[512,256]{1,0:T(8,128)S(1)} %get-tuple-element.109), channel_id=1, source_target_pairs={{1,2},{3,4},{5,6},{7,8},{9,10},{11,12},{13,14},{2,1},{4,3},{6,5},{... | collective-permute-start | bytes 1572872 | tf_op jit(solution)/shard_map/ppermute | solution.py:756

commit v4 on v3

--- a/solution.py
+++ b/solution.py
@@ -11,7 +11,7 @@
 PATCH_CELLS = 819
 CHUNK = 16
 LANES = 128
-GROUP = 80
+GROUP = 160
 F32 = jnp.float32
 VMEM = pltpu.VMEM
 in_vmem = pl.BlockSpec(memory_space=pltpu.VMEM)
@@ -321,24 +321,21 @@
     second(cx - 1)
 
 
-def join_two_kernel(
-    c, inv, own_a, own_b, near_a, near_b, wall_prior, u1, u2_in, u2, pay_a, pay_b
-):
+def join_two_kernel(side, c, inv, own, near, wall_prior, u1, u2_in, u2, pay):
     cx, side_cells = c.shape[0], c.shape[1]
-    for side, (own, near, pay) in enumerate(((own_a, near_a, pay_a), (own_b, near_b, pay_b))):
-        x0, x1 = (end_layer(own_parity(), side, k, cx) for k in range(2))
-        for row, count in chunks(side_cells):
-            at = pl.ds(row, count)
-            value = u2[x0, at, :] + own[at, :] * near[at, :]
-            u2[x0, at, :] = value
-            pay[at, :] = value
-        pay[2 * side_cells : 2 * side_cells + 4, :] = wall_prior[4 * side : 4 * side + 4, :]
-        pay[2 * side_cells + 4 : 2 * side_cells + 8, :] = jnp.zeros((4, side_cells), F32)
-        for row, count in chunks(side_cells):
-            pay[pl.ds(side_cells + row, count), :] = forward(
-                flat(pay, 0), layer(u1, x0), layer(c, x0), layer(inv, x0), [layer(u2, x1)],
-                row, count, side_cells,
-            )
+    x0, x1 = (end_layer(own_parity(), side, k, cx) for k in range(2))
+    for row, count in chunks(side_cells):
+        at = pl.ds(row, count)
+        value = u2[x0, at, :] + own[at, :] * near[at, :]
+        u2[x0, at, :] = value
+        pay[at, :] = value
+    pay[2 * side_cells : 2 * side_cells + 4, :] = wall_prior[4 * side : 4 * side + 4, :]
+    pay[2 * side_cells + 4 : 2 * side_cells + 8, :] = jnp.zeros((4, side_cells), F32)
+    for row, count in chunks(side_cells):
+        pay[pl.ds(side_cells + row, count), :] = forward(
+            flat(pay, 0), layer(u1, x0), layer(c, x0), layer(inv, x0), [layer(u2, x1)],
+            row, count, side_cells,
+        )
 
 
 def join_forward(x0, x1, edge, mid, last, c, inv, got_now, got_part, got_b, b, halo, delta, side_cells):
@@ -402,40 +399,40 @@
 
 
 def join_second_kernel(
-    c, inv, energy, edge_a, edge_b, own_a, own_b, got_a, got_b, b_a, b_b, u3_in, u4_in,
-    u3, u4, halo_a, halo_b, pay_a, pay_b, energy_rows, delta,
+    side, c, inv, energy_in, edge, own, got, gb, u3_in, u4_in, u3, u4, halo, pay, energy, delta
 ):
     cx, side_cells = c.shape[0], c.shape[1]
-    third = energy[2]
-    fourth = energy[3]
-    for side, (edge, own, got, gb, halo, pay) in enumerate(
-        ((edge_a, own_a, got_a, b_a, halo_a, pay_a), (edge_b, own_b, got_b, b_b, halo_b, pay_b))
-    ):
-        x0, x1 = (end_layer(own_parity(), side, k, cx) for k in range(2))
-        b = flat(own, 0)
-        join_forward(
-            x0, x1, flat(edge, 0), u3, u4, c, inv, flat(got, 0), flat(got, side_cells),
-            flat(gb, 0), b, halo, delta, side_cells,
-        )
-        for row, count in chunks(side_cells):
-            at = pl.ds(row, count)
-            value, other = u4[x0, at, :], u4[x1, at, :]
-            pay[at, :] = 2.0 * b(row, count) * value
-            third = third + fold(u3[x0, at, :] ** 2)
-            fourth = fourth + fold(value * value + other * other)
-        for row, count in chunks(side_cells):
-            at = pl.ds(row, count)
-            q, total = beside(flat(pay, 0), row, count, side_cells)
-            total = total + 2.0 * (c[x1, at, :] * inv[x1, at, :]) * u4[x1, at, :]
-            pay[pl.ds(side_cells + row, count), :] = b(row, count) * (
-                4.0 * (inv[x0, at, :] * u4[x0, at, :]) + total - 6.0 * q
-            )
-    lane = lax.broadcasted_iota(jnp.int32, energy_rows.shape, 1)
-    rows = jnp.zeros(energy_rows.shape, F32)
-    for n, part in enumerate((energy[0], energy[1], third, fourth)):
+    third, fourth = energy_in[2], energy_in[3]
+    x0, x1 = (end_layer(own_parity(), side, k, cx) for k in range(2))
+    b = flat(own, 0)
+    join_forward(
+        x0, x1, flat(edge, 0), u3, u4, c, inv, flat(got, 0), flat(got, side_cells),
+        flat(gb, 0), b, halo, delta, side_cells,
+    )
+    for row, count in chunks(side_cells):
+        at = pl.ds(row, count)
+        value, other = u4[x0, at, :], u4[x1, at, :]
+        pay[at, :] = 2.0 * b(row, count) * value
+        third = third + fold(u3[x0, at, :] ** 2)
+        fourth = fourth + fold(value * value + other * other)
+    for row, count in chunks(side_cells):
+        at = pl.ds(row, count)
+        q, total = beside(flat(pay, 0), row, count, side_cells)
+        total = total + 2.0 * (c[x1, at, :] * inv[x1, at, :]) * u4[x1, at, :]
+        pay[pl.ds(side_cells + row, count), :] = b(row, count) * (
+            4.0 * (inv[x0, at, :] * u4[x0, at, :]) + total - 6.0 * q
+        )
+    parts = (energy_in[0], energy_in[1], third, fourth)
+    if side == 0:
+        for n, part in enumerate(parts):
+            energy[n] = part
+        return
+    lane = lax.broadcasted_iota(jnp.int32, energy.shape, 1)
+    rows = jnp.zeros(energy.shape, F32)
+    for n, part in enumerate(parts):
         total = jnp.sum(jnp.sum(part, axis=0, keepdims=True), axis=1, keepdims=True)
         rows = jnp.where(lane == n, total, rows)
-    energy_rows[...] = rows
+    energy[...] = rows
 
 
 def adjoint_free_kernel(u4, c, inv, w4, w3, q4):
@@ -544,44 +541,26 @@
             )
 
 
-def result_kernel(w1, q1, w2, s, dealt, cur_hbm, prev_hbm, cur_ends, mine, cur, prev, sems):
+def result_kernel(w1, q1, w2, s, dealt, cur, mine):
     cx, side_cells = w1.shape[0], w1.shape[1]
     mine[...] = jnp.sum(dealt[...], axis=0, keepdims=True) / float(PATCH_CELLS)
 
-    def send_cur(x):
-        return pltpu.make_async_copy(cur.at[x], cur_hbm.at[x], sems.at[0, x])
-
-    def send_prev(x):
-        return pltpu.make_async_copy(prev.at[x], prev_hbm.at[x], sems.at[1, x])
-
-    def turn(x, ends=None):
+    def turn(x):
         for row, count in chunks(side_cells):
             at = pl.ds(row, count)
             q, total = beside(layer(q1, x), row, count, side_cells)
             for other in x_sides(q1, x, cx):
                 total = total + other(row, count)
-            w, keep = w1[x, at, :], s[x, at, :] - 1.0
-            value = 2.0 * w + total - 6.0 * q + keep * w2[x, at, :]
-            if ends is None:
-                cur[x, at, :] = value
-            else:
-                cur_ends[ends, at, :] = value
-            prev[x, at, :] = keep * w
-        if ends is None:
-            send_cur(x).start()
-        if ends in (None, 1, 2):
-            send_prev(x).start()
-
-    turn(1, 1)
-    turn(cx - 2, 2)
-    sweep(2, cx - 2, turn)
-    turn(0, 0)
-    turn(cx - 1, 3)
-    sweep(1, cx - 1, lambda x: send_prev(x).wait())
-    sweep(2, cx - 2, lambda x: send_cur(x).wait())
-
-
-def adjoint_end_kernel(weights, u1, w2, w3, q2, c, inv, w1, q1):
+            cur[x, at, :] = (
+                2.0 * w1[x, at, :] + total - 6.0 * q + (s[x, at, :] - 1.0) * w2[x, at, :]
+            )
+
+    turn(0)
+    sweep(1, cx - 1, turn)
+    turn(cx - 1)
+
+
+def adjoint_end_kernel(weights, u1, w2, w3, q2, c, inv, s, w1, q1, prev):
     cx, side_cells = u1.shape[0], u1.shape[1]
     g0 = spread_weight(weights, 0, CHUNK)
 
@@ -594,6 +573,7 @@
             )
             w1[x, at, :] = value
             q1[x, at, :] = c[x, at, :] * value
+            prev[x, at, :] = (s[x, at, :] - 1.0) * value
 
     first(0)
     sweep(1, cx - 1, first)
@@ -601,12 +581,15 @@
 
 
 def patch_kernel(
-    own, maps, wall_gain, wall_now, got_a, got_b, up, u, u1, u2, u3, u4, w4, w3, w2, w1, q2,
-    sums, values, columns, totals,
+    own, maps, wall_gain, wall_now, got_a, got_b, up, u, u1, u2, u3, u4, w4, w3, w2, w1, q2, prev,
+    sums, prev_hbm, values, columns, totals, sem,
 ):
     cx, side_cells = u.shape[0], u.shape[1]
     last = side_cells - 1
     ends = [end_layer(own_parity(), side, 0, cx) for side in range(2)]
+    inner = pl.ds(1, cx - 2)
+    leave = pltpu.make_async_copy(prev.at[inner], prev_hbm.at[inner], sem)
+    leave.start()
 
     def field(x, at, lanes):
         k = (x, at, lanes)
@@ -682,41 +665,41 @@
         return carry
 
     lax.fori_loop(0, sums.shape[0], owner, 0, unroll=8)
+    leave.wait()
 
 
 def join_last_kernel(
-    w1, q2, c, inv, s, got_a, got_b, b_a, b_b, cur_ends, cur_in, prev_in,
-    cur_hbm, prev_hbm, delta, cur, prev, sems,
+    w1, q2, c, inv, s, got_a, got_b, b_a, b_b, cur, prev_in, cur_hbm, prev_hbm, delta, prev, sems
 ):
     cx, side_cells = w1.shape[0], w1.shape[1]
     copies = []
 
-    def send(src, dst, x):
-        copies.append(pltpu.make_async_copy(src, dst.at[x], sems.at[len(copies)]))
+    def send(src, dst):
+        copies.append(pltpu.make_async_copy(src, dst, sems.at[len(copies)]))
         copies[-1].start()
 
+    inner = pl.ds(2, cx - 4)
+    send(cur.at[inner], cur_hbm.at[inner])
     for side, (got, b) in enumerate(((got_a, b_a), (got_b, b_b))):
         x0, x1 = (end_layer(own_parity(), side, k, cx) for k in range(2))
-        e0, e1 = (end_layer(own_parity(), side, k, 4) for k in range(2))
         for row, count in chunks(side_cells):
             at = pl.ds(row, count)
             change = inv[x0, at, :] * got[at, :]
             prev[side, at, :] = (s[x0, at, :] - 1.0) * (w1[x0, at, :] + change)
             change = c[x0, at, :] * change
             delta[at, :] = change
-            cur[2 * side + 1, at, :] = cur_ends[e1, at, :] + change
-        send(prev.at[side], prev_hbm, x0)
-        send(cur.at[2 * side + 1], cur_hbm, x1)
+            cur[x1, at, :] += change
+        send(prev.at[side], prev_hbm.at[x0])
+        send(cur.at[x1], cur_hbm.at[x1])
         for row, count in chunks(side_cells):
             at, below = pl.ds(row, count), pl.ds(side_cells + row, count)
             v, total = beside(flat(delta, 0), row, count, side_cells)
-            cur[2 * side, at, :] = (
-                cur_ends[e0, at, :]
-                + 2.0 * (inv[x0, at, :] * got[at, :])
+            cur[x0, at, :] += (
+                2.0 * (inv[x0, at, :] * got[at, :])
                 + (total - 6.0 * v)
                 + (got[below, :] + b[at, :] * q2[x0, at, :])
             )
-        send(cur.at[2 * side], cur_hbm, x0)
+        send(cur.at[x0], cur_hbm.at[x0])
     for copy in copies:
         copy.wait()
 
@@ -812,14 +795,17 @@
         us=3.5,
     )
     got_b = (b_a, b_b)
-    u2, *edge_2 = call(
-        join_two_kernel,
-        v(c, inv, *own_b, *near, wall_prior, u1, u2),
-        [("v", field)] + [("v", (2 * side + 8, side))] * 2,
-        aliases={8: 0},
-        name="edges_2",
-        us=0.8,
-    )
+    edge_2 = []
+    for k in range(2):
+        u2, pay = call(
+            functools.partial(join_two_kernel, k),
+            v(c, inv, own_b[k], near[k], wall_prior, u1, u2),
+            [("v", field), ("v", (2 * side + 8, side))],
+            aliases={6: 0},
+            name="edges_2",
+            us=0.4,
+        )
+        edge_2.append(pay)
     second = swap(*edge_2)
     u3, u4, energy, wall_now = call(
         ahead_again_kernel,
@@ -829,14 +815,21 @@
         name="forward_3_4",
         us=5.5,
     )
-    u3, u4, u3h_a, u3h_b, *edge_4, energy_rows = call(
-        join_second_kernel,
-        v(c, inv, energy, *edge_2, *own_b, *second, *got_b, u3, u4),
-        [("v", field)] * 2 + [("v", plane)] * 2 + [("v", double)] * 2 + [("v", (count, LANES))],
-        [VMEM(plane, F32)],
-        aliases={11: 0, 12: 1},
-        name="edges_3_4",
-    )
+    edge_4, u3h = [], []
+    for k in range(2):
+        u3, u4, halo, pay, energy = call(
+            functools.partial(join_second_kernel, k),
+            v(c, inv, energy, edge_2[k], own_b[k], second[k], got_b[k], u3, u4),
+            [("v", field)] * 2
+            + [("v", plane), ("v", double)]
+            + [("v", (count, LANES) if k else (STEPS, 8, side))],
+            [VMEM(plane, F32)],
+            aliases={7: 0, 8: 1},
+            name="edges_3_4",
+            us=0.6,
+        )
+        edge_4.append(pay)
+        u3h.append(halo)
     third = swap(*edge_4)
     w4, w3 = call(
         adjoint_free_kernel,
@@ -846,8 +839,8 @@
         name="adjoint_3",
         us=2.6,
     )
-    energy_rows, w4, w3 = lax.optimization_barrier((energy_rows, w4, w3))
-    sums = deal(energy_rows)
+    energy, w4, w3 = lax.optimization_barrier((energy, w4, w3))
+    sums = deal(energy)
     weights, w4, w3, w2, q2 = call(
         functools.partial(adjoint_kernel, all_cells),
         v(params, sums, u2, u3, c, inv, w4, w3),
@@ -859,41 +852,44 @@
     )
     w3, w2, q2, *edge_2 = call(
         join_third_kernel,
-        v(weights, u1, c, inv, u3h_a, u3h_b, *edge_4, *third, *got_b, w3, w2, q2),
+        v(weights, u1, c, inv, *u3h, *edge_4, *third, *got_b, w3, w2, q2),
         [("v", field)] * 3 + [("v", double)] * 2,
         [VMEM(plane, F32), VMEM(plane, F32)],
         aliases={12: 0, 13: 1, 14: 2},
         name="edges_adjoint_3_2",
     )
     fourth = swap(*edge_2)
-    w1, q1 = call(
-        adjoint_end_kernel, v(weights, u1, w2, w3, q2, c, inv), [("v", field)] * 2, name="adjoint_1"
-    )
-    (partial,) = call(
+    w1, q1, prev = call(
+        adjoint_end_kernel,
+        v(weights, u1, w2, w3, q2, c, inv, s),
+        [("v", field)] * 3,
+        name="adjoint_1",
+    )
+    partial, prev = call(
         functools.partial(patch_kernel, own),
-        v(maps, wall_gain, wall_now, *second, up, u, u1, u2, u3, u4, w4, w3, w2, w1, q2),
-        [("v", (count, LANES))],
+        v(maps, wall_gain, wall_now, *second, up, u, u1, u2, u3, u4, w4, w3, w2, w1, q2, prev),
+        [("v", (count, LANES)), ("h", field)],
         [
             VMEM((4 * cx + 8, side), F32),
             VMEM((side, LANES), F32),
             VMEM((-(-patches // GROUP) * GROUP + LANES, LANES), F32),
+            dma,
         ],
         name="patch_sums",
     )
-    cur, prev, cur_ends, mine = call(
+    cur, mine = call(
         result_kernel,
         v(w1, q1, w2, s, deal(partial)),
-        [("h", field)] * 2 + [("v", (4, side, side)), ("v", (1, LANES))],
-        [VMEM(field, F32), VMEM(field, F32), dma((2, cx))],
+        [("v", field), ("v", (1, LANES))],
         name="adjoint_0",
     )
     grad_absorb = mine[0, :own]
     cur, prev = call(
         join_last_kernel,
-        v(w1, q2, c, inv, s, *fourth, *got_b, cur_ends) + [("h", cur), ("h", prev)],
+        v(w1, q2, c, inv, s, *fourth, *got_b, cur) + [("h", prev)],
         [("h", field)] * 2,
-        [VMEM(plane, F32), VMEM((4, side, side), F32), VMEM((2, side, side), F32), dma((6,))],
-        aliases={10: 0, 11: 1},
+        [VMEM(plane, F32), VMEM((2, side, side), F32), dma((7,))],
+        aliases={10: 1},
         name="edges_adjoint_1_0",
     )
     return prev, cur, grad_absorb

time: 91 us -> 85 us (0.934)
  blocking collectives: 28.6 us -> 21.3 us
  starting transfers between devices: 28.7 us -> 31.3 us
  Pallas kernels: 30.6 us -> 29.3 us
    all_to_all x2, blocking collectives: 28.6 us -> 21.3 us  [deal(): return lax.all_to_all(rows, 'gx', 0, 0, tiled=True)]
    ppermute x4, starting transfers between devices: 24.1 us -> 26.7 us  [swap(): a = lax.ppermute(a, 'gx', within)]
    pallas_call x14 -> x16, Pallas kernels: 30.6 us -> 29.3 us  [call(): pl.pallas_call(kernel, out_shape=[(pltpu.VMEM if kind == 'v' else pltpu.H...]
  transfers between devices with their start and end apart: 11 -> 11, of which waited for: 0 -> 0; matrix products, arithmetic and copies ran while one was open for 1% -> 1% of each run, Pallas kernels for 28% -> 29%
where the time goes in v4:
time: 85 us; the launch traced here: 84.7 us
  starting transfers between devices  31.3 us (37%)
  Pallas kernels  29.3 us (34%)
  blocking collectives  21.3 us (25%)
  between operations  2.17 us (3%)
    pallas_call x16, Pallas kernels, call(): pl.pallas_call(kernel, out_shape=[(pltpu.VMEM if kind == 'v' else pltpu.H...  29.3 us
    ppermute x4, starting transfers between devices, swap(): a = lax.ppermute(a, 'gx', within)  26.7 us
    all_to_all x2, blocking collectives, deal(): return lax.all_to_all(rows, 'gx', 0, 0, tiled=True)  21.3 us
    ppermute x4, starting transfers between devices, swap(): return (a, lax.ppermute(b, 'gx', across))  2.74 us
  transfers between devices with their start and end apart: 11, of which 0 were waited for; matrix products, arithmetic and copies ran while one was open for 1% of the time, Pallas kernels for 29%

profile of v4, /device:TPU:0, one launch (start us, length us, event | category | flops | bytes accessed | tf_op | source)
XLA Modules:
  0.0 84.7 jit_solution(7575769271529879014)
XLA Ops:
  0.7 1.3 %edges.1 = (f32[520,256]{1,0:T(8,128)S(1)}, f32[256,256]{1,0:T(8,128)S(1)}, f32[264,256]{1,0:T(8,128)S(1)}) custom-call(s32[8,4,256]{2,1,0:T(4,128)} %map_hbm.3, f32[8,256,256]{2,1,0:T(8,128)} %u_hbm.3, f32[8,256,256]{2,1,0:T(8,128)} %c_hbm.3), custom_call_target="tpu_custom_call" | custom-call | bytes 3000000 | tf_op jit(solution)/shard_map/edges/pallas_call | solution.py:709
  1.9 0.5 collective-permute-start
  2.5 0.7 collective-permute-start.1
  3.1 0.7 collective-permute-start.2
  5.1 5.3 %forward_1.1 = (f32[8,256,256]{2,1,0:T(8,128)S(1)}, f32[8,256,256]{2,1,0:T(8,128)S(1)}, f32[8,256,256]{2,1,0:T(8,128)S(1)}, f32[8,256,256]{2,1,0:T(8,128)S(1)}, ...) custom-call(f32[160]{0:T(256)S(1)} %copy-done, ...), custom_call_target="tpu_custom_call" | custom-call | bytes 18000000 | tf_op jit(solution)/shard_map/forward_1/pallas_call | solution.py:709
  10.5 0.1 edges_1.1
  10.6 5.6 %collective-permute-start.4 = (f32[256,256]{1,0:T(8,128)S(1)}, f32[256,256]{1,0:T(8,128)S(1)}, u32[]{:S(2)}, u32[]{:S(2)}) collective-permute-start(f32[256,256]{1,0:T(8,128)S(1)} %get-tuple-element.82), channel_id=1, source_target_pairs={{0,1},{1,0},{2,3},{3,2},{4,5},{5,4},{6,7},{7,6},{8,9},{9,8},{10,11... | collective-permute-start | bytes 786440 | tf_op jit(solution)/shard_map/ppermute | solution.py:738
  16.2 0.7 collective-permute-start.3
  16.9 3.0 %forward_2.1 = (f32[8,256,256]{2,1,0:T(8,128)S(1)}, f32[256,256]{1,0:T(8,128)S(1)}, f32[256,256]{1,0:T(8,128)S(1)}, f32[256,256]{1,0:T(8,128)S(1)}, f32[256,256]...) custom-call(f32[160]{0:T(256)S(1)} %copy-done, ...), custom_call_target="tpu_custom_call" | custom-call | bytes 10500000 | tf_op jit(solution)/shard_map/forward_2/pallas_call | solution.py:709
  19.9 0.0 collective-permute-done.4.near.u1h_a
  19.9 0.3 edges_2.2
  20.2 4.0 %collective-permute-start.5 = (f32[520,256]{1,0:T(8,128)S(1)}, f32[520,256]{1,0:T(8,128)S(1)}, u32[]{:S(2)}, u32[]{:S(2)}) collective-permute-start(f32[520,256]{1,0:T(8,128)S(1)} %get-tuple-element.87.edge), channel_id=1, source_target_pairs={{0,1},{1,0},{2,3},{3,2},{4,5},{5,4},{6,7},{7,6},{8,9},{9,8},{10,11... | collective-permute-start | bytes 1597448 | tf_op jit(solution)/shard_map/ppermute | solution.py:738
  24.2 0.3 edges_2.3
  24.5 0.7 collective-permute-start.6
  25.2 4.0 %forward_3_4.1 = (f32[8,256,256]{2,1,0:T(8,128)S(1)}, f32[8,256,256]{2,1,0:T(8,128)S(1)}, f32[4,8,256]{2,1,0:T(8,128)S(1)}, f32[8,256]{1,0:T(8,128)S(1)}) custom-call(f32[8,256,256]{2,1,0:T(8,128)S(1)} %get-tuple-element.73.u1, f32[8,256,256]{2,1,0:T(8,128)S(1)} %get-tuple-element.85.u2, f32[8,256,256]{2,1,0:T(8,128)S(1)} %get-tuple-element.68.c, ...), custom_call_target="tpu_custom_call" | custom-call | bytes 16500000 | tf_op jit(solution)/shard_map/forward_3_4/pallas_call | solution.py:709
  29.2 0.0 collective-permute-done.5.got.got_a
  29.2 0.5 edges_3_4.2
  29.8 0.6 edges_3_4.3
  30.3 0.7 collective-permute-start.8
  31.0 17.0 %collective-permute-start.7 = (f32[512,256]{1,0:T(8,128)S(1)}, f32[512,256]{1,0:T(8,128)S(1)}, u32[]{:S(2)}, u32[]{:S(2)}) collective-permute-start(f32[512,256]{1,0:T(8,128)S(1)} %get-tuple-element.107.own_a), channel_id=1, source_target_pairs={{0,1},{1,0},{2,3},{3,2},{4,5},{5,4},{6,7},{7,6},{8,9},{9,8},{10,11... | collective-permute-start | bytes 1572872 | tf_op jit(solution)/shard_map/ppermute | solution.py:738
  48.1 2.1 %adjoint_3.1 = (f32[8,256,256]{2,1,0:T(8,128)S(1)}, f32[8,256,256]{2,1,0:T(8,128)S(1)}) custom-call(f32[8,256,256]{2,1,0:T(8,128)S(1)} %get-tuple-element.97.u4, f32[8,256,256]{2,1,0:T(8,128)S(1)} %get-tuple-element.68.c, f32[8,256,256]{2,1,0:T(8,128)S(1)} %get-tuple-element.69.inv), custom_call_target="tpu_custom_call" | custom-call | bytes 7800000 | tf_op jit(solution)/shard_map/adjoint_3/pallas_call | solution.py:709
  50.1 10.4 %all_to_all.22 = f32[16,1,128]{2,1,0:T(1,128)S(1)} all-to-all(f32[16,1,128]{2,1,0:T(1,128)S(1)} %bitcast.17), channel_id=1, replica_groups=mesh['groups'=2,'gx'=16] {'gx'}, dimensions={0} | all-to-all | bytes 16384 | tf_op jit(solution)/shard_map/all_to_all | solution.py:742
  60.5 2.7 %adjoint_2.1 = (f32[32,256]{1,0:T(8,128)S(1)}, f32[8,256,256]{2,1,0:T(8,128)S(1)}, f32[8,256,256]{2,1,0:T(8,128)S(1)}, f32[8,256,256]{2,1,0:T(8,128)S(1)}, f32[8,256,256]{2,1,0:T(8,128)S(1)}) custom-call(f32[8,128]{1,0:T(8,128)S(1)} %get-tuple-element.67.params, f32[16,128]{1,0:T(8,128)S(1)} %bitcast.15, ...), custom_call_target="tpu_custom_call", output_to_operand_aliasing={{1}: (6, {}), {2}: (7, {})} | custom-call | bytes 9000000 | tf_op jit(solution)/shard_map/adjoint_2/pallas_call | solution.py:709
  63.2 1.1 %edges_adjoint_3_2.1 = (f32[8,256,256]{2,1,0:T(8,128)S(1)}, f32[8,256,256]{2,1,0:T(8,128)S(1)}, f32[8,256,256]{2,1,0:T(8,128)S(1)}, f32[512,256]{1,0:T(8,128)S(1)}, f32[512,256]{1,0:T(8,128)S(1)}) custom-call(f32[32,256]{1,0:T(8,128)S(1)} %get-tuple-element.104.weights, ...), custom_call_target="tpu_custom_call", output_to_operand_aliasing={{0}: (12, {}), {1}: (13, {}), {2}: (14, {})} | custom-call | bytes 6000000 | tf_op jit(solution)/shard_map/edges_adjoint_3_2/pallas_call | solution.py:709
  64.4 0.1 collective-permute-start.9
  64.4 0.7 collective-permute-start.10
  65.1 2.1 %adjoint_1.1 = (f32[8,256,256]{2,1,0:T(8,128)S(1)}, f32[8,256,256]{2,1,0:T(8,128)S(1)}, f32[8,256,256]{2,1,0:T(8,128)S(1)}) custom-call(f32[32,256]{1,0:T(8,128)S(1)} %get-tuple-element.104.weights, f32[8,256,256]{2,1,0:T(8,128)S(1)} %get-tuple-element.73.u1, f32[8,256,256]{2,1,0:T(8,128)S(1)} %get-tuple-element.112.w2, ...), custom_call_target="tpu_custom_call" | custom-call | bytes 6000000 | tf_op jit(solution)/shard_map/adjoint_1/pallas_call | solution.py:709
  67.2 2.7 %patch_sums.1 = (f32[16,128]{1,0:T(8,128)S(1)}, f32[8,256,256]{2,1,0:T(8,128)}) custom-call(s32[40,256]{1,0:T(8,128)S(1)} %get-tuple-element.120.maps, f32[8,256]{1,0:T(8,128)S(1)} %get-tuple-element.121.wall_gain, f32[8,256]{1,0:T(8,128)S(1)} %get-tuple-element.122.wall_now, f32[520,256]{1,0:T(8,128)S(1)} %collective-permute-done.5.got.got_a, ...), custom_call_target="tpu_custom_call" | custom-call | bytes 6000000 | tf_op jit(solution)/shard_map/patch_sums/pallas_call | solution.py:709
  69.9 10.9 %all_to_all.23 = f32[16,1,128]{2,1,0:T(1,128)S(1)} all-to-all(f32[16,1,128]{2,1,0:T(1,128)S(1)} %bitcast.18), channel_id=1, replica_groups=mesh['groups'=2,'gx'=16] {'gx'}, dimensions={0} | all-to-all | bytes 16384 | tf_op jit(solution)/shard_map/all_to_all | solution.py:742
  80.8 1.8 %adjoint_0.1 = (f32[8,256,256]{2,1,0:T(8,128)S(1)}, f32[1,128]{1,0:T(1,128)S(1)}) custom-call(f32[8,256,256]{2,1,0:T(8,128)S(1)} %get-tuple-element.116.w1, f32[8,256,256]{2,1,0:T(8,128)S(1)} %get-tuple-element.119.q1, f32[8,256,256]{2,1,0:T(8,128)S(1)} %get-tuple-element.112.w2, f32[8,256,256]{2,1,0:T(8,128)S(1)} %get-tuple-element.115.s, ...), custom_call_target="tpu_custom_call" | custom-call | bytes 6000000 | tf_op jit(solution)/shard_map/adjoint_0/pallas_call | solution.py:709
  82.6 0.5 slice_bitcast_fusion
  83.1 1.5 %edges_adjoint_1_0.1 = (f32[8,256,256]{2,1,0:T(8,128)}, f32[8,256,256]{2,1,0:T(8,128)}) custom-call(f32[8,256,256]{2,1,0:T(8,128)S(1)} %get-tuple-element.116.w1, f32[8,256,256]{2,1,0:T(8,128)S(1)} %get-tuple-element.114.q2, f32[8,256,256]{2,1,0:T(8,128)S(1)} %get-tuple-element.68.c, ...), custom_call_target="tpu_custom_call", output_to_operand_aliasing={{1}: (10, {})} | custom-call | bytes 6000000 | tf_op jit(solution)/shard_map/edges_adjoint_1_0/pallas_call | solution.py:709
  (13 shorter events, 0.0 us)
Async XLA Ops:
  0.6 4.5 %copy-start = (f32[160]{0:T(256)S(1)}, f32[160]{0:T(256)}, u32[]{:S(2)}) copy-start(f32[160]{0:T(256)} %absorb_ref.3) | copy-start | bytes 1924
  0.6 4.5 %copy-start.1 = (f32[64]{0:T(128)S(1)}, f32[64]{0:T(128)}, u32[]{:S(2)}) copy-start(f32[64]{0:T(128)} %param.14) | copy-start | bytes 772
  1.9 8.6 %collective-permute-start = (f32[520,256]{1,0:T(8,128)S(1)}, f32[520,256]{1,0:T(8,128)S(1)}, u32[]{:S(2)}, u32[]{:S(2)}) collective-permute-start(f32[520,256]{1,0:T(8,128)S(1)} %get-tuple-element.70), channel_id=1, source_target_pairs={{0,1},{1,0},{2,3},{3,2},{4,5},{5,4},{6,7},{7,6},{8,9},{9,8},{10,11... | collective-permute-start | bytes 1597448 | tf_op jit(solution)/shard_map/ppermute | solution.py:760
  2.5 8.0 %collective-permute-start.1 = (f32[256,256]{1,0:T(8,128)S(1)}, f32[256,256]{1,0:T(8,128)S(1)}, u32[]{:S(2)}, u32[]{:S(2)}) collective-permute-start(f32[256,256]{1,0:T(8,128)S(1)} %get-tuple-element.71), channel_id=1, source_target_pairs={{1,2},{3,4},{5,6},{7,8},{9,10},{11,12},{13,14},{2,1},{4,3},{6,5},{... | collective-permute-start | bytes 786440 | tf_op jit(solution)/shard_map/ppermute | solution.py:761
  3.1 13.8 %collective-permute-start.2 = (f32[264,256]{1,0:T(8,128)S(1)}, f32[264,256]{1,0:T(8,128)S(1)}, u32[]{:S(2)}, u32[]{:S(2)}) collective-permute-start(f32[264,256]{1,0:T(8,128)S(1)} %get-tuple-element.77), channel_id=1, source_target_pairs={{1,2},{3,4},{5,6},{7,8},{9,10},{11,12},{13,14},{2,1},{4,3},{6,5},{... | collective-permute-start | bytes 811016 | tf_op jit(solution)/shard_map/ppermute | solution.py:762
  10.6 9.3 %collective-permute-start.4 = (f32[256,256]{1,0:T(8,128)S(1)}, f32[256,256]{1,0:T(8,128)S(1)}, u32[]{:S(2)}, u32[]{:S(2)}) collective-permute-start(f32[256,256]{1,0:T(8,128)S(1)} %get-tuple-element.82), channel_id=1, source_target_pairs={{0,1},{1,0},{2,3},{3,2},{4,5},{5,4},{6,7},{7,6},{8,9},{9,8},{10,11... | collective-permute-start | bytes 786440 | tf_op jit(solution)/shard_map/ppermute | solution.py:738
  16.2 8.0 %collective-permute-start.3 = (f32[256,256]{1,0:T(8,128)S(1)}, f32[256,256]{1,0:T(8,128)S(1)}, u32[]{:S(2)}, u32[]{:S(2)}) collective-permute-start(f32[256,256]{1,0:T(8,128)S(1)} %get-tuple-element.79), channel_id=1, source_target_pairs={{1,2},{3,4},{5,6},{7,8},{9,10},{11,12},{13,14},{2,1},{4,3},{6,5},{... | collective-permute-start | bytes 786440 | tf_op jit(solution)/shard_map/ppermute | solution.py:739
  20.2 9.0 %collective-permute-start.5 = (f32[520,256]{1,0:T(8,128)S(1)}, f32[520,256]{1,0:T(8,128)S(1)}, u32[]{:S(2)}, u32[]{:S(2)}) collective-permute-start(f32[520,256]{1,0:T(8,128)S(1)} %get-tuple-element.87.edge), channel_id=1, source_target_pairs={{0,1},{1,0},{2,3},{3,2},{4,5},{5,4},{6,7},{7,6},{8,9},{9,8},{10,11... | collective-permute-start | bytes 1597448 | tf_op jit(solution)/shard_map/ppermute | solution.py:738
  24.5 5.2 %collective-permute-start.6 = (f32[520,256]{1,0:T(8,128)S(1)}, f32[520,256]{1,0:T(8,128)S(1)}, u32[]{:S(2)}, u32[]{:S(2)}) collective-permute-start(f32[520,256]{1,0:T(8,128)S(1)} %get-tuple-element.92.edge), channel_id=1, source_target_pairs={{1,2},{3,4},{5,6},{7,8},{9,10},{11,12},{13,14},{2,1},{4,3},{6,5},{... | collective-permute-start | bytes 1597448 | tf_op jit(solution)/shard_map/ppermute | solution.py:739
  30.3 32.9 %collective-permute-start.8 = (f32[512,256]{1,0:T(8,128)S(1)}, f32[512,256]{1,0:T(8,128)S(1)}, u32[]{:S(2)}, u32[]{:S(2)}) collective-permute-start(f32[512,256]{1,0:T(8,128)S(1)} %get-tuple-element.108.own_b), channel_id=1, source_target_pairs={{1,2},{3,4},{5,6},{7,8},{9,10},{11,12},{13,14},{2,1},{4,3},{6,5},{... | collective-permute-start | bytes 1572872 | tf_op jit(solution)/shard_map/ppermute | solution.py:739
  31.0 32.2 %collective-permute-start.7 = (f32[512,256]{1,0:T(8,128)S(1)}, f32[512,256]{1,0:T(8,128)S(1)}, u32[]{:S(2)}, u32[]{:S(2)}) collective-permute-start(f32[512,256]{1,0:T(8,128)S(1)} %get-tuple-element.107.own_a), channel_id=1, source_target_pairs={{0,1},{1,0},{2,3},{3,2},{4,5},{5,4},{6,7},{7,6},{8,9},{9,8},{10,11... | collective-permute-start | bytes 1572872 | tf_op jit(solution)/shard_map/ppermute | solution.py:738
  64.4 18.7 %collective-permute-start.9 = (f32[512,256]{1,0:T(8,128)S(1)}, f32[512,256]{1,0:T(8,128)S(1)}, u32[]{:S(2)}, u32[]{:S(2)}) collective-permute-start(f32[512,256]{1,0:T(8,128)S(1)} %get-tuple-element.117), channel_id=1, source_target_pairs={{0,1},{1,0},{2,3},{3,2},{4,5},{5,4},{6,7},{7,6},{8,9},{9,8},{10,11... | collective-permute-start | bytes 1572872 | tf_op jit(solution)/shard_map/ppermute | solution.py:738
  64.4 18.7 %collective-permute-start.10 = (f32[512,256]{1,0:T(8,128)S(1)}, f32[512,256]{1,0:T(8,128)S(1)}, u32[]{:S(2)}, u32[]{:S(2)}) collective-permute-start(f32[512,256]{1,0:T(8,128)S(1)} %get-tuple-element.118), channel_id=1, source_target_pairs={{1,2},{3,4},{5,6},{7,8},{9,10},{11,12},{13,14},{2,1},{4,3},{6,5},{... | collective-permute-start | bytes 1572872 | tf_op jit(solution)/shard_map/ppermute | solution.py:739

commit v5 on v4

--- a/solution.py
+++ b/solution.py
@@ -236,16 +236,15 @@
     first(cx - 1)
 
 
-def join_one_kernel(c, inv, near_a, near_b, u1_in, u1, edge_a, edge_b):
+def join_one_kernel(side, c, inv, near, u1_in, u1, edge):
     cx, side_cells = c.shape[0], c.shape[1]
-    near_a = near_a.at[pl.ds(side_cells + 8, side_cells)]
-    for side, (near, edge) in enumerate(((near_a, edge_a), (near_b, edge_b))):
-        x0 = end_layer(own_parity(), side, 0, cx)
-        for row, count in chunks(side_cells):
-            at = pl.ds(row, count)
-            value = u1[x0, at, :] + (c[x0, at, :] * inv[x0, at, :]) * near[at, :]
-            u1[x0, at, :] = value
-            edge[at, :] = value
+    x0 = end_layer(own_parity(), side, 0, cx)
+    base = near.shape[0] - side_cells
+    for row, count in chunks(side_cells):
+        at = pl.ds(row, count)
+        value = u1[x0, at, :] + (c[x0, at, :] * inv[x0, at, :]) * near[pl.ds(base + row, count), :]
+        u1[x0, at, :] = value
+        edge[at, :] = value
 
 
 def wall_rows(plane, columns, side_cells):
@@ -398,9 +397,8 @@
     second(cx - 1, False)
 
 
-def join_second_kernel(
-    side, c, inv, energy_in, edge, own, got, gb, u3_in, u4_in, u3, u4, halo, pay, energy, delta
-):
+def join_second_kernel(side, c, inv, energy_in, edge, own, got, gb, u3_in, u4_in, *refs):
+    u3, u4, halo, pay, energy, delta = refs[-6:]
     cx, side_cells = c.shape[0], c.shape[1]
     third, fourth = energy_in[2], energy_in[3]
     x0, x1 = (end_layer(own_parity(), side, k, cx) for k in range(2))
@@ -435,28 +433,38 @@
     energy[...] = rows
 
 
-def adjoint_free_kernel(u4, c, inv, w4, w3, q4):
+def adjoint_free_kernel(part, u4, c, inv, *refs):
+    w4, w3, q4 = refs[-3:]
     cx, side_cells = u4.shape[0], u4.shape[1]
 
-    def zeroth(x):
+    def place(k):
+        return end_layer(own_parity(), 0, k, cx)
+
+    def zeroth(k):
+        x = place(k)
         for row, count in chunks(side_cells):
             at = pl.ds(row, count)
             value = 2.0 * (inv[x, at, :] * u4[x, at, :])
             w4[x, at, :] = value
             q4[x, at, :] = c[x, at, :] * value
 
-    def first(x):
+    def first(k):
+        x = place(k)
+        sides = [layer(q4, place(j)) for j in (k - 1, k + 1) if not isinstance(k, int) or 0 <= j < cx]
         for row, count in chunks(side_cells):
             at = pl.ds(row, count)
             w3[x, at, :] = backward(
-                layer(q4, x), w4[x, at, :], None, layer(inv, x), 0.0,
-                x_sides(q4, x, cx), row, count, side_cells,
-            )
-
-    sweep(0, cx, zeroth)
-    first(0)
-    sweep(1, cx - 1, first)
-    first(cx - 1)
+                layer(q4, x), w4[x, at, :], None, layer(inv, x), 0.0, sides, row, count, side_cells
+            )
+
+    if part == 0:
+        sweep(0, cx - 2, zeroth)
+        first(0)
+        sweep(1, cx - 3, first)
+    else:
+        sweep(cx - 2, cx, zeroth)
+        sweep(cx - 3, cx - 1, first)
+        first(cx - 1)
 
 
 def adjoint_kernel(
@@ -541,9 +549,8 @@
             )
 
 
-def result_kernel(w1, q1, w2, s, dealt, cur, mine):
+def result_kernel(w1, q1, w2, s, cur):
     cx, side_cells = w1.shape[0], w1.shape[1]
-    mine[...] = jnp.sum(dealt[...], axis=0, keepdims=True) / float(PATCH_CELLS)
 
     def turn(x):
         for row, count in chunks(side_cells):
@@ -581,15 +588,22 @@
 
 
 def patch_kernel(
-    own, maps, wall_gain, wall_now, got_a, got_b, up, u, u1, u2, u3, u4, w4, w3, w2, w1, q2, prev,
-    sums, prev_hbm, values, columns, totals, sem,
+    own, maps, wall_gain, wall_now, got_a, got_b, up, u, u1, u2, u3, u4, w4, w3, w2, w1, q2,
+    prev, prev_ends, cur, sums, prev_hbm, cur_hbm, values, columns, totals, sems,
 ):
     cx, side_cells = u.shape[0], u.shape[1]
     last = side_cells - 1
     ends = [end_layer(own_parity(), side, 0, cx) for side in range(2)]
     inner = pl.ds(1, cx - 2)
-    leave = pltpu.make_async_copy(prev.at[inner], prev_hbm.at[inner], sem)
-    leave.start()
+    leave = [
+        pltpu.make_async_copy(prev.at[inner], prev_hbm.at[inner], sems.at[0]),
+        pltpu.make_async_copy(prev_ends.at[0], prev_hbm.at[ends[0]], sems.at[1]),
+    ]
+    for k in range(cx - 2):
+        x = end_layer(own_parity(), 0, k, cx)
+        leave.append(pltpu.make_async_copy(cur.at[x], cur_hbm.at[x], sems.at[2 + k]))
+    for copy in leave:
+        copy.start()
 
     def field(x, at, lanes):
         k = (x, at, lanes)
@@ -665,41 +679,55 @@
         return carry
 
     lax.fori_loop(0, sums.shape[0], owner, 0, unroll=8)
-    leave.wait()
-
-
-def join_last_kernel(
-    w1, q2, c, inv, s, got_a, got_b, b_a, b_b, cur, prev_in, cur_hbm, prev_hbm, delta, prev, sems
+    for copy in leave:
+        copy.wait()
+
+
+def join_last(side, w1, q2, c, inv, s, got, b, cur, prev, delta):
+    cx, side_cells = w1.shape[0], w1.shape[1]
+    x0, x1 = (end_layer(own_parity(), side, k, cx) for k in range(2))
+    for row, count in chunks(side_cells):
+        at = pl.ds(row, count)
+        change = inv[x0, at, :] * got[at, :]
+        prev[side, at, :] = (s[x0, at, :] - 1.0) * (w1[x0, at, :] + change)
+        change = c[x0, at, :] * change
+        delta[at, :] = change
+        cur[x1, at, :] += change
+    for row, count in chunks(side_cells):
+        at, below = pl.ds(row, count), pl.ds(side_cells + row, count)
+        v, total = beside(flat(delta, 0), row, count, side_cells)
+        cur[x0, at, :] += (
+            2.0 * (inv[x0, at, :] * got[at, :])
+            + (total - 6.0 * v)
+            + (got[below, :] + b[at, :] * q2[x0, at, :])
+        )
+
+
+def join_near_kernel(w1, q2, c, inv, s, got, b, cur_in, cur, prev, delta):
+    join_last(0, w1, q2, c, inv, s, got, b, cur, prev, delta)
+
+
+def share_kernel(own, dealt, cur_in, cur, mine):
+    mine[...] = (jnp.sum(dealt[...], axis=0) / float(PATCH_CELLS))[:own]
+
+
+def join_far_kernel(
+    w1, q2, c, inv, s, got, b, mine, cur_in, ends_in, cur_hbm_in, prev_hbm_in,
+    cur, prev, cur_hbm, prev_hbm, mine_hbm, delta, sems,
 ):
-    cx, side_cells = w1.shape[0], w1.shape[1]
+    cx = w1.shape[0]
     copies = []
 
     def send(src, dst):
         copies.append(pltpu.make_async_copy(src, dst, sems.at[len(copies)]))
         copies[-1].start()
 
-    inner = pl.ds(2, cx - 4)
-    send(cur.at[inner], cur_hbm.at[inner])
-    for side, (got, b) in enumerate(((got_a, b_a), (got_b, b_b))):
-        x0, x1 = (end_layer(own_parity(), side, k, cx) for k in range(2))
-        for row, count in chunks(side_cells):
-            at = pl.ds(row, count)
-            change = inv[x0, at, :] * got[at, :]
-            prev[side, at, :] = (s[x0, at, :] - 1.0) * (w1[x0, at, :] + change)
-            change = c[x0, at, :] * change
-            delta[at, :] = change
-            cur[x1, at, :] += change
-        send(prev.at[side], prev_hbm.at[x0])
-        send(cur.at[x1], cur_hbm.at[x1])
-        for row, count in chunks(side_cells):
-            at, below = pl.ds(row, count), pl.ds(side_cells + row, count)
-            v, total = beside(flat(delta, 0), row, count, side_cells)
-            cur[x0, at, :] += (
-                2.0 * (inv[x0, at, :] * got[at, :])
-                + (total - 6.0 * v)
-                + (got[below, :] + b[at, :] * q2[x0, at, :])
-            )
-        send(cur.at[x0], cur_hbm.at[x0])
+    send(mine, mine_hbm)
+    x0, x1 = (end_layer(own_parity(), 1, k, cx) for k in range(2))
+    join_last(1, w1, q2, c, inv, s, got, b, cur, prev, delta)
+    send(prev.at[1], prev_hbm.at[x0])
+    send(cur.at[x1], cur_hbm.at[x1])
+    send(cur.at[x0], cur_hbm.at[x0])
     for copy in copies:
         copy.wait()
 
@@ -775,14 +803,17 @@
         name="forward_1",
         us=6.0,
     )
-    u1, *edge_1 = call(
-        join_one_kernel,
-        v(c, inv, *near, u1),
-        [("v", field)] + [("v", plane)] * 2,
-        aliases={4: 0},
-        name="edges_1",
-        us=0.5,
-    )
+    edge_1 = []
+    for k in range(2):
+        u1, plane_1 = call(
+            functools.partial(join_one_kernel, k),
+            v(c, inv, near[k], u1),
+            [("v", field), ("v", plane)],
+            aliases={3: 0},
+            name="edges_1",
+            us=0.1,
+        )
+        edge_1.append(plane_1)
     u1h_a, u1h_b = near = swap(*edge_1)
     u2, *own_b, b_a, b_b, maps, wall_gain, wall_prior = call(
         ahead_two_kernel,
@@ -815,11 +846,11 @@
         name="forward_3_4",
         us=5.5,
     )
-    edge_4, u3h = [], []
+    edge_4, u3h, free = [], [], []
     for k in range(2):
         u3, u4, halo, pay, energy = call(
             functools.partial(join_second_kernel, k),
-            v(c, inv, energy, edge_2[k], own_b[k], second[k], got_b[k], u3, u4),
+            v(c, inv, energy, edge_2[k], own_b[k], second[k], got_b[k], u3, u4, *free[:1]),
             [("v", field)] * 2
             + [("v", plane), ("v", double)]
             + [("v", (count, LANES) if k else (STEPS, 8, side))],
@@ -830,15 +861,16 @@
         )
         edge_4.append(pay)
         u3h.append(halo)
+        free = call(
+            functools.partial(adjoint_free_kernel, k),
+            v(u4, c, inv, *free),
+            [("v", field)] * 3,
+            aliases={3: 0, 4: 1, 5: 2} if k else None,
+            name="adjoint_3",
+            us=1.0,
+        )
     third = swap(*edge_4)
-    w4, w3 = call(
-        adjoint_free_kernel,
-        v(u4, c, inv),
-        [("v", field)] * 2,
-        [VMEM(field, F32)],
-        name="adjoint_3",
-        us=2.6,
-    )
+    w4, w3, _ = free
     energy, w4, w3 = lax.optimization_barrier((energy, w4, w3))
     sums = deal(energy)
     weights, w4, w3, w2, q2 = call(
@@ -865,34 +897,49 @@
         [("v", field)] * 3,
         name="adjoint_1",
     )
-    partial, prev = call(
+    (cur,) = call(result_kernel, v(w1, q1, w2, s), [("v", field)], name="adjoint_0", us=1.8)
+    cur, ends = call(
+        join_near_kernel,
+        v(w1, q2, c, inv, s, fourth[0], got_b[0], cur),
+        [("v", field), ("v", (2, side, side))],
+        [VMEM(plane, F32)],
+        aliases={7: 0},
+        name="near_edge_0",
+        us=0.4,
+    )
+    partial, prev_out, cur_out = call(
         functools.partial(patch_kernel, own),
-        v(maps, wall_gain, wall_now, *second, up, u, u1, u2, u3, u4, w4, w3, w2, w1, q2, prev),
-        [("v", (count, LANES)), ("h", field)],
+        v(maps, wall_gain, wall_now, second[0], second[1], up, u, u1, u2, u3, u4, w4, w3, w2, w1, q2)
+        + v(prev, ends, cur),
+        [("v", (count, LANES)), ("h", field), ("h", field)],
         [
             VMEM((4 * cx + 8, side), F32),
             VMEM((side, LANES), F32),
             VMEM((-(-patches // GROUP) * GROUP + LANES, LANES), F32),
-            dma,
+            dma((cx,)),
         ],
         name="patch_sums",
+        us=2.7,
     )
     cur, mine = call(
-        result_kernel,
-        v(w1, q1, w2, s, deal(partial)),
-        [("v", field), ("v", (1, LANES))],
-        name="adjoint_0",
-    )
-    grad_absorb = mine[0, :own]
-    cur, prev = call(
-        join_last_kernel,
-        v(w1, q2, c, inv, s, *fourth, *got_b, cur) + [("h", prev)],
-        [("h", field)] * 2,
-        [VMEM(plane, F32), VMEM((2, side, side), F32), dma((7,))],
-        aliases={10: 1},
-        name="edges_adjoint_1_0",
-    )
-    return prev, cur, grad_absorb
+        functools.partial(share_kernel, own),
+        v(deal(partial), cur),
+        [("v", field), ("v", (own,))],
+        aliases={1: 0},
+        name="share",
+        us=0.1,
+    )
+    _, _, cur, prev, mine = call(
+        join_far_kernel,
+        v(w1, q2, c, inv, s, fourth[1], got_b[1], mine, cur, ends)
+        + [("h", cur_out), ("h", prev_out)],
+        [("v", field), ("v", (2, side, side)), ("h", field), ("h", field), ("h", (own,))],
+        [VMEM(plane, F32), dma((4,))],
+        aliases={8: 0, 9: 1, 10: 2, 11: 3},
+        name="far_edge_0",
+        us=1.0,
+    )
+    return prev, cur, mine
 
 
 def solution(mesh):

time: 85 us -> 83.3 us (0.980)
  starting transfers between devices: 31.3 us -> 20.9 us
  blocking collectives: 21.3 us -> 30 us
    ppermute x4, starting transfers between devices: 26.7 us -> 16.1 us  [swap(): a = lax.ppermute(a, 'gx', within)]
    all_to_all x2, blocking collectives: 21.3 us -> 30 us  [deal(): return lax.all_to_all(rows, 'gx', 0, 0, tiled=True)]
    pallas_call x16 -> x20, Pallas kernels: 29.3 us -> 29.6 us  [call(): pl.pallas_call(kernel, out_shape=[(pltpu.VMEM if kind == 'v' else pltpu.H...]
  transfers between devices with their start and end apart: 11 -> 11, of which waited for: 0 -> 0; matrix products, arithmetic and copies ran while one was open for 1% -> 0% of each run, Pallas kernels for 29% -> 31%
where the time goes in v5:
time: 83.3 us; the launch traced here: 82.9 us
  blocking collectives  30 us (36%)
  Pallas kernels  29.6 us (36%)
  starting transfers between devices  20.9 us (25%)
  between operations  2.35 us (3%)
    all_to_all x2, blocking collectives, deal(): return lax.all_to_all(rows, 'gx', 0, 0, tiled=True)  30 us
    pallas_call x20, Pallas kernels, call(): pl.pallas_call(kernel, out_shape=[(pltpu.VMEM if kind == 'v' else pltpu.H...  29.6 us
    ppermute x4, starting transfers between devices, swap(): a = lax.ppermute(a, 'gx', within)  16.1 us
    ppermute x4, starting transfers between devices, swap(): return (a, lax.ppermute(b, 'gx', across))  2.93 us
  transfers between devices with their start and end apart: 11, of which 0 were waited for; matrix products, arithmetic and copies ran while one was open for 0% of the time, Pallas kernels for 31%

profile of v5, /device:TPU:0, one launch (start us, length us, event | category | flops | bytes accessed | tf_op | source)
XLA Modules:
  0.0 82.9 jit_solution(14566617108980903752)
XLA Ops:
  0.7 1.3 %edges.1 = (f32[520,256]{1,0:T(8,128)S(1)}, f32[256,256]{1,0:T(8,128)S(1)}, f32[264,256]{1,0:T(8,128)S(1)}) custom-call(s32[8,4,256]{2,1,0:T(4,128)} %map_hbm.3, f32[8,256,256]{2,1,0:T(8,128)} %u_hbm.3, f32[8,256,256]{2,1,0:T(8,128)} %c_hbm.3), custom_call_target="tpu_custom_call" | custom-call | bytes 3000000 | tf_op jit(solution)/shard_map/edges/pallas_call | solution.py:737
  1.9 0.5 collective-permute-start.1
  2.5 0.7 collective-permute-start
  3.1 0.7 collective-permute-start.2
  5.1 5.3 %forward_1.1 = (f32[8,256,256]{2,1,0:T(8,128)S(1)}, f32[8,256,256]{2,1,0:T(8,128)S(1)}, f32[8,256,256]{2,1,0:T(8,128)S(1)}, f32[8,256,256]{2,1,0:T(8,128)S(1)}, ...) custom-call(f32[160]{0:T(256)S(1)} %copy-done, ...), custom_call_target="tpu_custom_call" | custom-call | bytes 18000000 | tf_op jit(solution)/shard_map/forward_1/pallas_call | solution.py:737
  10.5 0.1 edges_1.2
  10.6 5.2 %collective-permute-start.4 = (f32[256,256]{1,0:T(8,128)S(1)}, f32[256,256]{1,0:T(8,128)S(1)}, u32[]{:S(2)}, u32[]{:S(2)}) collective-permute-start(f32[256,256]{1,0:T(8,128)S(1)} %get-tuple-element.91), channel_id=1, source_target_pairs={{0,1},{1,0},{2,3},{3,2},{4,5},{5,4},{6,7},{7,6},{8,9},{9,8},{10,11... | collective-permute-start | bytes 786440 | tf_op jit(solution)/shard_map/ppermute | solution.py:766
  15.8 0.1 edges_1.3
  15.8 0.7 collective-permute-start.3
  16.5 3.0 %forward_2.1 = (f32[8,256,256]{2,1,0:T(8,128)S(1)}, f32[256,256]{1,0:T(8,128)S(1)}, f32[256,256]{1,0:T(8,128)S(1)}, f32[256,256]{1,0:T(8,128)S(1)}, f32[256,256]...) custom-call(f32[160]{0:T(256)S(1)} %copy-done, ...), custom_call_target="tpu_custom_call" | custom-call | bytes 10500000 | tf_op jit(solution)/shard_map/forward_2/pallas_call | solution.py:737
  19.6 0.3 edges_2.2
  19.8 4.4 %collective-permute-start.5 = (f32[520,256]{1,0:T(8,128)S(1)}, f32[520,256]{1,0:T(8,128)S(1)}, u32[]{:S(2)}, u32[]{:S(2)}) collective-permute-start(f32[520,256]{1,0:T(8,128)S(1)} %get-tuple-element.96.edge), channel_id=1, source_target_pairs={{0,1},{1,0},{2,3},{3,2},{4,5},{5,4},{6,7},{7,6},{8,9},{9,8},{10,11... | collective-permute-start | bytes 1597448 | tf_op jit(solution)/shard_map/ppermute | solution.py:766
  24.2 0.3 edges_2.3
  24.5 0.7 collective-permute-start.6
  25.2 4.0 %forward_3_4.1 = (f32[8,256,256]{2,1,0:T(8,128)S(1)}, f32[8,256,256]{2,1,0:T(8,128)S(1)}, f32[4,8,256]{2,1,0:T(8,128)S(1)}, f32[8,256]{1,0:T(8,128)S(1)}) custom-call(f32[8,256,256]{2,1,0:T(8,128)S(1)} %get-tuple-element.82.u1, f32[8,256,256]{2,1,0:T(8,128)S(1)} %get-tuple-element.94.u2, f32[8,256,256]{2,1,0:T(8,128)S(1)} %get-tuple-element.76.c, ...), custom_call_target="tpu_custom_call" | custom-call | bytes 16500000 | tf_op jit(solution)/shard_map/forward_3_4/pallas_call | solution.py:737
  29.2 0.5 edges_3_4.2
  29.8 6.5 %collective-permute-start.7 = (f32[512,256]{1,0:T(8,128)S(1)}, f32[512,256]{1,0:T(8,128)S(1)}, u32[]{:S(2)}, u32[]{:S(2)}) collective-permute-start(f32[512,256]{1,0:T(8,128)S(1)} %get-tuple-element.119.own_a), channel_id=1, source_target_pairs={{0,1},{1,0},{2,3},{3,2},{4,5},{5,4},{6,7},{7,6},{8,9},{9,8},{10,11... | collective-permute-start | bytes 1572872 | tf_op jit(solution)/shard_map/ppermute | solution.py:766
  36.2 1.4 %adjoint_3.2 = (f32[8,256,256]{2,1,0:T(8,128)S(1)}, f32[8,256,256]{2,1,0:T(8,128)S(1)}, f32[8,256,256]{2,1,0:T(8,128)S(1)}) custom-call(f32[8,256,256]{2,1,0:T(8,128)S(1)} %get-tuple-element.104.u4.u4_in, f32[8,256,256]{2,1,0:T(8,128)S(1)} %get-tuple-element.76.c, f32[8,256,256]{2,1,0:T(8,128)S(1)} %get-tuple-element.77.inv), custom_call_target="tpu_custom_call" | custom-call | bytes 3000000 | tf_op jit(solution)/shard_map/adjoint_3/pallas_call | solution.py:737
  37.7 0.6 edges_3_4.3
  38.2 0.7 collective-permute-start.8
  38.9 0.8 adjoint_3.3
  39.7 18.6 %all_to_all.22 = f32[16,1,128]{2,1,0:T(1,128)S(1)} all-to-all(f32[16,1,128]{2,1,0:T(1,128)S(1)} %bitcast.15), channel_id=1, replica_groups=mesh['groups'=2,'gx'=16] {'gx'}, dimensions={0} | all-to-all | bytes 16384 | tf_op jit(solution)/shard_map/all_to_all | solution.py:770
  58.3 2.7 %adjoint_2.1 = (f32[32,256]{1,0:T(8,128)S(1)}, f32[8,256,256]{2,1,0:T(8,128)S(1)}, f32[8,256,256]{2,1,0:T(8,128)S(1)}, f32[8,256,256]{2,1,0:T(8,128)S(1)}, f32[8,256,256]{2,1,0:T(8,128)S(1)}) custom-call(f32[8,128]{1,0:T(8,128)S(1)} %get-tuple-element.75.params, f32[16,128]{1,0:T(8,128)S(1)} %bitcast.13, ...), custom_call_target="tpu_custom_call", output_to_operand_aliasing={{1}: (6, {}), {2}: (7, {})} | custom-call | bytes 9000000 | tf_op jit(solution)/shard_map/adjoint_2/pallas_call | solution.py:737
  61.1 1.2 %edges_adjoint_3_2.1 = (f32[8,256,256]{2,1,0:T(8,128)S(1)}, f32[8,256,256]{2,1,0:T(8,128)S(1)}, f32[8,256,256]{2,1,0:T(8,128)S(1)}, f32[512,256]{1,0:T(8,128)S(1)}, f32[512,256]{1,0:T(8,128)S(1)}) custom-call(f32[32,256]{1,0:T(8,128)S(1)} %get-tuple-element.116.weights, ...), custom_call_target="tpu_custom_call", output_to_operand_aliasing={{0}: (12, {}), {1}: (13, {}), {2}: (14, {})} | custom-call | bytes 6000000 | tf_op jit(solution)/shard_map/edges_adjoint_3_2/pallas_call | solution.py:737
  62.3 0.1 collective-permute-start.10
  62.4 0.9 %collective-permute-start.9 = (f32[512,256]{1,0:T(8,128)S(1)}, f32[512,256]{1,0:T(8,128)S(1)}, u32[]{:S(2)}, u32[]{:S(2)}) collective-permute-start(f32[512,256]{1,0:T(8,128)S(1)} %get-tuple-element.129), channel_id=1, source_target_pairs={{1,2},{3,4},{5,6},{7,8},{9,10},{11,12},{13,14},{2,1},{4,3},{6,5},{... | collective-permute-start | bytes 1572872 | tf_op jit(solution)/shard_map/ppermute | solution.py:767
  63.2 2.1 %adjoint_1.1 = (f32[8,256,256]{2,1,0:T(8,128)S(1)}, f32[8,256,256]{2,1,0:T(8,128)S(1)}, f32[8,256,256]{2,1,0:T(8,128)S(1)}) custom-call(f32[32,256]{1,0:T(8,128)S(1)} %get-tuple-element.116.weights, f32[8,256,256]{2,1,0:T(8,128)S(1)} %get-tuple-element.82.u1, f32[8,256,256]{2,1,0:T(8,128)S(1)} %get-tuple-element.124.w2, ...), custom_call_target="tpu_custom_call" | custom-call | bytes 6000000 | tf_op jit(solution)/shard_map/adjoint_1/pallas_call | solution.py:737
  65.4 1.8 %adjoint_0.1.cur_in = f32[8,256,256]{2,1,0:T(8,128)S(1)} custom-call(f32[8,256,256]{2,1,0:T(8,128)S(1)} %get-tuple-element.128.w1, f32[8,256,256]{2,1,0:T(8,128)S(1)} %get-tuple-element.136.q1, f32[8,256,256]{2,1,0:T(8,128)S(1)} %get-tuple-element.124.w2, f32[8,256,256]{2,1,0:T(8,128)S(1)} %get-tuple-element.127.s), custom_call_target="tpu_custom_call" | custom-call | bytes 5400000 | tf_op jit(solution)/shard_map/adjoint_0/pallas_call | solution.py:737
  67.2 0.3 near_edge_0.1
  67.5 2.7 %patch_sums.1 = (f32[16,128]{1,0:T(8,128)S(1)}, f32[8,256,256]{2,1,0:T(8,128)}, f32[8,256,256]{2,1,0:T(8,128)}) custom-call(s32[40,256]{1,0:T(8,128)S(1)} %get-tuple-element.130.maps, f32[8,256]{1,0:T(8,128)S(1)} %get-tuple-element.131.wall_gain, f32[8,256]{1,0:T(8,128)S(1)} %get-tuple-element.132.wall_now, f32[520,256]{1,0:T(8,128)S(1)} %collective-permute-done.5.got.got_a, ...), custom_call_target="tpu_custom_call" | custom-call | bytes 8100000 | tf_op jit(solution)/shard_map/patch_sums/pallas_call | solution.py:737
  70.3 11.3 %all_to_all.23 = f32[16,1,128]{2,1,0:T(1,128)S(1)} all-to-all(f32[16,1,128]{2,1,0:T(1,128)S(1)} %bitcast.16), channel_id=1, replica_groups=mesh['groups'=2,'gx'=16] {'gx'}, dimensions={0} | all-to-all | bytes 16384 | tf_op jit(solution)/shard_map/all_to_all | solution.py:770
  81.6 1.1 %far_edge_0.1 = (f32[8,256,256]{2,1,0:T(8,128)S(1)}, f32[2,256,256]{2,1,0:T(8,128)S(1)}, f32[8,256,256]{2,1,0:T(8,128)}, f32[8,256,256]{2,1,0:T(8,128)}, f32[10]{0:T(128)}) custom-call(f32[8,256,256]{2,1,0:T(8,128)S(1)} %get-tuple-element.128.w1, ...), custom_call_target="tpu_custom_call", output_to_operand_aliasing={{0}: (8, {}), {1}: (9, {}), {2}: (10, {}), {3}: (11, {})} | custom-call | bytes 3000000 | tf_op jit(solution)/shard_map/far_edge_0/pallas_call | solution.py:737
  (16 shorter events, 0.0 us)
Async XLA Ops:
  0.6 4.5 %copy-start = (f32[160]{0:T(256)S(1)}, f32[160]{0:T(256)}, u32[]{:S(2)}) copy-start(f32[160]{0:T(256)} %absorb_ref.3) | copy-start | bytes 1924
  0.6 4.5 %copy-start.1 = (f32[64]{0:T(128)S(1)}, f32[64]{0:T(128)}, u32[]{:S(2)}) copy-start(f32[64]{0:T(128)} %param.14) | copy-start | bytes 772
  1.9 8.5 %collective-permute-start.1 = (f32[520,256]{1,0:T(8,128)S(1)}, f32[520,256]{1,0:T(8,128)S(1)}, u32[]{:S(2)}, u32[]{:S(2)}) collective-permute-start(f32[520,256]{1,0:T(8,128)S(1)} %get-tuple-element.79), channel_id=1, source_target_pairs={{0,1},{1,0},{2,3},{3,2},{4,5},{5,4},{6,7},{7,6},{8,9},{9,8},{10,11... | collective-permute-start | bytes 1597448 | tf_op jit(solution)/shard_map/ppermute | solution.py:788
  2.5 13.3 %collective-permute-start = (f32[256,256]{1,0:T(8,128)S(1)}, f32[256,256]{1,0:T(8,128)S(1)}, u32[]{:S(2)}, u32[]{:S(2)}) collective-permute-start(f32[256,256]{1,0:T(8,128)S(1)} %get-tuple-element.78), channel_id=1, source_target_pairs={{1,2},{3,4},{5,6},{7,8},{9,10},{11,12},{13,14},{2,1},{4,3},{6,5},{... | collective-permute-start | bytes 786440 | tf_op jit(solution)/shard_map/ppermute | solution.py:789
  3.1 13.4 %collective-permute-start.2 = (f32[264,256]{1,0:T(8,128)S(1)}, f32[264,256]{1,0:T(8,128)S(1)}, u32[]{:S(2)}, u32[]{:S(2)}) collective-permute-start(f32[264,256]{1,0:T(8,128)S(1)} %get-tuple-element.86), channel_id=1, source_target_pairs={{1,2},{3,4},{5,6},{7,8},{9,10},{11,12},{13,14},{2,1},{4,3},{6,5},{... | collective-permute-start | bytes 811016 | tf_op jit(solution)/shard_map/ppermute | solution.py:790
  10.6 9.0 %collective-permute-start.4 = (f32[256,256]{1,0:T(8,128)S(1)}, f32[256,256]{1,0:T(8,128)S(1)}, u32[]{:S(2)}, u32[]{:S(2)}) collective-permute-start(f32[256,256]{1,0:T(8,128)S(1)} %get-tuple-element.91), channel_id=1, source_target_pairs={{0,1},{1,0},{2,3},{3,2},{4,5},{5,4},{6,7},{7,6},{8,9},{9,8},{10,11... | collective-permute-start | bytes 786440 | tf_op jit(solution)/shard_map/ppermute | solution.py:766
  15.8 8.4 %collective-permute-start.3 = (f32[256,256]{1,0:T(8,128)S(1)}, f32[256,256]{1,0:T(8,128)S(1)}, u32[]{:S(2)}, u32[]{:S(2)}) collective-permute-start(f32[256,256]{1,0:T(8,128)S(1)} %get-tuple-element.88), channel_id=1, source_target_pairs={{1,2},{3,4},{5,6},{7,8},{9,10},{11,12},{13,14},{2,1},{4,3},{6,5},{... | collective-permute-start | bytes 786440 | tf_op jit(solution)/shard_map/ppermute | solution.py:767
  19.8 9.4 %collective-permute-start.5 = (f32[520,256]{1,0:T(8,128)S(1)}, f32[520,256]{1,0:T(8,128)S(1)}, u32[]{:S(2)}, u32[]{:S(2)}) collective-permute-start(f32[520,256]{1,0:T(8,128)S(1)} %get-tuple-element.96.edge), channel_id=1, source_target_pairs={{0,1},{1,0},{2,3},{3,2},{4,5},{5,4},{6,7},{7,6},{8,9},{9,8},{10,11... | collective-permute-start | bytes 1597448 | tf_op jit(solution)/shard_map/ppermute | solution.py:766
  24.5 13.1 %collective-permute-start.6 = (f32[520,256]{1,0:T(8,128)S(1)}, f32[520,256]{1,0:T(8,128)S(1)}, u32[]{:S(2)}, u32[]{:S(2)}) collective-permute-start(f32[520,256]{1,0:T(8,128)S(1)} %get-tuple-element.101.edge), channel_id=1, source_target_pairs={{1,2},{3,4},{5,6},{7,8},{9,10},{11,12},{13,14},{2,1},{4,3},{6,5},{... | collective-permute-start | bytes 1597448 | tf_op jit(solution)/shard_map/ppermute | solution.py:767
  29.8 31.3 %collective-permute-start.7 = (f32[512,256]{1,0:T(8,128)S(1)}, f32[512,256]{1,0:T(8,128)S(1)}, u32[]{:S(2)}, u32[]{:S(2)}) collective-permute-start(f32[512,256]{1,0:T(8,128)S(1)} %get-tuple-element.119.own_a), channel_id=1, source_target_pairs={{0,1},{1,0},{2,3},{3,2},{4,5},{5,4},{6,7},{7,6},{8,9},{9,8},{10,11... | collective-permute-start | bytes 1572872 | tf_op jit(solution)/shard_map/ppermute | solution.py:766
  38.2 22.9 %collective-permute-start.8 = (f32[512,256]{1,0:T(8,128)S(1)}, f32[512,256]{1,0:T(8,128)S(1)}, u32[]{:S(2)}, u32[]{:S(2)}) collective-permute-start(f32[512,256]{1,0:T(8,128)S(1)} %get-tuple-element.120.own_b), channel_id=1, source_target_pairs={{1,2},{3,4},{5,6},{7,8},{9,10},{11,12},{13,14},{2,1},{4,3},{6,5},{... | collective-permute-start | bytes 1572872 | tf_op jit(solution)/shard_map/ppermute | solution.py:767
  62.3 5.0 %collective-permute-start.10 = (f32[512,256]{1,0:T(8,128)S(1)}, f32[512,256]{1,0:T(8,128)S(1)}, u32[]{:S(2)}, u32[]{:S(2)}) collective-permute-start(f32[512,256]{1,0:T(8,128)S(1)} %get-tuple-element.135), channel_id=1, source_target_pairs={{0,1},{1,0},{2,3},{3,2},{4,5},{5,4},{6,7},{7,6},{8,9},{9,8},{10,11... | collective-permute-start | bytes 1572872 | tf_op jit(solution)/shard_map/ppermute | solution.py:766
  62.4 19.3 %collective-permute-start.9 = (f32[512,256]{1,0:T(8,128)S(1)}, f32[512,256]{1,0:T(8,128)S(1)}, u32[]{:S(2)}, u32[]{:S(2)}) collective-permute-start(f32[512,256]{1,0:T(8,128)S(1)} %get-tuple-element.129), channel_id=1, source_target_pairs={{1,2},{3,4},{5,6},{7,8},{9,10},{11,12},{13,14},{2,1},{4,3},{6,5},{... | collective-permute-start | bytes 1572872 | tf_op jit(solution)/shard_map/ppermute | solution.py:767

commit v6 on v5

--- a/solution.py
+++ b/solution.py
@@ -118,24 +118,28 @@
 
 def start_kernel(map_hbm, u_hbm, c_hbm, c_a, u_b, c_b, maps, sems):
     cx, side_cells = u_hbm.shape[0], u_hbm.shape[1]
-    copies = []
     ends = [end_layer(own_parity(), side, 0, cx) for side in range(2)]
-    u_a = c_a.at[pl.ds(side_cells + 8, side_cells)]
-    for side, (u, c) in enumerate(((u_a, c_a), (u_b, c_b))):
-        x0 = ends[side]
+    plane = pl.ds(0, side_cells)
+    copies = [
+        pltpu.make_async_copy(src, dst, sems.at[k])
         for k, (src, dst) in enumerate(
-            ((map_hbm, maps.at[side]), (u_hbm, u), (c_hbm, c.at[pl.ds(0, side_cells)]))
-        ):
-            copies.append(pltpu.make_async_copy(src.at[x0], dst, sems.at[k, side]))
+            (
+                (map_hbm, maps),
+                (u_hbm.at[ends[1]], u_b),
+                (c_hbm.at[ends[1]], c_b.at[plane]),
+                (c_hbm.at[ends[0]], c_a.at[plane]),
+                (u_hbm.at[ends[0]], c_a.at[pl.ds(side_cells + 8, side_cells)]),
+            )
+        )
+    ]
     for copy in copies:
         copy.start()
+    copies[0].wait()
     for side, c in enumerate((c_a, c_b)):
-        copies[3 * side].wait()
-        c[side_cells : side_cells + 4, :] = maps[side].astype(F32)
+        c[side_cells : side_cells + 4, :] = maps[ends[side]].astype(F32)
         c[side_cells + 4 : side_cells + 8, :] = jnp.zeros((4, side_cells), F32)
-    for k, copy in enumerate(copies):
-        if k % 3:
-            copy.wait()
+    for copy in copies[1:]:
+        copy.wait()
 
 
 def lookup(maps, absorb_ref):
@@ -178,20 +182,20 @@
 
 
 def ahead_one_kernel(
-    absorb_ref, checkpoint, target, tail, map_hbm, u_hbm, up_hbm, c_hbm,
-    u, up, c, s, inv, u1, params, map_ref,
+    absorb_ref, checkpoint, target, tail, map_ref, u_hbm, up_hbm, c_hbm,
+    u, up, c, s, inv, u1, params,
     maps, found, turned, columns, gains, sems,
 ):
     cx, side_cells = u.shape[0], u.shape[1]
-    copies = [
-        pltpu.make_async_copy(src, dst, sems.at[k])
-        for k, (src, dst) in enumerate(
-            ((map_hbm, map_ref), (u_hbm, u), (up_hbm, up), (c_hbm, c))
-        )
-    ]
-    for copy in copies:
-        copy.start()
-    copies[0].wait()
+    arrays = ((u_hbm, u), (up_hbm, up), (c_hbm, c))
+
+    def load(k, x):
+        src, dst = arrays[k]
+        return pltpu.make_async_copy(src.at[x], dst.at[x], sems.at[k, x])
+
+    for x in range(cx):
+        for k in range(3):
+            load(k, x).start()
     for x in range(cx):
         maps[4 * x : 4 * x + 4, :] = map_ref[x]
     found[...] = lookup(maps[...], absorb_ref)
@@ -220,8 +224,6 @@
             )
 
     sweep(0, cx, spread)
-    for copy in copies[1:]:
-        copy.wait()
     history = target.shape[1]
     lane = lax.broadcasted_iota(jnp.int32, params.shape, 1)
     spot = lax.broadcasted_iota(jnp.int32, target.shape, 1)
@@ -231,8 +233,21 @@
         value = jnp.sum(jnp.where(spot == start + n, target[...], 0.0), axis=1, keepdims=True)
         row = jnp.where(lane == n, value, row)
     params[...] = row
+    for x in range(2):
+        load(0, x).wait()
+    for k in (1, 2):
+        load(k, 0).wait()
     first(0)
-    sweep(1, cx - 1, first)
+
+    def turn(x):
+        load(0, x + 1).wait()
+        load(1, x).wait()
+        load(2, x).wait()
+        first(x)
+
+    sweep(1, cx - 1, turn)
+    for k in (1, 2):
+        load(k, cx - 1).wait()
     first(cx - 1)
 
 
@@ -777,28 +792,28 @@
         ("h", pltpu.with_memory_space_constraint(a, pltpu.HBM))
         for a in (patch_map, u_cur, u_prev, courant_sq)
     ]
-    c_a, u_b, c_b = call(
+    c_a, u_b, c_b, own_maps = call(
         start_kernel,
         [raw[0], raw[1], raw[3]],
-        [("v", (2 * side + 8, side)), ("v", plane), ("v", tall)],
-        [VMEM((2, 4, side), jnp.int32), dma((3, 2))],
+        [("v", (2 * side + 8, side)), ("v", plane), ("v", tall), ("v", (cx, 4, side), jnp.int32)],
+        [dma((5,))],
         name="edges",
         us=1.0,
     )
     near_a = lax.ppermute(c_a, "gx", within)
     near = (near_a, lax.ppermute(u_b, "gx", across))
     got_c = (near_a, lax.ppermute(c_b, "gx", across))
-    u, up, c, s, inv, u1, params, own_maps = call(
+    u, up, c, s, inv, u1, params = call(
         ahead_one_kernel,
-        [ab] + v(*small) + raw,
-        [("v", field)] * 6 + [("v", (8, LANES)), ("v", (cx, 4, side), jnp.int32)],
+        [ab] + v(*small, own_maps) + raw[1:],
+        [("v", field)] * 6 + [("v", (8, LANES))],
         [
             VMEM((4 * cx, side), jnp.int32),
             VMEM((4 * cx, side), F32),
             VMEM((LANES, side), F32),
             VMEM((side, LANES), F32),
             VMEM((side, LANES), F32),
-            dma((4,)),
+            dma((3, cx)),
         ],
         name="forward_1",
         us=6.0,

time: 83.3 us -> 82.8 us (level)
  no operation moved by 1% of the time
where the time goes in v6:
time: 82.8 us; the launch traced here: 82.4 us
  blocking collectives  29.9 us (36%)
  Pallas kernels  29.1 us (35%)
  starting transfers between devices  21 us (25%)
  between operations  2.35 us (3%)
    all_to_all x2, blocking collectives, deal(): return lax.all_to_all(rows, 'gx', 0, 0, tiled=True)  29.9 us
    pallas_call x20, Pallas kernels, call(): pl.pallas_call(kernel, out_shape=[(pltpu.VMEM if kind == 'v' else pltpu.H...  29.1 us
    ppermute x4, starting transfers between devices, swap(): a = lax.ppermute(a, 'gx', within)  16.2 us
    ppermute x4, starting transfers between devices, swap(): return (a, lax.ppermute(b, 'gx', across))  2.93 us
  transfers between devices with their start and end apart: 11, of which 0 were waited for; matrix products, arithmetic and copies ran while one was open for 0% of the time, Pallas kernels for 31%

profile of v6, /device:TPU:0, one launch (start us, length us, event | category | flops | bytes accessed | tf_op | source)
XLA Modules:
  0.0 82.4 jit_solution(2291129592032475599)
XLA Ops:
  0.7 1.3 %edges.1 = (f32[520,256]{1,0:T(8,128)S(1)}, f32[256,256]{1,0:T(8,128)S(1)}, f32[264,256]{1,0:T(8,128)S(1)}, s32[8,4,256]{2,1,0:T(4,128)S(1)}) custom-call(s32[8,4,256]{2,1,0:T(4,128)} %map_hbm.1, f32[8,256,256]{2,1,0:T(8,128)} %u_hbm.3, f32[8,256,256]{2,1,0:T(8,128)} %c_hbm.3), custom_call_target="tpu_custom_call" | custom-call | bytes 3000000 | tf_op jit(solution)/shard_map/edges/pallas_call | solution.py:752
  1.9 0.5 collective-permute-start.1
  2.4 0.7 collective-permute-start
  3.1 0.7 collective-permute-start.2
  5.1 4.9 %forward_1.1 = (f32[8,256,256]{2,1,0:T(8,128)S(1)}, f32[8,256,256]{2,1,0:T(8,128)S(1)}, f32[8,256,256]{2,1,0:T(8,128)S(1)}, f32[8,256,256]{2,1,0:T(8,128)S(1)}, ...) custom-call(f32[160]{0:T(256)S(1)} %copy-done, s32[1,1]{1,0:T(1,128)} %bitcast.11.checkpoint, ...), custom_call_target="tpu_custom_call" | custom-call | bytes 18000000 | tf_op jit(solution)/shard_map/forward_1/pallas_call | solution.py:752
  10.0 0.1 edges_1.2
  10.1 5.2 %collective-permute-start.4 = (f32[256,256]{1,0:T(8,128)S(1)}, f32[256,256]{1,0:T(8,128)S(1)}, u32[]{:S(2)}, u32[]{:S(2)}) collective-permute-start(f32[256,256]{1,0:T(8,128)S(1)} %get-tuple-element.91), channel_id=1, source_target_pairs={{0,1},{1,0},{2,3},{3,2},{4,5},{5,4},{6,7},{7,6},{8,9},{9,8},{10,11... | collective-permute-start | bytes 786440 | tf_op jit(solution)/shard_map/ppermute | solution.py:781
  15.3 0.1 edges_1.3
  15.3 0.7 collective-permute-start.3
  16.0 3.0 %forward_2.1 = (f32[8,256,256]{2,1,0:T(8,128)S(1)}, f32[256,256]{1,0:T(8,128)S(1)}, f32[256,256]{1,0:T(8,128)S(1)}, f32[256,256]{1,0:T(8,128)S(1)}, f32[256,256]...) custom-call(f32[160]{0:T(256)S(1)} %copy-done, ...), custom_call_target="tpu_custom_call" | custom-call | bytes 10500000 | tf_op jit(solution)/shard_map/forward_2/pallas_call | solution.py:752
  19.1 0.3 edges_2.2
  19.4 4.5 %collective-permute-start.5 = (f32[520,256]{1,0:T(8,128)S(1)}, f32[520,256]{1,0:T(8,128)S(1)}, u32[]{:S(2)}, u32[]{:S(2)}) collective-permute-start(f32[520,256]{1,0:T(8,128)S(1)} %get-tuple-element.96.edge), channel_id=1, source_target_pairs={{0,1},{1,0},{2,3},{3,2},{4,5},{5,4},{6,7},{7,6},{8,9},{9,8},{10,11... | collective-permute-start | bytes 1597448 | tf_op jit(solution)/shard_map/ppermute | solution.py:781
  23.8 0.2 edges_2.3
  24.1 0.7 collective-permute-start.6
  24.8 4.0 %forward_3_4.1 = (f32[8,256,256]{2,1,0:T(8,128)S(1)}, f32[8,256,256]{2,1,0:T(8,128)S(1)}, f32[4,8,256]{2,1,0:T(8,128)S(1)}, f32[8,256]{1,0:T(8,128)S(1)}) custom-call(f32[8,256,256]{2,1,0:T(8,128)S(1)} %get-tuple-element.83.u1, f32[8,256,256]{2,1,0:T(8,128)S(1)} %get-tuple-element.94.u2, f32[8,256,256]{2,1,0:T(8,128)S(1)} %get-tuple-element.77.c, ...), custom_call_target="tpu_custom_call" | custom-call | bytes 16500000 | tf_op jit(solution)/shard_map/forward_3_4/pallas_call | solution.py:752
  28.8 0.6 edges_3_4.2
  29.3 6.5 %collective-permute-start.7 = (f32[512,256]{1,0:T(8,128)S(1)}, f32[512,256]{1,0:T(8,128)S(1)}, u32[]{:S(2)}, u32[]{:S(2)}) collective-permute-start(f32[512,256]{1,0:T(8,128)S(1)} %get-tuple-element.119.own_a), channel_id=1, source_target_pairs={{0,1},{1,0},{2,3},{3,2},{4,5},{5,4},{6,7},{7,6},{8,9},{9,8},{10,11... | collective-permute-start | bytes 1572872 | tf_op jit(solution)/shard_map/ppermute | solution.py:781
  35.8 1.4 %adjoint_3.2 = (f32[8,256,256]{2,1,0:T(8,128)S(1)}, f32[8,256,256]{2,1,0:T(8,128)S(1)}, f32[8,256,256]{2,1,0:T(8,128)S(1)}) custom-call(f32[8,256,256]{2,1,0:T(8,128)S(1)} %get-tuple-element.104.u4.u4_in, f32[8,256,256]{2,1,0:T(8,128)S(1)} %get-tuple-element.77.c, f32[8,256,256]{2,1,0:T(8,128)S(1)} %get-tuple-element.78.inv), custom_call_target="tpu_custom_call" | custom-call | bytes 3000000 | tf_op jit(solution)/shard_map/adjoint_3/pallas_call | solution.py:752
  37.2 0.5 edges_3_4.3
  37.8 0.7 collective-permute-start.8
  38.5 0.8 adjoint_3.3
  39.3 18.6 %all_to_all.22 = f32[16,1,128]{2,1,0:T(1,128)S(1)} all-to-all(f32[16,1,128]{2,1,0:T(1,128)S(1)} %bitcast.15), channel_id=1, replica_groups=mesh['groups'=2,'gx'=16] {'gx'}, dimensions={0} | all-to-all | bytes 16384 | tf_op jit(solution)/shard_map/all_to_all | solution.py:785
  57.9 2.7 %adjoint_2.1 = (f32[32,256]{1,0:T(8,128)S(1)}, f32[8,256,256]{2,1,0:T(8,128)S(1)}, f32[8,256,256]{2,1,0:T(8,128)S(1)}, f32[8,256,256]{2,1,0:T(8,128)S(1)}, f32[8,256,256]{2,1,0:T(8,128)S(1)}) custom-call(f32[8,128]{1,0:T(8,128)S(1)} %get-tuple-element.76.params, f32[16,128]{1,0:T(8,128)S(1)} %bitcast.13, ...), custom_call_target="tpu_custom_call", output_to_operand_aliasing={{1}: (6, {}), {2}: (7, {})} | custom-call | bytes 9000000 | tf_op jit(solution)/shard_map/adjoint_2/pallas_call | solution.py:752
  60.6 1.2 %edges_adjoint_3_2.1 = (f32[8,256,256]{2,1,0:T(8,128)S(1)}, f32[8,256,256]{2,1,0:T(8,128)S(1)}, f32[8,256,256]{2,1,0:T(8,128)S(1)}, f32[512,256]{1,0:T(8,128)S(1)}, f32[512,256]{1,0:T(8,128)S(1)}) custom-call(f32[32,256]{1,0:T(8,128)S(1)} %get-tuple-element.116.weights, ...), custom_call_target="tpu_custom_call", output_to_operand_aliasing={{0}: (12, {}), {1}: (13, {}), {2}: (14, {})} | custom-call | bytes 6000000 | tf_op jit(solution)/shard_map/edges_adjoint_3_2/pallas_call | solution.py:752
  61.8 0.1 collective-permute-start.10
  61.9 0.9 %collective-permute-start.9 = (f32[512,256]{1,0:T(8,128)S(1)}, f32[512,256]{1,0:T(8,128)S(1)}, u32[]{:S(2)}, u32[]{:S(2)}) collective-permute-start(f32[512,256]{1,0:T(8,128)S(1)} %get-tuple-element.129), channel_id=1, source_target_pairs={{1,2},{3,4},{5,6},{7,8},{9,10},{11,12},{13,14},{2,1},{4,3},{6,5},{... | collective-permute-start | bytes 1572872 | tf_op jit(solution)/shard_map/ppermute | solution.py:782
  62.8 2.1 %adjoint_1.1 = (f32[8,256,256]{2,1,0:T(8,128)S(1)}, f32[8,256,256]{2,1,0:T(8,128)S(1)}, f32[8,256,256]{2,1,0:T(8,128)S(1)}) custom-call(f32[32,256]{1,0:T(8,128)S(1)} %get-tuple-element.116.weights, f32[8,256,256]{2,1,0:T(8,128)S(1)} %get-tuple-element.83.u1, f32[8,256,256]{2,1,0:T(8,128)S(1)} %get-tuple-element.124.w2, ...), custom_call_target="tpu_custom_call" | custom-call | bytes 6000000 | tf_op jit(solution)/shard_map/adjoint_1/pallas_call | solution.py:752
  64.9 1.8 %adjoint_0.1.cur_in = f32[8,256,256]{2,1,0:T(8,128)S(1)} custom-call(f32[8,256,256]{2,1,0:T(8,128)S(1)} %get-tuple-element.128.w1, f32[8,256,256]{2,1,0:T(8,128)S(1)} %get-tuple-element.136.q1, f32[8,256,256]{2,1,0:T(8,128)S(1)} %get-tuple-element.124.w2, f32[8,256,256]{2,1,0:T(8,128)S(1)} %get-tuple-element.127.s), custom_call_target="tpu_custom_call" | custom-call | bytes 5400000 | tf_op jit(solution)/shard_map/adjoint_0/pallas_call | solution.py:752
  66.8 0.3 near_edge_0.1
  67.1 2.7 %patch_sums.1 = (f32[16,128]{1,0:T(8,128)S(1)}, f32[8,256,256]{2,1,0:T(8,128)}, f32[8,256,256]{2,1,0:T(8,128)}) custom-call(s32[40,256]{1,0:T(8,128)S(1)} %get-tuple-element.130.maps, f32[8,256]{1,0:T(8,128)S(1)} %get-tuple-element.131.wall_gain, f32[8,256]{1,0:T(8,128)S(1)} %get-tuple-element.132.wall_now, f32[520,256]{1,0:T(8,128)S(1)} %collective-permute-done.5.got.got_a, ...), custom_call_target="tpu_custom_call" | custom-call | bytes 8100000 | tf_op jit(solution)/shard_map/patch_sums/pallas_call | solution.py:752
  69.8 11.3 %all_to_all.23 = f32[16,1,128]{2,1,0:T(1,128)S(1)} all-to-all(f32[16,1,128]{2,1,0:T(1,128)S(1)} %bitcast.16), channel_id=1, replica_groups=mesh['groups'=2,'gx'=16] {'gx'}, dimensions={0} | all-to-all | bytes 16384 | tf_op jit(solution)/shard_map/all_to_all | solution.py:785
  81.1 1.1 %far_edge_0.1 = (f32[8,256,256]{2,1,0:T(8,128)S(1)}, f32[2,256,256]{2,1,0:T(8,128)S(1)}, f32[8,256,256]{2,1,0:T(8,128)}, f32[8,256,256]{2,1,0:T(8,128)}, f32[10]{0:T(128)}) custom-call(f32[8,256,256]{2,1,0:T(8,128)S(1)} %get-tuple-element.128.w1, ...), custom_call_target="tpu_custom_call", output_to_operand_aliasing={{0}: (8, {}), {1}: (9, {}), {2}: (10, {}), {3}: (11, {})} | custom-call | bytes 3000000 | tf_op jit(solution)/shard_map/far_edge_0/pallas_call | solution.py:752
  (16 shorter events, 0.0 us)
Async XLA Ops:
  0.6 4.5 %copy-start = (f32[160]{0:T(256)S(1)}, f32[160]{0:T(256)}, u32[]{:S(2)}) copy-start(f32[160]{0:T(256)} %absorb_ref.3) | copy-start | bytes 1924
  0.6 4.5 %copy-start.1 = (f32[64]{0:T(128)S(1)}, f32[64]{0:T(128)}, u32[]{:S(2)}) copy-start(f32[64]{0:T(128)} %param.14) | copy-start | bytes 772
  1.9 8.1 %collective-permute-start.1 = (f32[520,256]{1,0:T(8,128)S(1)}, f32[520,256]{1,0:T(8,128)S(1)}, u32[]{:S(2)}, u32[]{:S(2)}) collective-permute-start(f32[520,256]{1,0:T(8,128)S(1)} %get-tuple-element.80), channel_id=1, source_target_pairs={{0,1},{1,0},{2,3},{3,2},{4,5},{5,4},{6,7},{7,6},{8,9},{9,8},{10,11... | collective-permute-start | bytes 1597448 | tf_op jit(solution)/shard_map/ppermute | solution.py:803
  2.4 12.9 %collective-permute-start = (f32[256,256]{1,0:T(8,128)S(1)}, f32[256,256]{1,0:T(8,128)S(1)}, u32[]{:S(2)}, u32[]{:S(2)}) collective-permute-start(f32[256,256]{1,0:T(8,128)S(1)} %get-tuple-element.79), channel_id=1, source_target_pairs={{1,2},{3,4},{5,6},{7,8},{9,10},{11,12},{13,14},{2,1},{4,3},{6,5},{... | collective-permute-start | bytes 786440 | tf_op jit(solution)/shard_map/ppermute | solution.py:804
  3.1 12.9 %collective-permute-start.2 = (f32[264,256]{1,0:T(8,128)S(1)}, f32[264,256]{1,0:T(8,128)S(1)}, u32[]{:S(2)}, u32[]{:S(2)}) collective-permute-start(f32[264,256]{1,0:T(8,128)S(1)} %get-tuple-element.86), channel_id=1, source_target_pairs={{1,2},{3,4},{5,6},{7,8},{9,10},{11,12},{13,14},{2,1},{4,3},{6,5},{... | collective-permute-start | bytes 811016 | tf_op jit(solution)/shard_map/ppermute | solution.py:805
  10.1 9.0 %collective-permute-start.4 = (f32[256,256]{1,0:T(8,128)S(1)}, f32[256,256]{1,0:T(8,128)S(1)}, u32[]{:S(2)}, u32[]{:S(2)}) collective-permute-start(f32[256,256]{1,0:T(8,128)S(1)} %get-tuple-element.91), channel_id=1, source_target_pairs={{0,1},{1,0},{2,3},{3,2},{4,5},{5,4},{6,7},{7,6},{8,9},{9,8},{10,11... | collective-permute-start | bytes 786440 | tf_op jit(solution)/shard_map/ppermute | solution.py:781
  15.3 8.5 %collective-permute-start.3 = (f32[256,256]{1,0:T(8,128)S(1)}, f32[256,256]{1,0:T(8,128)S(1)}, u32[]{:S(2)}, u32[]{:S(2)}) collective-permute-start(f32[256,256]{1,0:T(8,128)S(1)} %get-tuple-element.88), channel_id=1, source_target_pairs={{1,2},{3,4},{5,6},{7,8},{9,10},{11,12},{13,14},{2,1},{4,3},{6,5},{... | collective-permute-start | bytes 786440 | tf_op jit(solution)/shard_map/ppermute | solution.py:782
  19.4 9.4 %collective-permute-start.5 = (f32[520,256]{1,0:T(8,128)S(1)}, f32[520,256]{1,0:T(8,128)S(1)}, u32[]{:S(2)}, u32[]{:S(2)}) collective-permute-start(f32[520,256]{1,0:T(8,128)S(1)} %get-tuple-element.96.edge), channel_id=1, source_target_pairs={{0,1},{1,0},{2,3},{3,2},{4,5},{5,4},{6,7},{7,6},{8,9},{9,8},{10,11... | collective-permute-start | bytes 1597448 | tf_op jit(solution)/shard_map/ppermute | solution.py:781
  24.1 13.1 %collective-permute-start.6 = (f32[520,256]{1,0:T(8,128)S(1)}, f32[520,256]{1,0:T(8,128)S(1)}, u32[]{:S(2)}, u32[]{:S(2)}) collective-permute-start(f32[520,256]{1,0:T(8,128)S(1)} %get-tuple-element.101.edge), channel_id=1, source_target_pairs={{1,2},{3,4},{5,6},{7,8},{9,10},{11,12},{13,14},{2,1},{4,3},{6,5},{... | collective-permute-start | bytes 1597448 | tf_op jit(solution)/shard_map/ppermute | solution.py:782
  29.3 31.2 %collective-permute-start.7 = (f32[512,256]{1,0:T(8,128)S(1)}, f32[512,256]{1,0:T(8,128)S(1)}, u32[]{:S(2)}, u32[]{:S(2)}) collective-permute-start(f32[512,256]{1,0:T(8,128)S(1)} %get-tuple-element.119.own_a), channel_id=1, source_target_pairs={{0,1},{1,0},{2,3},{3,2},{4,5},{5,4},{6,7},{7,6},{8,9},{9,8},{10,11... | collective-permute-start | bytes 1572872 | tf_op jit(solution)/shard_map/ppermute | solution.py:781
  37.8 22.8 %collective-permute-start.8 = (f32[512,256]{1,0:T(8,128)S(1)}, f32[512,256]{1,0:T(8,128)S(1)}, u32[]{:S(2)}, u32[]{:S(2)}) collective-permute-start(f32[512,256]{1,0:T(8,128)S(1)} %get-tuple-element.120.own_b), channel_id=1, source_target_pairs={{1,2},{3,4},{5,6},{7,8},{9,10},{11,12},{13,14},{2,1},{4,3},{6,5},{... | collective-permute-start | bytes 1572872 | tf_op jit(solution)/shard_map/ppermute | solution.py:782
  61.8 5.0 %collective-permute-start.10 = (f32[512,256]{1,0:T(8,128)S(1)}, f32[512,256]{1,0:T(8,128)S(1)}, u32[]{:S(2)}, u32[]{:S(2)}) collective-permute-start(f32[512,256]{1,0:T(8,128)S(1)} %get-tuple-element.135), channel_id=1, source_target_pairs={{0,1},{1,0},{2,3},{3,2},{4,5},{5,4},{6,7},{7,6},{8,9},{9,8},{10,11... | collective-permute-start | bytes 1572872 | tf_op jit(solution)/shard_map/ppermute | solution.py:781
  61.9 19.3 %collective-permute-start.9 = (f32[512,256]{1,0:T(8,128)S(1)}, f32[512,256]{1,0:T(8,128)S(1)}, u32[]{:S(2)}, u32[]{:S(2)}) collective-permute-start(f32[512,256]{1,0:T(8,128)S(1)} %get-tuple-element.129), channel_id=1, source_target_pairs={{1,2},{3,4},{5,6},{7,8},{9,10},{11,12},{13,14},{2,1},{4,3},{6,5},{... | collective-permute-start | bytes 1572872 | tf_op jit(solution)/shard_map/ppermute | solution.py:782
